TPU v7x, 32 devices: a whole 2x2x4 slice. The times are simulated.
32 devices in a mesh: shell: 16 (over z, y, x), radial: 2 (over core).
Axes of the slice: x: 2, y: 2, z: 4, core: 2. Of those that a mesh axis runs over, the one named last changes fastest.
Arguments:
- state: float32 [8, 32, 128, 128], P(None, 'radial', 'shell')
- footpoints: int32 [32, 128, 128], P('radial', 'shell'), may hold values from 0 to 32767, as said below
- conductance: float32 [4, 128, 256], P(None, 'shell', 'radial'), may hold values from 0.1 to 0.45
- inverse_blocks: float32 [128, 2, 128, 128], P('shell', 'radial')
Outputs:
- state_next: float32 [8, 32, 128, 128], P(None, 'radial', 'shell')
- potential: float32 [128, 256], P('shell', 'radial')
- footpoint_potential: float32 [32, 128, 128], P('radial', 'shell')
Inputs may be any that keep to these rules, and one draw needn't show every extreme that they name: `footpoints`: A cell whose longitude index lon lies in shell block s = lon // 8 maps to a node whose column (node % 256) lies in s * 16 to (s + 1) * 16 - 1.
All inputs are finite; a program needn't handle non-finite values.
Results may differ from a plain program's by a relative error of at most 0.0003.
Values sent between devices are 32-bit elements; how exact they have to be, the bound alone decides.
No kernel may reach another device: no remote copies, remote signals or barrier semaphores. Data moves between devices by JAX's collectives and lax.ppermute only.
A program may use at most 64 MiB of HBM per device.

v0:
```python
import jax
import jax.numpy as jnp
from jax import lax
from jax.sharding import PartitionSpec as P

NLAT_I = 128
NLON_I = 256
ITERS_I = 4


GAMMA = 5.0 / 3.0
TIME_STEP = 0.02
CELL_AREA = 0.125


def padded_2(block, sides, width, periodic):
    for axis, dim in sides:
        count = lax.axis_size(axis)
        forward = [(i, i + 1) for i in range(count - 1)]
        if periodic:
            forward.append((count - 1, 0))
        backward = [(target, source) for source, target in forward]
        low = lax.ppermute(
            lax.slice_in_dim(block, block.shape[dim] - width, None, axis=dim), axis, forward
        )
        high = lax.ppermute(lax.slice_in_dim(block, 0, width, axis=dim), axis, backward)
        block = jnp.concatenate([low, block, high], axis=dim)
    return block


def minmod(first_jump, second_jump):
    return (
        0.5
        * (jnp.sign(first_jump) + jnp.sign(second_jump))
        * jnp.minimum(jnp.abs(first_jump), jnp.abs(second_jump))
    )


def physical_flux(conserved, direction):
    density = conserved[0]
    velocity = conserved[1:4] / density
    magnetic = conserved[4:7]
    energy = conserved[7]
    field_sq = jnp.sum(magnetic * magnetic, axis=0)
    kinetic = jnp.sum(velocity * velocity, axis=0)
    pressure = (GAMMA - 1.0) * (energy - 0.5 * density * kinetic - 0.5 * field_sq)
    total_pressure = pressure + 0.5 * field_sq
    normal_speed = velocity[direction]
    normal_field = magnetic[direction]
    selector = (jnp.arange(3) == direction).astype(jnp.float32).reshape((3,) + (1,) * density.ndim)
    momentum_flux = (
        density * velocity * normal_speed - magnetic * normal_field + total_pressure * selector
    )
    induction = normal_speed * magnetic - normal_field * velocity
    alignment = jnp.sum(velocity * magnetic, axis=0)
    energy_flux = (energy + total_pressure) * normal_speed - normal_field * alignment
    fluxes = jnp.concatenate(
        [(density * normal_speed)[None], momentum_flux, induction, energy_flux[None]], axis=0
    )
    signal = jnp.abs(normal_speed) + jnp.sqrt((GAMMA * jnp.abs(pressure) + field_sq) / density)
    return (fluxes, signal)


def face_divergence(padded, direction):
    dimension = direction + 1
    cell_count = padded.shape[dimension] - 4

    def window_slice(array, first_index, length):
        return lax.slice_in_dim(array, first_index, first_index + length, axis=dimension)

    jumps = window_slice(padded, 1, cell_count + 3) - window_slice(padded, 0, cell_count + 3)
    slopes = minmod(window_slice(jumps, 1, cell_count + 2), window_slice(jumps, 0, cell_count + 2))
    left_state = window_slice(padded, 1, cell_count + 1) + 0.5 * window_slice(
        slopes, 0, cell_count + 1
    )
    right_state = window_slice(padded, 2, cell_count + 1) - 0.5 * window_slice(
        slopes, 1, cell_count + 1
    )
    left_flux, left_signal = physical_flux(left_state, direction)
    right_flux, right_signal = physical_flux(right_state, direction)
    signal_max = jnp.maximum(left_signal, right_signal)
    face_flux = 0.5 * (left_flux + right_flux) - 0.5 * signal_max * (right_state - left_state)
    return window_slice(face_flux, 1, cell_count) - window_slice(face_flux, 0, cell_count)


def tendency(padded):
    total_div = face_divergence(padded[:, :, 2:-2, 2:-2], 0)
    total_div = total_div + face_divergence(padded[:, 2:-2, :, 2:-2], 1)
    total_div = total_div + face_divergence(padded[:, 2:-2, 2:-2, :], 2)
    return -total_div


def shifted(values, direction, offset):
    for dimension in range(3):
        first_index = offset if dimension == direction else 2
        length = values.shape[dimension] - 4
        values = lax.slice_in_dim(values, first_index, first_index + length, axis=dimension)
    return values


def field_current(padded):
    magnetic = padded[4:7]

    def derivative(component, direction):
        return 0.5 * (
            shifted(magnetic[component], direction, 3) - shifted(magnetic[component], direction, 1)
        )

    curl_first = derivative(2, 1) - derivative(1, 2)
    curl_second = derivative(0, 2) - derivative(2, 0)
    curl_third = derivative(1, 0) - derivative(0, 1)
    centre = [shifted(magnetic[component], 0, 2) for component in range(3)]
    field_sq = centre[0] * centre[0] + centre[1] * centre[1] + centre[2] * centre[2]
    aligned = curl_first * centre[0] + curl_second * centre[1] + curl_third * centre[2]
    return CELL_AREA * aligned / jnp.sqrt(1.0 + field_sq)


def pad_latitude(field):
    return jnp.pad(field, ((0, 0), (0, 0), (0, 0), (2, 2)), mode="edge")


def fill_radial(field, margin):
    position = lax.axis_index("radial")
    last_index = lax.axis_size("radial") - 1
    extent = field.shape[1]
    layer_index = lax.broadcasted_iota(jnp.int32, (1, extent, 1, 1), 1)
    lower_edge = lax.slice_in_dim(field, margin, margin + 1, axis=1)
    upper_edge = lax.slice_in_dim(field, extent - margin - 1, extent - margin, axis=1)
    field = jnp.where((layer_index < margin) & (position == 0), lower_edge, field)
    return jnp.where((layer_index >= extent - margin) & (position == last_index), upper_edge, field)


def extended_cells(field):
    grown = padded_2(field, (("shell", 2), ("radial", 1)), 2, True)
    return pad_latitude(fill_radial(grown, 2))


def body(state, footpoints, conductance, inverse_blocks):
    first_padded = extended_cells(state)
    section_one = state + TIME_STEP * tendency(first_padded)
    second_padded = extended_cells(section_one)
    state_next = 0.5 * state + 0.5 * (section_one + TIME_STEP * tendency(second_padded))
    cell_current = field_current(first_padded).reshape(-1)
    shell_count = lax.axis_size("shell")
    sector_width = NLON_I // shell_count
    latitude_node = footpoints // NLON_I
    column_node = footpoints % NLON_I
    local_column = column_node - lax.axis_index("shell") * sector_width
    node_slot = latitude_node * sector_width + local_column
    partial_sums = jax.ops.segment_sum(
        cell_current, node_slot.reshape(-1), num_segments=NLAT_I * sector_width
    )
    row_partials = lax.all_to_all(
        partial_sums.reshape(NLAT_I, sector_width), "shell", split_axis=0, concat_axis=1, tiled=True
    )
    currents = lax.psum_scatter(row_partials, "radial", scatter_dimension=1, tiled=True)
    block_matrices = inverse_blocks[:, 0]

    def apply_blocks(vector):
        return jnp.einsum("rij,rj->ri", block_matrices, vector, precision=lax.Precision.HIGHEST)

    potential = apply_blocks(currents)
    for sweep_index in range(ITERS_I - 1):
        padded_panel = padded_2(potential, (("shell", 0), ("radial", 1)), 1, False)
        coupled = currents + conductance[0] * padded_panel[:-2, 1:-1]
        coupled = coupled + conductance[1] * padded_panel[2:, 1:-1]
        coupled = coupled + conductance[2] * padded_panel[1:-1, :-2]
        coupled = coupled + conductance[3] * padded_panel[1:-1, 2:]
        potential = apply_blocks(coupled)
    full_rows = lax.all_gather(potential, "radial", axis=1, tiled=True)
    block_columns = lax.all_to_all(full_rows, "shell", split_axis=1, concat_axis=0, tiled=True)
    footpoint_potential = block_columns.reshape(-1)[node_slot]
    return (state_next, potential, footpoint_potential)


def solution(mesh):
    return jax.shard_map(
        body,
        mesh=mesh,
        in_specs=(
            P(None, "radial", "shell", None),
            P("radial", "shell", None),
            P(None, "shell", "radial"),
            P("shell", "radial", None, None),
        ),
        out_specs=(
            P(None, "radial", "shell", None),
            P("shell", "radial"),
            P("radial", "shell", None),
        ),
        check_vma=False,
    )
```

profile of v0, /device:TPU:0, one launch (start us, length us, event | category | flops | bytes accessed | tf_op | source)
XLA Modules:
  0.0 455.1 jit_solution(4446663145745851666)
XLA Ops:
  8.6 3.0 collective-permute-start
  11.6 4.1 collective-permute-start.1
  25.4 1.5 fusion.238
  26.9 2.5 copy.870
  32.6 2.6 pad_maximum_fusion
  41.5 1.6 multiply_reduce_fusion.19
  45.6 111.9 %scatter_custom_fusion = f32[2048]{0:T(1024)S(1)} fusion(s32[16384]{0:T(1024)} %fusion.224, f32[16384]{0:T(1024)} %bitcast.570, f32[]{:T(128)} %constant.25.clone.1), kind=kCustom, calls=%fused_computation.505 | custom fusion | flops 16384 | bytes 8704 | tf_op jit(solution)/shard_map/scatter-add | solution.py:150
  159.7 5.3 %all-to-all-start = ((f32[16,1,128]{2,1,0:T(1,128)}), f32[16,1,128]{2,1,0:T(1,128)S(1)}, u32[]{:S(2)}, u32[]{:S(2)}) async-start(f32[16,1,128]{2,1,0:T(1,128)} %reshape.278), calls=%async_computation | async-start | bytes 16384 | tf_op jit(solution)/shard_map/all_to_all | solution.py:153
  165.3 2.6 slice_subtract_fusion.1
  183.5 1.6 fusion.197
  185.0 7.3 %reduce-scatter.2.cloned.1.call-done = f32[8,128]{1,0:T(8,128)} async-done(((f32[8,256]{1,0:T(8,128)}), f32[8,128]{1,0:T(8,128)}) %reduce-scatter.2.cloned.1.call-update) | async-done | bytes 4112 | tf_op jit(solution)/shard_map/reduce_scatter | solution.py:156
  192.3 1.7 fusion.45
  194.0 3.6 collective-permute-start.8
  200.3 2.8 collective-permute-done.9
  205.7 1.8 collective-permute-done.11
  208.5 4.3 collective-permute-start.12
  214.3 3.9 collective-permute-done.13
  220.9 1.8 collective-permute-done.15
  223.7 3.7 collective-permute-start.16
  229.0 3.8 collective-permute-done.17
  235.5 1.8 collective-permute-done.19
  238.3 1.8 all_gather.3
  240.9 7.1 %all-to-all-start.1 = ((f32[16,1,128]{2,1,0:T(1,128)}), f32[16,1,128]{2,1,0:T(1,128)S(1)}, u32[]{:S(2)}, u32[]{:S(2)}) async-start(f32[16,1,128]{2,1,0:T(1,128)} %reshape.280), calls=%async_computation.2 | async-start | bytes 16384 | tf_op jit(solution)/shard_map/all_to_all | solution.py:171
  248.1 2.0 collective-permute-start.4
  250.0 3.9 collective-permute-start.5
  256.1 160.6 %gather_fusion = f32[16384]{0:T(1024)} fusion(f32[2048]{0:T(1024)S(1)} %reshape.248, s32[16384]{0:T(1024)S(1)} %copy-done.77), kind=kCustom, calls=%fused_computation | custom fusion | bytes 196608 | tf_op jit(solution)/shard_map/gather | solution.py:172
  419.0 1.9 fusion.237
  421.3 1.6 multiply_reduce_fusion.28
  425.5 1.7 multiply_reduce_fusion.10
  427.9 1.6 multiply_reduce_fusion.7
  430.2 3.2 copy.887
  433.4 3.2 copy.888
  (336 shorter events, 78.1 us)
Async XLA Ops:
  7.2 185.1 %copy-start = (f32[8,1,128,128]{3,2,1,0:T(8,128)S(1)}, f32[8,1,128,128]{3,2,1,0:T(8,128)}, u32[]{:S(2)}) copy-start(f32[8,1,128,128]{3,2,1,0:T(8,128)} %param.7) | copy-start | bytes 1572868
  8.6 11.9 %collective-permute-start = (f32[8,16,2,128]{3,2,1,0:T(2,128)S(1)}, f32[8,16,2,128]{3,2,1,0:T(2,128)S(1)}, u32[]{:S(2)}, u32[]{:S(2)}) collective-permute-start(f32[8,16,2,128]{3,2,1,0:T(2,128)S(1)} %get-tuple-element.176), channel_id=1, source_target_pairs={{0,2},{2,4},{4,6},{6,8},{8,10},{10,12},{12,14},{14,16},{16,18},{18... | collective-permute-start | bytes 393224 | tf_op jit(solution)/shard_map/ppermute | solution.py:23
  11.6 8.9 %collective-permute-start.1 = (f32[8,16,2,128]{3,2,1,0:T(2,128)S(1)}, f32[8,16,2,128]{3,2,1,0:T(2,128)S(1)}, u32[]{:S(2)}, u32[]{:S(2)}) collective-permute-start(f32[8,16,2,128]{3,2,1,0:T(2,128)S(1)} %get-tuple-element.177), channel_id=1, source_target_pairs={{2,0},{4,2},{6,4},{8,6},{10,8},{12,10},{14,12},{16,14},{18,16},{20... | collective-permute-start | bytes 393224 | tf_op jit(solution)/shard_map/ppermute | solution.py:26
  21.4 1.4 collective-permute-start.2
  21.5 1.5 collective-permute-start.3
  159.7 18.8 %all-to-all-start = ((f32[16,1,128]{2,1,0:T(1,128)}), f32[16,1,128]{2,1,0:T(1,128)S(1)}, u32[]{:S(2)}, u32[]{:S(2)}) async-start(f32[16,1,128]{2,1,0:T(1,128)} %reshape.278), calls=%async_computation | async-start | bytes 16384 | tf_op jit(solution)/shard_map/all_to_all | solution.py:153
  165.0 27.2 %reduce-scatter.2.cloned.1.call-start = ((), (), s32[]{:S(2)}) async-start(), calls=%async_computation.3 | async-start | bytes 12288 | tf_op jit(solution)/shard_map/reduce_scatter | solution.py:156
  177.8 21.1 %copy-start.28 = (f32[3,17,8,128]{3,2,1,0:T(8,128)S(1)}, f32[3,17,8,128]{3,2,1,0:T(8,128)}, u32[]{:S(2)}) copy-start(f32[3,17,8,128]{3,2,1,0:T(8,128)} %get-tuple-element.84) | copy-start | bytes 626692
  177.8 21.1 %copy-start.47 = (f32[17,8,128]{2,1,0:T(8,128)S(1)}, f32[17,8,128]{2,1,0:T(8,128)}, u32[]{:S(2)}) copy-start(f32[17,8,128]{2,1,0:T(8,128)} %copy-done.46) | copy-start | bytes 208900
  177.8 21.1 %copy-start.49 = (f32[17,8,128]{2,1,0:T(8,128)S(1)}, f32[17,8,128]{2,1,0:T(8,128)}, u32[]{:S(2)}) copy-start(f32[17,8,128]{2,1,0:T(8,128)} %copy-done.48) | copy-start | bytes 208900
  177.8 21.1 %copy-start.70 = (f32[17,8,128]{2,1,0:T(8,128)S(1)}, f32[17,8,128]{2,1,0:T(8,128)}, u32[]{:S(2)}) copy-start(f32[17,8,128]{2,1,0:T(8,128)} %get-tuple-element.170) | copy-start | bytes 208900
  177.8 21.1 %copy-start.85 = (f32[3]{0:T(128)S(1)}, f32[3]{0:T(128)}, u32[]{:S(2)}) copy-start(f32[3]{0:T(128)} %compare_convert_fusion.2) | copy-start | bytes 40
  192.3 15.2 %copy-start.79 = (f32[8,128]{1,0:T(8,128)S(1)}, f32[8,128]{1,0:T(8,128)}, u32[]{:S(2)}) copy-start(f32[8,128]{1,0:T(8,128)} %reduce-scatter.2.cloned.1.call-done) | copy-start | bytes 12292
  194.0 6.3 %collective-permute-start.8 = (f32[1,128]{1,0:T(1,128)S(1)}, f32[1,128]{1,0:T(1,128)S(1)}, u32[]{:S(2)}, u32[]{:S(2)}) collective-permute-start(f32[1,128]{1,0:T(1,128)S(1)} %get-tuple-element.224), channel_id=1, source_target_pairs={{0,2},{2,4},{4,6},{6,8},{8,10},{10,12},{12,14},{14,16},{16,18},{18... | collective-permute-start | bytes 1544 | tf_op jit(solution)/shard_map/ppermute | solution.py:23
  197.6 5.4 %collective-permute-start.9 = (f32[1,128]{1,0:T(1,128)S(1)}, f32[1,128]{1,0:T(1,128)S(1)}, u32[]{:S(2)}, u32[]{:S(2)}) collective-permute-start(f32[1,128]{1,0:T(1,128)S(1)} %get-tuple-element.225), channel_id=1, source_target_pairs={{2,0},{4,2},{6,4},{8,6},{10,8},{12,10},{14,12},{16,14},{18,16},{20... | collective-permute-start | bytes 1544 | tf_op jit(solution)/shard_map/ppermute | solution.py:26
  203.1 2.6 collective-permute-start.10
  204.4 3.1 collective-permute-start.11
  208.5 5.8 %collective-permute-start.12 = (f32[1,128]{1,0:T(1,128)S(1)}, f32[1,128]{1,0:T(1,128)S(1)}, u32[]{:S(2)}, u32[]{:S(2)}) collective-permute-start(f32[1,128]{1,0:T(1,128)S(1)} %get-tuple-element.222), channel_id=1, source_target_pairs={{0,2},{2,4},{4,6},{6,8},{8,10},{10,12},{12,14},{14,16},{16,18},{18... | collective-permute-start | bytes 1544 | tf_op jit(solution)/shard_map/ppermute | solution.py:23
  212.8 5.4 %collective-permute-start.13 = (f32[1,128]{1,0:T(1,128)S(1)}, f32[1,128]{1,0:T(1,128)S(1)}, u32[]{:S(2)}, u32[]{:S(2)}) collective-permute-start(f32[1,128]{1,0:T(1,128)S(1)} %get-tuple-element.223), channel_id=1, source_target_pairs={{2,0},{4,2},{6,4},{8,6},{10,8},{12,10},{14,12},{16,14},{18,16},{20... | collective-permute-start | bytes 1544 | tf_op jit(solution)/shard_map/ppermute | solution.py:26
  218.3 2.6 collective-permute-start.14
  219.6 3.1 collective-permute-start.15
  223.7 5.4 %collective-permute-start.16 = (f32[1,128]{1,0:T(1,128)S(1)}, f32[1,128]{1,0:T(1,128)S(1)}, u32[]{:S(2)}, u32[]{:S(2)}) collective-permute-start(f32[1,128]{1,0:T(1,128)S(1)} %get-tuple-element.220), channel_id=1, source_target_pairs={{0,2},{2,4},{4,6},{6,8},{8,10},{10,12},{12,14},{14,16},{16,18},{18... | collective-permute-start | bytes 1544 | tf_op jit(solution)/shard_map/ppermute | solution.py:23
  227.4 5.4 %collective-permute-start.17 = (f32[1,128]{1,0:T(1,128)S(1)}, f32[1,128]{1,0:T(1,128)S(1)}, u32[]{:S(2)}, u32[]{:S(2)}) collective-permute-start(f32[1,128]{1,0:T(1,128)S(1)} %get-tuple-element.221), channel_id=1, source_target_pairs={{2,0},{4,2},{6,4},{8,6},{10,8},{12,10},{14,12},{16,14},{18,16},{20... | collective-permute-start | bytes 1544 | tf_op jit(solution)/shard_map/ppermute | solution.py:26
  229.0 27.1 %copy-start.77 = (s32[16384]{0:T(1024)S(1)}, s32[16384]{0:T(1024)}, u32[]{:S(2)}) copy-start(s32[16384]{0:T(1024)} %fusion.165) | copy-start | bytes 196612
  232.9 2.6 collective-permute-start.18
  234.2 3.1 collective-permute-start.19
  238.3 178.4 %copy-start.80 = (f32[8,1,128]{2,1,0:T(1,128)}, f32[8,1,128]{2,1,0:T(1,128)S(1)}, u32[]{:S(2)}) copy-start(f32[8,1,128]{2,1,0:T(1,128)S(1)} %fusion.39) | copy-start | bytes 12292
  240.9 14.4 %all-to-all-start.1 = ((f32[16,1,128]{2,1,0:T(1,128)}), f32[16,1,128]{2,1,0:T(1,128)S(1)}, u32[]{:S(2)}, u32[]{:S(2)}) async-start(f32[16,1,128]{2,1,0:T(1,128)} %reshape.280), calls=%async_computation.2 | async-start | bytes 16384 | tf_op jit(solution)/shard_map/all_to_all | solution.py:171
  248.1 168.6 %collective-permute-start.4 = (f32[8,16,2,128]{3,2,1,0:T(2,128)S(1)}, f32[8,16,2,128]{3,2,1,0:T(2,128)S(1)}, u32[]{:S(2)}, u32[]{:S(2)}) collective-permute-start(f32[8,16,2,128]{3,2,1,0:T(2,128)S(1)} %get-tuple-element.174), channel_id=1, source_target_pairs={{0,2},{2,4},{4,6},{6,8},{8,10},{10,12},{12,14},{14,16},{16,18},{18... | collective-permute-start | bytes 393224 | tf_op jit(solution)/shard_map/ppermute | solution.py:23
  250.0 166.7 %collective-permute-start.5 = (f32[8,16,2,128]{3,2,1,0:T(2,128)S(1)}, f32[8,16,2,128]{3,2,1,0:T(2,128)S(1)}, u32[]{:S(2)}, u32[]{:S(2)}) collective-permute-start(f32[8,16,2,128]{3,2,1,0:T(2,128)S(1)} %get-tuple-element.175), channel_id=1, source_target_pairs={{2,0},{4,2},{6,4},{8,6},{10,8},{12,10},{14,12},{16,14},{18,16},{20... | collective-permute-start | bytes 393224 | tf_op jit(solution)/shard_map/ppermute | solution.py:26
  416.8 1.4 collective-permute-start.6
  416.9 1.5 collective-permute-start.7
  (78 other events, 267.9 us)
Sparse Core Ops, SparseCore 0:
  183.6 8.6 reduce-scatter.1
where the time goes:
time: 456 us; the launch traced here: 455 us
  local copies, waits for them, and re-layouts  198 us (43%)
  other arithmetic  159 us (35%)
  starting transfers between devices  49.9 us (11%)
  waiting for transfers between devices  26.4 us (6%)
  between operations  15.5 us (3%)
    gather x1, local copies, waits for them, and re-layouts, body(): footpoint_potential = block_columns.reshape(-1)[node_slot]  161 us
    scatter-add x1, other arithmetic, body(): jax.ops.segment_sum(cell_current, node_slot.reshape(-1), num_segments=NLA...  112 us
    ppermute x10, starting transfers between devices, padded_2(): lax.ppermute(lax.slice_in_dim(block, block.shape[dim] - width, None, axis...  20.6 us
    ppermute x10, starting transfers between devices, padded_2(): lax.ppermute(lax.slice_in_dim(block, 0, width, axis=dim), axis, backward)  16.7 us
    ppermute x10, waiting for transfers between devices, padded_2(): lax.ppermute(lax.slice_in_dim(block, 0, width, axis=dim), axis, backward)  16.1 us
    slice x6, local copies, waits for them, and re-layouts, pad_latitude(): return jnp.pad(field, ((0, 0), (0, 0), (0, 0), (2, 2)), mode='edge')  13.6 us
    reduce_sum x12, other arithmetic, physical_flux(): field_sq = jnp.sum(magnetic * magnetic, axis=0)  12.4 us
    unnamed x178, local copies, waits for them, and re-layouts  11 us
  transfers between devices with their start and end apart: 23, of which 12 were waited for; matrix products, arithmetic and copies ran while one was open for 39% of the time, Pallas kernels for 0%

commit v1 on v0

v1 whole, which is shorter than its diff:
```python
import functools
import jax
import jax.numpy as jnp
from jax import lax
from jax.experimental import pallas as pl
from jax.experimental.pallas import tpu as pltpu
from jax.sharding import PartitionSpec as P

ITERS_I = 4
HALO = ITERS_I - 1
GAMMA = 5.0 / 3.0
TIME_STEP = 0.02
CELL_AREA = 0.125
LANES = 128
SUB = 8
PARTS = 3
VMEM_LIMIT = 40 * 1024 * 1024


def call(kernel, out_shape, name, flops=1_000_000, nbytes=1_000_000, scratch=()):
    return pl.pallas_call(
        kernel,
        out_shape=out_shape,
        scratch_shapes=list(scratch),
        compiler_params=pltpu.CompilerParams(vmem_limit_bytes=VMEM_LIMIT),
        cost_estimate=pl.CostEstimate(flops=flops, bytes_accessed=nbytes, transcendentals=0),
        name=name,
    )


def shape_of(*dims):
    return jax.ShapeDtypeStruct(dims, jnp.float32)


def lane_index(rows, width=LANES):
    return lax.broadcasted_iota(jnp.int32, (rows, width), 1)


def row_index(rows, width=LANES):
    return lax.broadcasted_iota(jnp.int32, (rows, width), 0)


def minmod(a, b):
    return jnp.maximum(jnp.minimum(a, b), 0.0) + jnp.minimum(jnp.maximum(a, b), 0.0)


def reciprocal(value):
    guess = pl.reciprocal(value, approx=True)
    return guess * (2.0 - value * guess)


def flux_and_speed(u, d):
    density, m, b, energy = u[0], u[1:4], u[4:7], u[7]
    inverse = reciprocal(density)
    v = [component * inverse for component in m]
    field_sq = b[0] * b[0] + b[1] * b[1] + b[2] * b[2]
    twice_kinetic = m[0] * v[0] + m[1] * v[1] + m[2] * v[2]
    pressure = (GAMMA - 1.0) * (energy - 0.5 * (twice_kinetic + field_sq))
    total = pressure + 0.5 * field_sq
    alignment = v[0] * b[0] + v[1] * b[1] + v[2] * b[2]
    vn, bn = v[d], b[d]
    momentum = [m[j] * vn - b[j] * bn for j in range(3)]
    momentum[d] = momentum[d] + total
    induction = [None if j == d else vn * b[j] - bn * v[j] for j in range(3)]
    flux = [m[d]] + momentum + induction + [(energy + total) * vn - bn * alignment]
    speed = jnp.abs(vn) + jnp.sqrt((GAMMA * jnp.abs(pressure) + field_sq) * inverse)
    return flux, speed


def face_flux(left, right, d):
    left_flux, left_speed = flux_and_speed(left, d)
    right_flux, right_speed = flux_and_speed(right, d)
    speed = jnp.maximum(left_speed, right_speed)
    out = []
    for k in range(8):
        jump = speed * (right[k] - left[k])
        if left_flux[k] is None:
            out.append(-0.5 * jump)
        else:
            out.append(0.5 * (left_flux[k] + right_flux[k] - jump))
    return out, left_flux


def march(load, cells, d, emit):
    before, here, after = load(-2), load(-1), load(0)
    half = [0.5 * minmod(after[k] - here[k], here[k] - before[k]) for k in range(8)]
    left = [here[k] + half[k] for k in range(8)]
    jump = [after[k] - here[k] for k in range(8)]

    def face(f, here, left, jump):
        ahead = load(f + 1)
        next_jump = [ahead[k] - here[k] for k in range(8)]
        half = [0.5 * minmod(next_jump[k], jump[k]) for k in range(8)]
        right = [here[k] - half[k] for k in range(8)]
        flux, _ = face_flux(left, right, d)
        return ahead, [here[k] + half[k] for k in range(8)], next_jump, flux

    here, left, jump, flux = face(0, after, left, jump)

    def step(f, carry):
        here, left, jump, flux = carry
        here, left, jump, new = face(f, here, left, jump)
        emit(f - 1, [new[k] - flux[k] for k in range(8)])
        return here, left, jump, new

    lax.fori_loop(1, cells + 1, step, (here, left, jump, flux), unroll=2)


def pack_halos(source, low_ref, high_ref, edge_ref, layers, position):
    for k in range(8):
        for j in range(2):
            low_ref[k, j] = source[k, pl.ds(j, layers, stride=SUB), :]
            high_ref[k, j] = source[k, pl.ds(SUB - 2 + j, layers, stride=SUB), :]
    first = jnp.where(position == 0, (layers - 2) * SUB, 0)
    first = pl.multiple_of(first, SUB)
    for k in range(8):
        edge_ref[k] = source[k, pl.ds(first, 2 * SUB), :]


def tendency_into(x_ref, low_ref, high_ref, edge_ref, xr, xl, div, layers, position, last, finish):
    cells = layers * SUB
    for k in range(8):
        xr[k, 2 * SUB : 2 * SUB + cells] = x_ref[k]
        first, final = x_ref[k, 0:SUB], x_ref[k, cells - SUB : cells]
        for j in range(2):
            rows = slice(j * SUB, (j + 1) * SUB)
            xr[k, j * SUB : (j + 1) * SUB] = jnp.where(position == 0, first, edge_ref[k, rows])
            xr[k, cells + (2 + j) * SUB : cells + (3 + j) * SUB] = jnp.where(
                position == last, final, edge_ref[k, rows]
            )
            xl[k, j * layers : (j + 1) * layers] = low_ref[k, j]
            xl[k, (SUB + 2 + j) * layers : (SUB + 3 + j) * layers] = high_ref[k, j]
        for j in range(SUB):
            xl[k, (2 + j) * layers : (3 + j) * layers] = x_ref[k, pl.ds(j, layers, stride=SUB), :]

    def load_radial(c):
        start = (c + 2) * SUB
        if not isinstance(start, int):
            start = pl.multiple_of(start, SUB)
        return [xr[k, pl.ds(start, SUB), :] for k in range(8)]

    def emit_radial(c, values):
        start = pl.multiple_of(c * SUB, SUB)
        for k in range(8):
            div[k, pl.ds(start, SUB), :] = values[k]

    march(load_radial, layers, 0, emit_radial)

    def load_lon(c):
        start = (c + 2) * layers
        if not isinstance(start, int):
            start = pl.multiple_of(start, SUB)
        return [xl[k, pl.ds(start, layers), :] for k in range(8)]

    def emit_lon(c, values):
        for k in range(8):
            rows = pl.ds(c, layers, stride=SUB)
            div[k, rows, :] = div[k, rows, :] + values[k]

    march(load_lon, SUB, 1, emit_lon)

    lane = lane_index(SUB)
    at_first, at_last = lane == 0, lane == LANES - 1

    def layer(r, carry):
        rows = pl.ds(pl.multiple_of(r * SUB, SUB), SUB)
        x = [x_ref[k, rows, :] for k in range(8)]
        left, right = [], []
        for k in range(8):
            jump = jnp.where(at_last, 0.0, pltpu.roll(x[k], LANES - 1, 1) - x[k])
            half = 0.5 * minmod(jump, pltpu.roll(jump, 1, 1))
            left.append(x[k] + half)
            down = x[k] - half
            right.append(jnp.where(at_last, down, pltpu.roll(down, LANES - 1, 1)))
        flux, left_flux = face_flux(left, right, 2)
        total = []
        for k in range(8):
            edge = 0.0 if left_flux[k] is None else left_flux[k]
            total.append(
                div[k, rows, :] + flux[k] - jnp.where(at_first, edge, pltpu.roll(flux[k], 1, 1))
            )
        finish(rows, x, total)
        return carry

    lax.fori_loop(0, layers, layer, 0, unroll=2)


def pack_kernel(layers, x_ref, low_ref, high_ref, edge_ref):
    pack_halos(x_ref, low_ref, high_ref, edge_ref, layers, lax.axis_index("radial"))


def first_stage_kernel(
    layers, x_ref, low, high, edge, out_ref, low_ref, high_ref, edge_ref, xr, xl, div
):
    position, last = lax.axis_index("radial"), lax.axis_size("radial") - 1

    def finish(rows, x, total):
        for k in range(8):
            out_ref[k, rows, :] = x[k] - TIME_STEP * total[k]

    tendency_into(x_ref, low, high, edge, xr, xl, div, layers, position, last, finish)
    pack_halos(out_ref, low_ref, high_ref, edge_ref, layers, position)


def second_stage_kernel(layers, x_ref, low, high, edge, state_ref, out_ref, xr, xl, div):
    position, last = lax.axis_index("radial"), lax.axis_size("radial") - 1

    def finish(rows, x, total):
        for k in range(8):
            out_ref[k, rows, :] = 0.5 * state_ref[k, rows, :] + 0.5 * (x[k] - TIME_STEP * total[k])

    tendency_into(x_ref, low, high, edge, xr, xl, div, layers, position, last, finish)


def log2_of(value):
    assert value & (value - 1) == 0
    return value.bit_length() - 1


def node_row_column(nodes, columns):
    return lax.shift_right_logical(nodes, log2_of(columns)), nodes & (columns - 1)


def three_parts(value):
    parts = []
    for _ in range(PARTS):
        part = value.astype(jnp.bfloat16).astype(jnp.float32)
        parts.append(part)
        value = value - part
    return parts


def current_kernel(layers, width, columns, window, x_ref, low, high, edge, nodes_ref, out_ref, held):
    position, last = lax.axis_index("radial"), lax.axis_size("radial") - 1
    first_column = lax.axis_index("shell") * width
    lane, sub = lane_index(SUB), row_index(SUB)
    groups = max(16, width)
    group_rows = row_index(groups)
    slot_rows = row_index(LANES)

    def radial_pair(k, r):
        rows = lambda c: slice(c * SUB, (c + 1) * SUB)
        if r == 0:
            below = jnp.where(position == 0, x_ref[4 + k, rows(0)], edge[4 + k, rows(1)])
        else:
            below = x_ref[4 + k, rows(r - 1)]
        if r == layers - 1:
            above = jnp.where(position == last, x_ref[4 + k, rows(r)], edge[4 + k, rows(0)])
        else:
            above = x_ref[4 + k, rows(r + 1)]
        return 0.5 * (above - below)

    def lat_pair(value):
        above = jnp.where(lane == LANES - 1, value, pltpu.roll(value, LANES - 1, 1))
        below = jnp.where(lane == 0, value, pltpu.roll(value, 1, 1))
        return 0.5 * (above - below)

    def lon_pair(k, r, value):
        above = jnp.where(sub == SUB - 1, high[4 + k, 0, r : r + 1, :], pltpu.roll(value, SUB - 1, 0))
        below = jnp.where(sub == 0, low[4 + k, 1, r : r + 1, :], pltpu.roll(value, 1, 0))
        return 0.5 * (above - below)

    total = jnp.zeros((PARTS * groups, LANES), jnp.float32)
    for r in range(layers):
        b = [x_ref[4 + k, r * SUB : (r + 1) * SUB] for k in range(3)]
        first = lon_pair(2, r, b[2]) - lat_pair(b[1])
        second = lat_pair(b[0]) - radial_pair(2, r)
        third = radial_pair(1, r) - lon_pair(0, r, b[0])
        aligned = first * b[0] + second * b[1] + third * b[2]
        field_sq = b[0] * b[0] + b[1] * b[1] + b[2] * b[2]
        current = CELL_AREA * aligned * lax.rsqrt(1.0 + field_sq)
        row, column = node_row_column(nodes_ref[r * SUB : (r + 1) * SUB], columns)
        slot = row * width + (column - first_column)
        group, place = lax.shift_right_logical(slot, 7), slot & (LANES - 1)
        parts = three_parts(current)
        lefts, rights = [], []
        for l in range(SUB):
            here = group_rows == group[l : l + 1, :]
            lefts.append(
                jnp.concatenate([jnp.where(here, part[l : l + 1, :], 0.0) for part in parts], axis=0)
            )
            rights.append(jnp.where(slot_rows == place[l : l + 1, :], 1.0, 0.0))
        left = jnp.concatenate(lefts, axis=1).astype(jnp.bfloat16)
        right = jnp.concatenate(rights, axis=1).astype(jnp.bfloat16)
        total = total + lax.dot_general(
            left, right, (((1,), (1,)), ((), ())), preferred_element_type=jnp.float32
        )
    sums = total[:groups]
    for part in range(1, PARTS):
        sums = sums + total[part * groups : (part + 1) * groups]
    if not window:
        out_ref[...] = sums[: out_ref.shape[0]]
        return
    held[...] = jnp.zeros_like(held)
    held[SUB : SUB + groups] = sums
    out_ref[...] = jnp.zeros_like(out_ref)
    for twin in range(2):
        for j in range(3):
            out_ref[pl.ds(twin * 4 + j, groups, stride=8), :] = held[SUB - 1 + j : SUB - 1 + j + groups]


def rim_kernel(blocks_ref, conductance_ref, low_ref, high_ref):
    rows = blocks_ref.shape[0]
    size = blocks_ref.shape[1]
    for ref, first in ((low_ref, 0), (high_ref, rows - HALO)):
        ref[...] = jnp.zeros_like(ref)
        for e in range(HALO):
            ref[e, :size] = blocks_ref[first + e]
            for way in range(4):
                ref[e, size + way : size + way + 1] = conductance_ref[way, first + e : first + e + 1]


def swap_blocks(tile, piece):
    sub = row_index(SUB)
    block = lax.shift_right_logical(lane_index(SUB), log2_of(piece))
    for bit in (1, 2, 4):
        up, across = (sub & bit) != 0, (block & bit) != 0
        from_below = pltpu.roll(pltpu.roll(tile, SUB - bit, 0), bit * piece, 1)
        from_above = pltpu.roll(pltpu.roll(tile, bit, 0), LANES - bit * piece, 1)
        tile = jnp.where(up == across, tile, jnp.where(up, from_above, from_below))
    return tile


def sweep_kernel(
    width,
    arrived,
    own_blocks,
    own_conductance,
    own_low,
    own_high,
    twin_blocks,
    twin_conductance,
    twin_low,
    twin_high,
    out_ref,
    send_ref,
    pot,
    rhs_ref,
    cond,
):
    position = lax.axis_index("radial")
    size = LANES
    rows = SUB
    span = 3 * SUB
    base = SUB
    halves = []
    for h in range(2):
        tiles = []
        for g in range(3):
            both = [arrived[pl.ds(h * 64 + r * 4 + g, SUB, stride=8), :] for r in range(2)]
            tiles.append(swap_blocks(both[0] + both[1], width))
        halves.append(jnp.concatenate(tiles, axis=0))
    own_currents = jnp.where(position == 0, halves[0], halves[1])
    twin_currents = jnp.where(position == 0, halves[1], halves[0])
    currents = [own_currents, twin_currents]

    cond[...] = jnp.zeros_like(cond)
    sources = ((own_conductance, own_low, own_high), (twin_conductance, twin_low, twin_high))
    for side, (mid, low, high) in enumerate(sources):
        for way in range(4):
            cond[side, way, SUB : 2 * SUB] = mid[way]
            for e in range(HALO):
                row = size + way
                cond[side, way, SUB - HALO + e : SUB - HALO + e + 1] = low[e, row : row + 1]
                cond[side, way, 2 * SUB + e : 2 * SUB + e + 1] = high[e, row : row + 1]
    pot[...] = jnp.zeros_like(pot)
    eye = row_index(size, size) == lane_index(size, size)
    blocks = ((own_blocks, own_low, own_high), (twin_blocks, twin_low, twin_high))

    def matrix(side, e):
        mid, low, high = blocks[side]
        if e < SUB:
            return low[e - (SUB - HALO), :size]
        if e < 2 * SUB:
            return mid[e - SUB]
        return high[e - 2 * SUB, :size]

    lane = lane_index(span)
    for sweep in range(ITERS_I):
        reach = ITERS_I - 1 - sweep
        sides = (0, 1) if reach else (0,)
        if sweep == 0:
            rhs = currents
        else:
            mid = [pot[side, base : base + span] for side in range(2)]
            west = [pltpu.roll(mid[side], 1, 1) for side in range(2)]
            east = [pltpu.roll(mid[side], LANES - 1, 1) for side in range(2)]
            rhs = []
            for side in sides:
                is_right = position == (1 - side)
                west_edge = jnp.where(is_right, west[1 - side], 0.0)
                east_edge = jnp.where(is_right, 0.0, east[1 - side])
                coupled = currents[side] + cond[side, 0] * pot[side, base - 1 : base - 1 + span]
                coupled = coupled + cond[side, 1] * pot[side, base + 1 : base + 1 + span]
                coupled = coupled + cond[side, 2] * jnp.where(lane == 0, west_edge, west[side])
                coupled = coupled + cond[side, 3] * jnp.where(lane == LANES - 1, east_edge, east[side])
                rhs.append(coupled)
        for side in sides:
            rhs_ref[side] = rhs[side]
        for side in sides:
            for e in range(SUB - reach, 2 * SUB + reach):
                product = matrix(side, e) * rhs_ref[side, e : e + 1]
                column = jnp.sum(product, axis=1, keepdims=True)
                line = jnp.sum(jnp.where(eye, column, 0.0), axis=0, keepdims=True)
                pot[side, base + e : base + e + 1] = line
    result = pot[0, base + SUB : base + 2 * SUB]
    out_ref[...] = result
    for d in range(send_ref.shape[0] // rows):
        send_ref[d * rows : (d + 1) * rows] = result


def gather_kernel(width, columns, direct, table_ref, nodes_ref, out_ref):
    first_column = lax.axis_index("shell") * width
    if direct:
        table = table_ref[...]
    else:
        half = lax.shift_right_logical(first_column, 7)
        strip = table_ref[:, pl.ds(half, 1), :, :]
        strip = strip.reshape(strip.shape[0] * SUB, LANES)
        pick = lane_index(width) == row_index(width) + (first_column & (LANES - 1))
        table = lax.dot_general(
            jnp.where(pick, 1.0, 0.0),
            strip,
            (((1,), (1,)), ((), ())),
            precision=lax.Precision.HIGHEST,
            preferred_element_type=jnp.float32,
        )
    lines = [jnp.broadcast_to(table[c : c + 1, :], (SUB, LANES)) for c in range(width)]
    for r in range(nodes_ref.shape[0] // SUB):
        rows = slice(r * SUB, (r + 1) * SUB)
        row, column = node_row_column(nodes_ref[rows], columns)
        column = column - first_column
        value = jnp.zeros((SUB, LANES), jnp.float32)
        for c in range(width):
            value = jnp.where(column == c, jnp.take_along_axis(lines[c], row, axis=1), value)
        out_ref[rows] = value


def ring(axis, step, periodic):
    count = lax.axis_size(axis)
    pairs = [(i, i + step) for i in range(count)]
    if periodic:
        return [(i, j % count) for i, j in pairs]
    return [(i, j) for i, j in pairs if 0 <= j < count]


def exchange_halos(low, high, edge):
    from_below = lax.ppermute(high, "shell", ring("shell", 1, True))
    from_above = lax.ppermute(low, "shell", ring("shell", -1, True))
    other = lax.ppermute(edge, "radial", [(0, 1), (1, 0)])
    return from_below, from_above, other


def padded_2(block, sides, width):
    for axis, dim in sides:
        low = lax.ppermute(
            lax.slice_in_dim(block, block.shape[dim] - width, None, axis=dim), axis, ring(axis, 1, False)
        )
        high = lax.ppermute(lax.slice_in_dim(block, 0, width, axis=dim), axis, ring(axis, -1, False))
        block = jnp.concatenate([low, block, high], axis=dim)
    return block


def general_solve(partial, conductance, blocks, rows_total, width):
    row_partials = lax.all_to_all(
        partial.reshape(rows_total, width), "shell", split_axis=0, concat_axis=1, tiled=True
    )
    currents = lax.psum_scatter(row_partials, "radial", scatter_dimension=1, tiled=True)

    def apply_blocks(vector):
        return jnp.einsum("rij,rj->ri", blocks, vector, precision=lax.Precision.HIGHEST)

    potential = apply_blocks(currents)
    for _ in range(ITERS_I - 1):
        panel = padded_2(potential, (("shell", 0), ("radial", 1)), 1)
        coupled = currents + conductance[0] * panel[:-2, 1:-1]
        coupled = coupled + conductance[1] * panel[2:, 1:-1]
        coupled = coupled + conductance[2] * panel[1:-1, :-2]
        coupled = coupled + conductance[3] * panel[1:-1, 2:]
        potential = apply_blocks(coupled)
    full_rows = lax.all_gather(potential, "radial", axis=1, tiled=True)
    strip = lax.all_to_all(full_rows, "shell", split_axis=1, concat_axis=0, tiled=True)
    return potential, strip.T


def body(state, footpoints, conductance, inverse_blocks):
    fields, layers, lons, lats = state.shape
    shells, radials = lax.axis_size("shell"), lax.axis_size("radial")
    assert (fields, lons, lats, radials) == (8, SUB, LANES, 2)
    cells = layers * SUB
    own_rows, half = conductance.shape[1:]
    assert half == LANES
    rows_total, columns = own_rows * shells, half * radials
    width = columns // shells
    x = state.reshape(fields, cells, lats)
    nodes = footpoints.reshape(cells, lats)
    blocks = inverse_blocks[:, 0]
    fast = own_rows == SUB and width * SUB == LANES

    halo_shapes = [shape_of(8, 2, layers, lats), shape_of(8, 2, layers, lats), shape_of(8, 2 * SUB, lats)]
    stage_scratch = [
        pltpu.VMEM((8, cells + 4 * SUB, lats), jnp.float32),
        pltpu.VMEM((8, (SUB + 4) * layers, lats), jnp.float32),
        pltpu.VMEM((8, cells, lats), jnp.float32),
    ]
    packed = call(functools.partial(pack_kernel, layers), halo_shapes, "pack")(x)
    below, above, other = exchange_halos(*packed)

    if fast:
        rim_shape = shape_of(HALO, half + SUB, half)
        rim_low, rim_high = call(rim_kernel, [rim_shape, rim_shape], "rim")(blocks, conductance)
        own_low = lax.ppermute(rim_high, "shell", ring("shell", 1, False))
        own_high = lax.ppermute(rim_low, "shell", ring("shell", -1, False))
        twin = [(0, 1), (1, 0)]
        twin_parts = [lax.ppermute(v, "radial", twin) for v in (blocks, conductance, own_low, own_high)]

    send_shape = shape_of(shells * radials * 4, LANES) if fast else shape_of(width, LANES)
    sums = call(
        functools.partial(current_kernel, layers, width, columns, fast),
        send_shape,
        "currents",
        flops=10_000_000,
        scratch=[pltpu.VMEM((max(16, width) + 2 * SUB, LANES), jnp.float32)],
    )(x, below, above, other, nodes)

    stage = call(
        functools.partial(first_stage_kernel, layers),
        [shape_of(fields, cells, lats)] + halo_shapes,
        "first_stage",
        flops=20_000_000,
        scratch=stage_scratch,
    )(x, below, above, other)
    section_one = stage[0]
    second_halos = exchange_halos(*stage[1:])

    if fast:
        arrived = lax.all_to_all(sums, ("shell", "radial"), split_axis=0, concat_axis=0, tiled=True)
        potential, spread = call(
            functools.partial(sweep_kernel, width),
            [shape_of(own_rows, half), shape_of(shells * radials * own_rows, half)],
            "sweeps",
            scratch=[
                pltpu.VMEM((2, 5 * SUB, half), jnp.float32),
                pltpu.VMEM((2, 3 * SUB, half), jnp.float32),
                pltpu.VMEM((2, 4, 3 * SUB, half), jnp.float32),
            ],
        )(arrived, blocks, conductance, own_low, own_high, *twin_parts)
        table = lax.all_to_all(spread, ("shell", "radial"), split_axis=0, concat_axis=0, tiled=True)
        table = table.reshape(shells, radials, own_rows, half)
    else:
        potential, table = general_solve(sums, conductance, blocks, rows_total, width)

    state_next = call(
        functools.partial(second_stage_kernel, layers),
        shape_of(fields, cells, lats),
        "second_stage",
        flops=20_000_000,
        scratch=stage_scratch,
    )(section_one, *second_halos, x)

    footpoint_potential = call(
        functools.partial(gather_kernel, width, columns, not fast), shape_of(cells, lats), "gather"
    )(table, nodes)
    return (
        state_next.reshape(state.shape),
        potential,
        footpoint_potential.reshape(footpoints.shape),
    )


def solution(mesh):
    return jax.shard_map(
        body,
        mesh=mesh,
        in_specs=(
            P(None, "radial", "shell", None),
            P("radial", "shell", None),
            P(None, "shell", "radial"),
            P("shell", "radial", None, None),
        ),
        out_specs=(
            P(None, "radial", "shell", None),
            P("shell", "radial"),
            P("radial", "shell", None),
        ),
        check_vma=False,
    )
```

time: 456 us -> 64.9 us (0.14)
  local copies, waits for them, and re-layouts: 198 us -> 1.78 us
  other arithmetic: 159 us -> 0 us
  starting transfers between devices: 49.9 us -> 27.7 us
  Pallas kernels: 0 us -> 15.7 us
  between operations: 15.5 us -> 0.74 us
  waiting for transfers between devices: 26.4 us -> 18.6 us
    gather x1 -> x0, local copies, waits for them, and re-layouts: 161 us -> none  [body(): footpoint_potential = block_columns.reshape(-1)[node_slot]]
    scatter-add x1 -> x0, other arithmetic: 112 us -> none  [body(): jax.ops.segment_sum(cell_current, node_slot.reshape(-1), num_segments=NLA...]
    ppermute x20 -> x12, starting transfers between devices: 37.3 us -> 20.2 us  [the longest x2 9.16 us: exchange_halos(): from_above = lax.ppermute(low, 'shell', ring('shell', -1, True))]
    slice x21 -> x0, local copies, waits for them, and re-layouts: 16.1 us -> none  [the longest x6 13.6 us: pad_latitude(): return jnp.pad(field, ((0, 0), (0, 0), (0, 0), (2, 2)), mode='edge')]
    pallas_call x0 -> x7, Pallas kernels: none -> 15.7 us  [the longest x1 5.11 us: body(): call(functools.partial(second_stage_kernel, layers), shape_of(fields, cel...]
    reduce_sum x12 -> x0, other arithmetic: 12.4 us -> none  [physical_flux(): field_sq = jnp.sum(magnetic * magnetic, axis=0)]
    sub x18 -> x0, other arithmetic: 10.8 us -> none  [the longest x6 5.85 us: face_divergence(): window_slice(padded, 1, cell_count + 3)]
    unnamed x178 -> x12, local copies, waits for them, and re-layouts: 11 us -> 1.78 us
  transfers between devices with their start and end apart: 23 -> 14, of which waited for: 12 -> 8; matrix products, arithmetic and copies ran while one was open for 39% -> 0% of each run, Pallas kernels for 0% -> 18%
where the time goes in v1:
time: 64.9 us; the launch traced here: 64.6 us
  starting transfers between devices  27.7 us (43%)
  waiting for transfers between devices  18.6 us (29%)
  Pallas kernels  15.7 us (24%)
  local copies, waits for them, and re-layouts  1.78 us (3%)
  between operations  0.74 us (1%)
    ppermute x2, starting transfers between devices, exchange_halos(): from_above = lax.ppermute(low, 'shell', ring('shell', -1, True))  9.16 us
    all_to_all x1, waiting for transfers between devices, body(): lax.all_to_all(sums, ('shell', 'radial'), split_axis=0, concat_axis=0, ti...  6.15 us
    ppermute x2, waiting for transfers between devices, exchange_halos(): from_below = lax.ppermute(high, 'shell', ring('shell', 1, True))  5.72 us
    pallas_call x1, Pallas kernels, body(): call(functools.partial(second_stage_kernel, layers), shape_of(fields, cel...  5.11 us
    all_to_all x1, starting transfers between devices, body(): lax.all_to_all(sums, ('shell', 'radial'), split_axis=0, concat_axis=0, ti...  4.89 us
    ppermute x1, starting transfers between devices, body(): own_low = lax.ppermute(rim_high, 'shell', ring('shell', 1, False))  4.47 us
    pallas_call x1, Pallas kernels, body(): call(functools.partial(first_stage_kernel, layers), [shape_of(fields, cel...  4.36 us
    ppermute x2, starting transfers between devices, exchange_halos(): from_below = lax.ppermute(high, 'shell', ring('shell', 1, True))  4.23 us
  transfers between devices with their start and end apart: 14, of which 8 were waited for; matrix products, arithmetic and copies ran while one was open for 0% of the time, Pallas kernels for 18%

profile of v1, /device:TPU:0, one launch (start us, length us, event | category | flops | bytes accessed | tf_op | source)
XLA Modules:
  0.0 64.6 jit_solution(14229695946585832183)
XLA Ops:
  0.6 0.5 collective-permute-start.8
  1.2 1.0 %copy-done.1 = f32[8,1,128,128]{3,2,1,0:T(8,128)S(1)} copy-done((f32[8,1,128,128]{3,2,1,0:T(8,128)S(1)}, f32[8,1,128,128]{3,2,1,0:T(8,128)}, u32[]{:S(2)}) %copy-start.1) | copy-done | bytes 524312
  2.2 0.7 %copy-done.4 = f32[4,8,128]{2,1,0:T(8,128)S(1)} copy-done((f32[4,8,128]{2,1,0:T(8,128)S(1)}, f32[4,8,128]{2,1,0:T(8,128)}, u32[]{:S(2)}) %copy-start.4) | copy-done | bytes 16408
  3.0 4.5 %collective-permute-start.6 = (f32[3,136,128]{2,1,0:T(8,128)S(1)}, f32[3,136,128]{2,1,0:T(8,128)S(1)}, u32[]{:S(2)}, u32[]{:S(2)}) collective-permute-start(f32[3,136,128]{2,1,0:T(8,128)S(1)} %get-tuple-element.21), channel_id=1, source_target_pairs={{0,2},{2,4},{4,6},{6,8},{8,10},{10,12},{12,14},{14,16},{16,18},{18... | collective-permute-start | bytes 626696 | tf_op jit(solution)/shard_map/ppermute | solution.py:512
  7.4 1.3 %collective-permute-start.7 = (f32[3,136,128]{2,1,0:T(8,128)S(1)}, f32[3,136,128]{2,1,0:T(8,128)S(1)}, u32[]{:S(2)}, u32[]{:S(2)}) collective-permute-start(f32[3,136,128]{2,1,0:T(8,128)S(1)} %get-tuple-element.22), channel_id=1, source_target_pairs={{2,0},{4,2},{6,4},{8,6},{10,8},{12,10},{14,12},{16,14},{18,16},{20... | collective-permute-start | bytes 626696 | tf_op jit(solution)/shard_map/ppermute | solution.py:513
  8.7 0.0 copy-start.3
  8.8 0.1 pack.1
  8.8 0.2 collective-permute-start.2
  9.0 2.5 %collective-permute-start = (f32[8,2,16,128]{3,2,1,0:T(8,128)S(1)}, f32[8,2,16,128]{3,2,1,0:T(8,128)S(1)}, u32[]{:S(2)}, u32[]{:S(2)}) collective-permute-start(f32[8,2,16,128]{3,2,1,0:T(8,128)S(1)} %get-tuple-element.14), channel_id=1, source_target_pairs={{0,2},{2,4},{4,6},{6,8},{8,10},{10,12},{12,14},{14,16},{16,18},{18... | collective-permute-start | bytes 393224 | tf_op jit(solution)/shard_map/ppermute | solution.py:448
  11.6 5.2 %collective-permute-start.1 = (f32[8,2,16,128]{3,2,1,0:T(8,128)S(1)}, f32[8,2,16,128]{3,2,1,0:T(8,128)S(1)}, u32[]{:S(2)}, u32[]{:S(2)}) collective-permute-start(f32[8,2,16,128]{3,2,1,0:T(8,128)S(1)} %get-tuple-element.15), channel_id=1, source_target_pairs={{0,30},{2,0},{4,2},{6,4},{8,6},{10,8},{12,10},{14,12},{16,14},{18,... | collective-permute-start | bytes 393224 | tf_op jit(solution)/shard_map/ppermute | solution.py:449
  16.8 0.0 collective-permute-done.6.own_low
  16.8 0.0 collective-permute-start.10
  16.8 2.5 %collective-permute-done.7.own_high = f32[3,136,128]{2,1,0:T(8,128)S(1)} collective-permute-done((f32[3,136,128]{2,1,0:T(8,128)S(1)}, f32[3,136,128]{2,1,0:T(8,128)S(1)}, u32[]{:S(2)}, u32[]{:S(2)}) %collective-permute-start.7) | collective-permute-done | bytes 208928 | tf_op jit(solution)/shard_map/ppermute | solution.py:513
  19.3 0.0 collective-permute-start.11
  19.3 3.2 %collective-permute-done.low = f32[8,2,16,128]{3,2,1,0:T(8,128)S(1)} collective-permute-done((f32[8,2,16,128]{3,2,1,0:T(8,128)S(1)}, f32[8,2,16,128]{3,2,1,0:T(8,128)S(1)}, u32[]{:S(2)}, u32[]{:S(2)}) %collective-permute-start) | collective-permute-done | bytes 131104 | tf_op jit(solution)/shard_map/ppermute | solution.py:448
  22.5 1.9 %collective-permute-done.1.high = f32[8,2,16,128]{3,2,1,0:T(8,128)S(1)} collective-permute-done((f32[8,2,16,128]{3,2,1,0:T(8,128)S(1)}, f32[8,2,16,128]{3,2,1,0:T(8,128)S(1)}, u32[]{:S(2)}, u32[]{:S(2)}) %collective-permute-start.1) | collective-permute-done | bytes 131104 | tf_op jit(solution)/shard_map/ppermute | solution.py:449
  24.5 2.1 %currents.1 = f32[128,128]{1,0:T(8,128)} custom-call(f32[8,128,128]{2,1,0:T(8,128)S(1)} %bitcast.10, f32[8,2,16,128]{3,2,1,0:T(8,128)S(1)} %collective-permute-done.low, f32[8,2,16,128]{3,2,1,0:T(8,128)S(1)} %collective-permute-done.1.high, f32[8,16,128]{2,1,0:T(8,128)S(1)} %collective-permute-done.2.edge, s32[128,128]{1,0:T(8,128)S(1)} %bitcast.18), custom_call_target="tpu_custom_call" | custom-call | flops 10000000 | bytes 1000000 | tf_op jit(solution)/shard_map/currents/pallas_call | solution.py:518
  26.6 4.9 %all-to-all-start = ((f32[32,4,128]{2,1,0:T(4,128)}), f32[32,4,128]{2,1,0:T(4,128)S(1)}, u32[]{:S(2)}, u32[]{:S(2)}) async-start(f32[32,4,128]{2,1,0:T(4,128)} %bitcast.3), calls=%async_computation | async-start | bytes 131072 | tf_op jit(solution)/shard_map/all_to_all | solution.py:537
  31.5 0.3 collective-permute-start.9
  31.8 0.9 %collective-permute-done.9.twin_conductance = f32[4,8,128]{2,1,0:T(8,128)S(1)} collective-permute-done((f32[4,8,128]{2,1,0:T(8,128)S(1)}, f32[4,8,128]{2,1,0:T(8,128)S(1)}, u32[]{:S(2)}, u32[]{:S(2)}) %collective-permute-start.9) | collective-permute-done | bytes 16416 | tf_op jit(solution)/shard_map/ppermute | solution.py:515
  32.7 6.1 %all-to-all-done = f32[32,4,128]{2,1,0:T(4,128)S(1)} async-done(((f32[32,4,128]{2,1,0:T(4,128)}), f32[32,4,128]{2,1,0:T(4,128)S(1)}, u32[]{:S(2)}, u32[]{:S(2)}) %all-to-all-start) | async-done | bytes 65568 | tf_op jit(solution)/shard_map/all_to_all | solution.py:537
  38.9 0.0 collective-permute-done.10.twin_low
  38.9 2.8 %sweeps.1 = (f32[8,128]{1,0:T(8,128)}, f32[256,128]{1,0:T(8,128)}) custom-call(f32[128,128]{1,0:T(8,128)S(1)} %bitcast.17, f32[8,128,128]{2,1,0:T(8,128)S(1)} %bitcast.15, f32[4,8,128]{2,1,0:T(8,128)S(1)} %copy-done.5, f32[3,136,128]{2,1,0:T(8,128)S(1)} %collective-permute-done.6.own_low, f32[3,136,128]{2,1,0:T(8,128)S(1)} %collective-permute-done.7.own_high, ...), custom_call_target="tpu_custom_call" | custom-call | flops 1000000 | bytes 1000000 | tf_op jit(solution)/shard_map/sweeps/pallas_call | solution.py:538
  41.7 2.6 %all-to-all-start.1 = ((f32[32,8,128]{2,1,0:T(8,128)}), f32[32,8,128]{2,1,0:T(8,128)S(1)}, u32[]{:S(2)}, u32[]{:S(2)}) async-start(f32[32,8,128]{2,1,0:T(8,128)} %bitcast.6), calls=%async_computation.1 | async-start | bytes 262144 | tf_op jit(solution)/shard_map/all_to_all | solution.py:548
  44.3 4.4 %first_stage.1 = (f32[8,128,128]{2,1,0:T(8,128)S(1)}, f32[8,2,16,128]{3,2,1,0:T(8,128)S(1)}, f32[8,2,16,128]{3,2,1,0:T(8,128)S(1)}, f32[8,16,128]{2,1,0:T(8,128)S(1)}) custom-call(f32[8,128,128]{2,1,0:T(8,128)S(1)} %bitcast.11, f32[8,2,16,128]{3,2,1,0:T(8,128)S(1)} %collective-permute-done.low, f32[8,2,16,128]{3,2,1,0:T(8,128)S(1)} %collective-permute-done.1.high, ...), custom_call_target="tpu_custom_call" | custom-call | flops 20000000 | bytes 1000000 | tf_op jit(solution)/shard_map/first_stage/pallas_call | solution.py:526
  48.7 1.7 %collective-permute-start.3 = (f32[8,2,16,128]{3,2,1,0:T(8,128)S(1)}, f32[8,2,16,128]{3,2,1,0:T(8,128)S(1)}, u32[]{:S(2)}, u32[]{:S(2)}) collective-permute-start(f32[8,2,16,128]{3,2,1,0:T(8,128)S(1)} %get-tuple-element.18), channel_id=1, source_target_pairs={{0,2},{2,4},{4,6},{6,8},{8,10},{10,12},{12,14},{14,16},{16,18},{18... | collective-permute-start | bytes 393224 | tf_op jit(solution)/shard_map/ppermute | solution.py:448
  50.4 4.0 %collective-permute-start.4 = (f32[8,2,16,128]{3,2,1,0:T(8,128)S(1)}, f32[8,2,16,128]{3,2,1,0:T(8,128)S(1)}, u32[]{:S(2)}, u32[]{:S(2)}) collective-permute-start(f32[8,2,16,128]{3,2,1,0:T(8,128)S(1)} %get-tuple-element.19), channel_id=1, source_target_pairs={{0,30},{2,0},{4,2},{6,4},{8,6},{10,8},{12,10},{14,12},{16,14},{18,... | collective-permute-start | bytes 393224 | tf_op jit(solution)/shard_map/ppermute | solution.py:449
  54.3 1.3 %collective-permute-done.5.edge = f32[8,16,128]{2,1,0:T(8,128)S(1)} collective-permute-done((f32[8,16,128]{2,1,0:T(8,128)S(1)}, f32[8,16,128]{2,1,0:T(8,128)S(1)}, u32[]{:S(2)}, u32[]{:S(2)}) %collective-permute-start.5) | collective-permute-done | bytes 65568 | tf_op jit(solution)/shard_map/ppermute | solution.py:450
  55.6 2.5 %collective-permute-done.3.low = f32[8,2,16,128]{3,2,1,0:T(8,128)S(1)} collective-permute-done((f32[8,2,16,128]{3,2,1,0:T(8,128)S(1)}, f32[8,2,16,128]{3,2,1,0:T(8,128)S(1)}, u32[]{:S(2)}, u32[]{:S(2)}) %collective-permute-start.3) | collective-permute-done | bytes 131104 | tf_op jit(solution)/shard_map/ppermute | solution.py:448
  58.1 0.1 collective-permute-done.4.high
  58.2 5.1 %second_stage.1 = f32[8,128,128]{2,1,0:T(8,128)} custom-call(f32[8,128,128]{2,1,0:T(8,128)S(1)} %get-tuple-element.17.x_ref, f32[8,2,16,128]{3,2,1,0:T(8,128)S(1)} %collective-permute-done.3.low, f32[8,2,16,128]{3,2,1,0:T(8,128)S(1)} %collective-permute-done.4.high, f32[8,16,128]{2,1,0:T(8,128)S(1)} %collective-permute-done.5.edge, f32[8,128,128]{2,1,0:T(8,128)S(1)} %bitcast.12), custom_call_target="tpu_custom_call" | custom-call | flops 20000000 | bytes 1000000 | tf_op jit(solution)/shard_map/second_stage/pallas_call | solution.py:553
  63.3 1.3 %gather.1 = f32[128,128]{1,0:T(8,128)} custom-call(f32[16,2,8,128]{3,2,1,0:T(8,128)S(1)} %bitcast.16, s32[128,128]{1,0:T(8,128)S(1)} %bitcast.19), custom_call_target="tpu_custom_call" | custom-call | flops 1000000 | bytes 1000000 | tf_op jit(solution)/shard_map/gather/pallas_call | solution.py:561
  (15 shorter events, 0.1 us)
Async XLA Ops:
  0.6 8.1 %copy-start = (f32[8,16,8,128]{3,2,1,0:T(8,128)S(1)}, f32[8,16,8,128]{3,2,1,0:T(8,128)}, u32[]{:S(2)}) copy-start(f32[8,16,8,128]{3,2,1,0:T(8,128)} %param.4) | copy-start | bytes 1572868
  0.6 38.2 %collective-permute-start.8 = (f32[8,128,128]{2,1,0:T(8,128)}, f32[8,128,128]{2,1,0:T(8,128)S(1)}, u32[]{:S(2)}, u32[]{:S(2)}) collective-permute-start(f32[8,128,128]{2,1,0:T(8,128)} %bitcast.13), channel_id=1, source_target_pairs={{0,1},{1,0},{2,3},{3,2},{4,5},{5,4},{6,7},{7,6},{8,9},{9,8},{10,11... | collective-permute-start | bytes 1572872 | tf_op jit(solution)/shard_map/ppermute | solution.py:515
  1.2 1.0 %copy-start.1 = (f32[8,1,128,128]{3,2,1,0:T(8,128)S(1)}, f32[8,1,128,128]{3,2,1,0:T(8,128)}, u32[]{:S(2)}) copy-start(f32[8,1,128,128]{3,2,1,0:T(8,128)} %param.7) | copy-start | bytes 1572868
  2.2 0.7 %copy-start.4 = (f32[4,8,128]{2,1,0:T(8,128)S(1)}, f32[4,8,128]{2,1,0:T(8,128)}, u32[]{:S(2)}) copy-start(f32[4,8,128]{2,1,0:T(8,128)} %own_conductance.1) | copy-start | bytes 49156
  3.0 13.8 %collective-permute-start.6 = (f32[3,136,128]{2,1,0:T(8,128)S(1)}, f32[3,136,128]{2,1,0:T(8,128)S(1)}, u32[]{:S(2)}, u32[]{:S(2)}) collective-permute-start(f32[3,136,128]{2,1,0:T(8,128)S(1)} %get-tuple-element.21), channel_id=1, source_target_pairs={{0,2},{2,4},{4,6},{6,8},{8,10},{10,12},{12,14},{14,16},{16,18},{18... | collective-permute-start | bytes 626696 | tf_op jit(solution)/shard_map/ppermute | solution.py:512
  7.4 11.9 %collective-permute-start.7 = (f32[3,136,128]{2,1,0:T(8,128)S(1)}, f32[3,136,128]{2,1,0:T(8,128)S(1)}, u32[]{:S(2)}, u32[]{:S(2)}) collective-permute-start(f32[3,136,128]{2,1,0:T(8,128)S(1)} %get-tuple-element.22), channel_id=1, source_target_pairs={{2,0},{4,2},{6,4},{8,6},{10,8},{12,10},{14,12},{16,14},{18,16},{20... | collective-permute-start | bytes 626696 | tf_op jit(solution)/shard_map/ppermute | solution.py:513
  8.7 15.7 %copy-start.3 = (s32[16,8,128]{2,1,0:T(8,128)S(1)}, s32[16,8,128]{2,1,0:T(8,128)}, u32[]{:S(2)}) copy-start(s32[16,8,128]{2,1,0:T(8,128)} %param.5) | copy-start | bytes 196612
  8.8 2.8 %collective-permute-start.2 = (f32[8,16,128]{2,1,0:T(8,128)S(1)}, f32[8,16,128]{2,1,0:T(8,128)S(1)}, u32[]{:S(2)}, u32[]{:S(2)}) collective-permute-start(f32[8,16,128]{2,1,0:T(8,128)S(1)} %get-tuple-element.16), channel_id=1, source_target_pairs={{0,1},{1,0},{2,3},{3,2},{4,5},{5,4},{6,7},{7,6},{8,9},{9,8},{10,11... | collective-permute-start | bytes 196616 | tf_op jit(solution)/shard_map/ppermute | solution.py:450
  9.0 13.5 %collective-permute-start = (f32[8,2,16,128]{3,2,1,0:T(8,128)S(1)}, f32[8,2,16,128]{3,2,1,0:T(8,128)S(1)}, u32[]{:S(2)}, u32[]{:S(2)}) collective-permute-start(f32[8,2,16,128]{3,2,1,0:T(8,128)S(1)} %get-tuple-element.14), channel_id=1, source_target_pairs={{0,2},{2,4},{4,6},{6,8},{8,10},{10,12},{12,14},{14,16},{16,18},{18... | collective-permute-start | bytes 393224 | tf_op jit(solution)/shard_map/ppermute | solution.py:448
  11.6 12.9 %collective-permute-start.1 = (f32[8,2,16,128]{3,2,1,0:T(8,128)S(1)}, f32[8,2,16,128]{3,2,1,0:T(8,128)S(1)}, u32[]{:S(2)}, u32[]{:S(2)}) collective-permute-start(f32[8,2,16,128]{3,2,1,0:T(8,128)S(1)} %get-tuple-element.15), channel_id=1, source_target_pairs={{0,30},{2,0},{4,2},{6,4},{8,6},{10,8},{12,10},{14,12},{16,14},{18,... | collective-permute-start | bytes 393224 | tf_op jit(solution)/shard_map/ppermute | solution.py:449
  16.8 22.1 %collective-permute-start.10 = (f32[3,136,128]{2,1,0:T(8,128)S(1)}, f32[3,136,128]{2,1,0:T(8,128)S(1)}, u32[]{:S(2)}, u32[]{:S(2)}) collective-permute-start(f32[3,136,128]{2,1,0:T(8,128)S(1)} %collective-permute-done.6.own_low), channel_id=1, source_target_pairs={{0,1},{1,0},{2,3},{3,2},{4,5},{5,4},{6,7},{7,6},{8,9},{9,8},{10,11... | collective-permute-start | bytes 626696 | tf_op jit(solution)/shard_map/ppermute | solution.py:515
  19.3 19.6 %collective-permute-start.11 = (f32[3,136,128]{2,1,0:T(8,128)S(1)}, f32[3,136,128]{2,1,0:T(8,128)S(1)}, u32[]{:S(2)}, u32[]{:S(2)}) collective-permute-start(f32[3,136,128]{2,1,0:T(8,128)S(1)} %collective-permute-done.7.own_high), channel_id=1, source_target_pairs={{0,1},{1,0},{2,3},{3,2},{4,5},{5,4},{6,7},{7,6},{8,9},{9,8},{10,11... | collective-permute-start | bytes 626696 | tf_op jit(solution)/shard_map/ppermute | solution.py:515
  24.5 14.4 %copy-start.2 = (f32[8,1,128,128]{3,2,1,0:T(8,128)S(1)}, f32[8,1,128,128]{3,2,1,0:T(8,128)}, u32[]{:S(2)}) copy-start(f32[8,1,128,128]{3,2,1,0:T(8,128)} %param.7) | copy-start | bytes 1572868
  26.6 4.9 %copy-start.5 = (f32[4,8,128]{2,1,0:T(8,128)S(1)}, f32[4,8,128]{2,1,0:T(8,128)}, u32[]{:S(2)}) copy-start(f32[4,8,128]{2,1,0:T(8,128)} %own_conductance.1) | copy-start | bytes 49156
  26.6 12.3 %all-to-all-start = ((f32[32,4,128]{2,1,0:T(4,128)}), f32[32,4,128]{2,1,0:T(4,128)S(1)}, u32[]{:S(2)}, u32[]{:S(2)}) async-start(f32[32,4,128]{2,1,0:T(4,128)} %bitcast.3), calls=%async_computation | async-start | bytes 131072 | tf_op jit(solution)/shard_map/all_to_all | solution.py:537
  31.5 1.2 %collective-permute-start.9 = (f32[4,8,128]{2,1,0:T(8,128)S(1)}, f32[4,8,128]{2,1,0:T(8,128)S(1)}, u32[]{:S(2)}, u32[]{:S(2)}) collective-permute-start(f32[4,8,128]{2,1,0:T(8,128)S(1)} %copy-done.5), channel_id=1, source_target_pairs={{0,1},{1,0},{2,3},{3,2},{4,5},{5,4},{6,7},{7,6},{8,9},{9,8},{10,11... | collective-permute-start | bytes 49160 | tf_op jit(solution)/shard_map/ppermute | solution.py:515
  41.7 21.6 %all-to-all-start.1 = ((f32[32,8,128]{2,1,0:T(8,128)}), f32[32,8,128]{2,1,0:T(8,128)S(1)}, u32[]{:S(2)}, u32[]{:S(2)}) async-start(f32[32,8,128]{2,1,0:T(8,128)} %bitcast.6), calls=%async_computation.1 | async-start | bytes 262144 | tf_op jit(solution)/shard_map/all_to_all | solution.py:548
  48.7 9.4 %collective-permute-start.3 = (f32[8,2,16,128]{3,2,1,0:T(8,128)S(1)}, f32[8,2,16,128]{3,2,1,0:T(8,128)S(1)}, u32[]{:S(2)}, u32[]{:S(2)}) collective-permute-start(f32[8,2,16,128]{3,2,1,0:T(8,128)S(1)} %get-tuple-element.18), channel_id=1, source_target_pairs={{0,2},{2,4},{4,6},{6,8},{8,10},{10,12},{12,14},{14,16},{16,18},{18... | collective-permute-start | bytes 393224 | tf_op jit(solution)/shard_map/ppermute | solution.py:448
  50.4 7.8 %collective-permute-start.4 = (f32[8,2,16,128]{3,2,1,0:T(8,128)S(1)}, f32[8,2,16,128]{3,2,1,0:T(8,128)S(1)}, u32[]{:S(2)}, u32[]{:S(2)}) collective-permute-start(f32[8,2,16,128]{3,2,1,0:T(8,128)S(1)} %get-tuple-element.19), channel_id=1, source_target_pairs={{0,30},{2,0},{4,2},{6,4},{8,6},{10,8},{12,10},{14,12},{16,14},{18,... | collective-permute-start | bytes 393224 | tf_op jit(solution)/shard_map/ppermute | solution.py:449
  54.3 1.3 %collective-permute-start.5 = (f32[8,16,128]{2,1,0:T(8,128)S(1)}, f32[8,16,128]{2,1,0:T(8,128)S(1)}, u32[]{:S(2)}, u32[]{:S(2)}) collective-permute-start(f32[8,16,128]{2,1,0:T(8,128)S(1)} %get-tuple-element.20), channel_id=1, source_target_pairs={{0,1},{1,0},{2,3},{3,2},{4,5},{5,4},{6,7},{7,6},{8,9},{9,8},{10,11... | collective-permute-start | bytes 196616 | tf_op jit(solution)/shard_map/ppermute | solution.py:450

commit v2 on v1

--- a/solution.py
+++ b/solution.py
@@ -15,12 +15,16 @@
 SUB = 8
 PARTS = 3
 VMEM_LIMIT = 40 * 1024 * 1024
-
-
-def call(kernel, out_shape, name, flops=1_000_000, nbytes=1_000_000, scratch=()):
+CHEAP, CURRENTS, RELAY, DEAR = 1_000, 2_000_000_000, 1_000, 10_000_000_000
+IN_VMEM = pl.BlockSpec(memory_space=pltpu.VMEM)
+UNREAD = pl.BlockSpec(memory_space=pl.ANY)
+
+
+def call(kernel, out_shape, name, flops=CHEAP, nbytes=1_000, scratch=(), **specs):
     return pl.pallas_call(
         kernel,
         out_shape=out_shape,
+        **specs,
         scratch_shapes=list(scratch),
         compiler_params=pltpu.CompilerParams(vmem_limit_bytes=VMEM_LIMIT),
         cost_estimate=pl.CostEstimate(flops=flops, bytes_accessed=nbytes, transcendentals=0),
@@ -106,19 +110,26 @@
     lax.fori_loop(1, cells + 1, step, (here, left, jump, flux), unroll=2)
 
 
-def pack_halos(source, low_ref, high_ref, edge_ref, layers, position):
+def parity():
+    return lax.axis_index("shell") & 1
+
+
+def pack_halos(source, pair_ref, next_ref, edge_ref, layers, position):
+    odd = parity()
+    to_pair, to_next = jnp.where(odd == 1, 0, SUB - 2), jnp.where(odd == 1, SUB - 2, 0)
     for k in range(8):
         for j in range(2):
-            low_ref[k, j] = source[k, pl.ds(j, layers, stride=SUB), :]
-            high_ref[k, j] = source[k, pl.ds(SUB - 2 + j, layers, stride=SUB), :]
+            pair_ref[k, j] = source[k, pl.ds(to_pair + j, layers, stride=SUB), :]
+            next_ref[k, j] = source[k, pl.ds(to_next + j, layers, stride=SUB), :]
     first = jnp.where(position == 0, (layers - 2) * SUB, 0)
     first = pl.multiple_of(first, SUB)
     for k in range(8):
         edge_ref[k] = source[k, pl.ds(first, 2 * SUB), :]
 
 
-def tendency_into(x_ref, low_ref, high_ref, edge_ref, xr, xl, div, layers, position, last, finish):
+def tendency_into(x_ref, pair_ref, next_ref, edge_ref, xr, xl, div, layers, position, last, finish):
     cells = layers * SUB
+    from_below = parity() == 1
     for k in range(8):
         xr[k, 2 * SUB : 2 * SUB + cells] = x_ref[k]
         first, final = x_ref[k, 0:SUB], x_ref[k, cells - SUB : cells]
@@ -128,8 +139,9 @@
             xr[k, cells + (2 + j) * SUB : cells + (3 + j) * SUB] = jnp.where(
                 position == last, final, edge_ref[k, rows]
             )
-            xl[k, j * layers : (j + 1) * layers] = low_ref[k, j]
-            xl[k, (SUB + 2 + j) * layers : (SUB + 3 + j) * layers] = high_ref[k, j]
+            pair, after = pair_ref[k, j], next_ref[k, j]
+            xl[k, j * layers : (j + 1) * layers] = jnp.where(from_below, pair, after)
+            xl[k, (SUB + 2 + j) * layers : (SUB + 3 + j) * layers] = jnp.where(from_below, after, pair)
         for j in range(SUB):
             xl[k, (2 + j) * layers : (3 + j) * layers] = x_ref[k, pl.ds(j, layers, stride=SUB), :]
 
@@ -189,8 +201,12 @@
     pack_halos(x_ref, low_ref, high_ref, edge_ref, layers, lax.axis_index("radial"))
 
 
+def relay_kernel(*refs):
+    pass
+
+
 def first_stage_kernel(
-    layers, x_ref, low, high, edge, out_ref, low_ref, high_ref, edge_ref, xr, xl, div
+    layers, x_ref, low, high, edge, _, out_ref, low_ref, high_ref, edge_ref, xr, xl, div
 ):
     position, last = lax.axis_index("radial"), lax.axis_size("radial") - 1
 
@@ -202,7 +218,7 @@
     pack_halos(out_ref, low_ref, high_ref, edge_ref, layers, position)
 
 
-def second_stage_kernel(layers, x_ref, low, high, edge, state_ref, out_ref, xr, xl, div):
+def second_stage_kernel(layers, x_ref, low, high, edge, state_ref, _, out_ref, xr, xl, div):
     position, last = lax.axis_index("radial"), lax.axis_size("radial") - 1
 
     def finish(rows, x, total):
@@ -230,7 +246,10 @@
     return parts
 
 
-def current_kernel(layers, width, columns, window, x_ref, low, high, edge, nodes_ref, out_ref, held):
+def current_kernel(layers, width, columns, window, x_ref, pair, after, edge, nodes_ref, out_ref, held):
+    from_below = parity() == 1
+    below_all = [None if k == 1 else jnp.where(from_below, pair[4 + k, 1], after[4 + k, 1]) for k in range(3)]
+    above_all = [None if k == 1 else jnp.where(from_below, after[4 + k, 0], pair[4 + k, 0]) for k in range(3)]
     position, last = lax.axis_index("radial"), lax.axis_size("radial") - 1
     first_column = lax.axis_index("shell") * width
     lane, sub = lane_index(SUB), row_index(SUB)
@@ -256,8 +275,8 @@
         return 0.5 * (above - below)
 
     def lon_pair(k, r, value):
-        above = jnp.where(sub == SUB - 1, high[4 + k, 0, r : r + 1, :], pltpu.roll(value, SUB - 1, 0))
-        below = jnp.where(sub == 0, low[4 + k, 1, r : r + 1, :], pltpu.roll(value, 1, 0))
+        above = jnp.where(sub == SUB - 1, above_all[k][r : r + 1, :], pltpu.roll(value, SUB - 1, 0))
+        below = jnp.where(sub == 0, below_all[k][r : r + 1, :], pltpu.roll(value, 1, 0))
         return 0.5 * (above - below)
 
     total = jnp.zeros((PARTS * groups, LANES), jnp.float32)
@@ -299,15 +318,16 @@
             out_ref[pl.ds(twin * 4 + j, groups, stride=8), :] = held[SUB - 1 + j : SUB - 1 + j + groups]
 
 
-def rim_kernel(blocks_ref, conductance_ref, low_ref, high_ref):
-    rows = blocks_ref.shape[0]
+def rim_kernel(blocks_ref, conductance_ref, _, pair_ref, next_ref):
     size = blocks_ref.shape[1]
-    for ref, first in ((low_ref, 0), (high_ref, rows - HALO)):
+    high = blocks_ref.shape[0] - HALO
+    odd = parity()
+    for ref, first in ((pair_ref, jnp.where(odd == 1, 0, high)), (next_ref, jnp.where(odd == 1, high, 0))):
         ref[...] = jnp.zeros_like(ref)
         for e in range(HALO):
             ref[e, :size] = blocks_ref[first + e]
             for way in range(4):
-                ref[e, size + way : size + way + 1] = conductance_ref[way, first + e : first + e + 1]
+                ref[e, size + way : size + way + 1] = conductance_ref[way, pl.ds(first + e, 1)]
 
 
 def swap_blocks(tile, piece):
@@ -326,12 +346,13 @@
     arrived,
     own_blocks,
     own_conductance,
-    own_low,
-    own_high,
+    own_pair,
+    own_next,
     twin_blocks,
     twin_conductance,
-    twin_low,
-    twin_high,
+    twin_pair,
+    twin_next,
+    _,
     out_ref,
     send_ref,
     pot,
@@ -355,25 +376,30 @@
     currents = [own_currents, twin_currents]
 
     cond[...] = jnp.zeros_like(cond)
-    sources = ((own_conductance, own_low, own_high), (twin_conductance, twin_low, twin_high))
-    for side, (mid, low, high) in enumerate(sources):
+    odd = parity()
+    rims = ((own_pair, twin_pair, odd == 1), (own_next, twin_next, odd == 0))
+
+    def rim_rows(reach):
+        for own, twin, is_low in rims:
+            for i in range(reach):
+                row = jnp.where(is_low, HALO - reach + i, i)
+                yield own, twin, row, jnp.where(is_low, SUB - reach + i, 2 * SUB + i)
+
+    for side, mid in enumerate((own_conductance, twin_conductance)):
         for way in range(4):
             cond[side, way, SUB : 2 * SUB] = mid[way]
-            for e in range(HALO):
-                row = size + way
-                cond[side, way, SUB - HALO + e : SUB - HALO + e + 1] = low[e, row : row + 1]
-                cond[side, way, 2 * SUB + e : 2 * SUB + e + 1] = high[e, row : row + 1]
+    for own, twin, row, place in rim_rows(HALO):
+        for side, rim in enumerate((own, twin)):
+            for way in range(4):
+                cond[side, way, pl.ds(place, 1)] = rim[row, size + way : size + way + 1]
     pot[...] = jnp.zeros_like(pot)
     eye = row_index(size, size) == lane_index(size, size)
-    blocks = ((own_blocks, own_low, own_high), (twin_blocks, twin_low, twin_high))
-
-    def matrix(side, e):
-        mid, low, high = blocks[side]
-        if e < SUB:
-            return low[e - (SUB - HALO), :size]
-        if e < 2 * SUB:
-            return mid[e - SUB]
-        return high[e - 2 * SUB, :size]
+
+    def solve_row(side, matrix, row):
+        product = matrix * rhs_ref[side, pl.ds(row, 1)]
+        column = jnp.sum(product, axis=1, keepdims=True)
+        line = jnp.sum(jnp.where(eye, column, 0.0), axis=0, keepdims=True)
+        pot[side, pl.ds(base + row, 1)] = line
 
     lane = lane_index(span)
     for sweep in range(ITERS_I):
@@ -397,12 +423,12 @@
                 rhs.append(coupled)
         for side in sides:
             rhs_ref[side] = rhs[side]
+        for own, twin, row, place in rim_rows(reach):
+            for side, rim in enumerate((own, twin)):
+                solve_row(side, rim[row, :size], place)
         for side in sides:
-            for e in range(SUB - reach, 2 * SUB + reach):
-                product = matrix(side, e) * rhs_ref[side, e : e + 1]
-                column = jnp.sum(product, axis=1, keepdims=True)
-                line = jnp.sum(jnp.where(eye, column, 0.0), axis=0, keepdims=True)
-                pot[side, base + e : base + e + 1] = line
+            for e in range(SUB):
+                solve_row(side, (own_blocks, twin_blocks)[side][e], SUB + e)
     result = pot[0, base + SUB : base + 2 * SUB]
     out_ref[...] = result
     for d in range(send_ref.shape[0] // rows):
@@ -444,11 +470,23 @@
     return [(i, j) for i, j in pairs if 0 <= j < count]
 
 
-def exchange_halos(low, high, edge):
-    from_below = lax.ppermute(high, "shell", ring("shell", 1, True))
-    from_above = lax.ppermute(low, "shell", ring("shell", -1, True))
-    other = lax.ppermute(edge, "radial", [(0, 1), (1, 0)])
-    return from_below, from_above, other
+def pairs(first, periodic):
+    count = lax.axis_size("shell")
+    assert count % 2 == 0
+    out = []
+    for i in range(first, count, 2):
+        if i + 1 < count or periodic:
+            j = (i + 1) % count
+            out += [(i, j), (j, i)]
+    return out
+
+
+def exchange_halos(pair, after, edge):
+    return (
+        lax.ppermute(pair, "shell", pairs(0, True)),
+        lax.ppermute(after, "shell", pairs(1, True)),
+        lax.ppermute(edge, "radial", [(0, 1), (1, 0)]),
+    )
 
 
 def padded_2(block, sides, width):
@@ -508,32 +546,46 @@
 
     if fast:
         rim_shape = shape_of(HALO, half + SUB, half)
-        rim_low, rim_high = call(rim_kernel, [rim_shape, rim_shape], "rim")(blocks, conductance)
-        own_low = lax.ppermute(rim_high, "shell", ring("shell", 1, False))
-        own_high = lax.ppermute(rim_low, "shell", ring("shell", -1, False))
-        twin = [(0, 1), (1, 0)]
-        twin_parts = [lax.ppermute(v, "radial", twin) for v in (blocks, conductance, own_low, own_high)]
+        rim_pair, rim_next = call(
+            rim_kernel, [rim_shape, rim_shape], "rim", in_specs=[IN_VMEM, IN_VMEM, UNREAD]
+        )(blocks, conductance, packed[2])
+        rims = [
+            lax.ppermute(rim_pair, "shell", pairs(0, False)),
+            lax.ppermute(rim_next, "shell", pairs(1, False)),
+        ]
 
     send_shape = shape_of(shells * radials * 4, LANES) if fast else shape_of(width, LANES)
     sums = call(
         functools.partial(current_kernel, layers, width, columns, fast),
         send_shape,
         "currents",
-        flops=10_000_000,
+        flops=CURRENTS,
         scratch=[pltpu.VMEM((max(16, width) + 2 * SUB, LANES), jnp.float32)],
     )(x, below, above, other, nodes)
 
-    stage = call(
+    section_one, *packed = call(
         functools.partial(first_stage_kernel, layers),
         [shape_of(fields, cells, lats)] + halo_shapes,
         "first_stage",
-        flops=20_000_000,
+        flops=DEAR,
         scratch=stage_scratch,
-    )(x, below, above, other)
-    section_one = stage[0]
-    second_halos = exchange_halos(*stage[1:])
+        in_specs=[IN_VMEM] * 4 + [UNREAD],
+    )(x, below, above, other, sums)
+    second_halos = exchange_halos(*packed)
+    after = sums
 
     if fast:
+        rims = call(
+            relay_kernel,
+            [rim_shape] * 2,
+            "relay",
+            flops=RELAY,
+            in_specs=[UNREAD] * 3,
+            out_specs=[UNREAD] * 2,
+            input_output_aliases={0: 0, 1: 1},
+        )(*rims, sums)
+        twin = [(0, 1), (1, 0)]
+        twin_parts = [lax.ppermute(v, "radial", twin) for v in (blocks, conductance, *rims)]
         arrived = lax.all_to_all(sums, ("shell", "radial"), split_axis=0, concat_axis=0, tiled=True)
         potential, spread = call(
             functools.partial(sweep_kernel, width),
@@ -544,7 +596,10 @@
                 pltpu.VMEM((2, 3 * SUB, half), jnp.float32),
                 pltpu.VMEM((2, 4, 3 * SUB, half), jnp.float32),
             ],
-        )(arrived, blocks, conductance, own_low, own_high, *twin_parts)
+            flops=DEAR,
+            in_specs=[IN_VMEM] * 9 + [UNREAD],
+        )(arrived, blocks, conductance, *rims, *twin_parts, section_one)
+        after = spread
         table = lax.all_to_all(spread, ("shell", "radial"), split_axis=0, concat_axis=0, tiled=True)
         table = table.reshape(shells, radials, own_rows, half)
     else:
@@ -554,9 +609,10 @@
         functools.partial(second_stage_kernel, layers),
         shape_of(fields, cells, lats),
         "second_stage",
-        flops=20_000_000,
+        flops=DEAR,
         scratch=stage_scratch,
-    )(section_one, *second_halos, x)
+        in_specs=[IN_VMEM] * 5 + [UNREAD],
+    )(section_one, *second_halos, x, after)
 
     footpoint_potential = call(
         functools.partial(gather_kernel, width, columns, not fast), shape_of(cells, lats), "gather"

time: 64.9 us -> 48.8 us (0.75)
  waiting for transfers between devices: 18.6 us -> 3.98 us
  starting transfers between devices: 27.7 us -> 23.1 us
  local copies, waits for them, and re-layouts: 1.78 us -> 4.68 us
    ppermute x8, waiting for transfers between devices: 11.5 us -> 1.94 us  [the longest x2 1.92 us: exchange_halos(): lax.ppermute(after, 'shell', pairs(1, True))]
    all_to_all x1, waiting for transfers between devices: 6.15 us -> 0.01 us  [body(): lax.all_to_all(sums, ('shell', 'radial'), split_axis=0, concat_axis=0, ti...]
    ppermute x8, starting transfers between devices: 19.4 us -> 14.5 us  [the longest x2 8.5 us: exchange_halos(): lax.ppermute(after, 'shell', pairs(1, True))]
    unnamed x12 -> x18, local copies, waits for them, and re-layouts: 1.78 us -> 4.68 us
    all_to_all x1, waiting for transfers between devices: 0.01 us -> 2.03 us  [body(): lax.all_to_all(spread, ('shell', 'radial'), split_axis=0, concat_axis=0,...]
    ppermute x4, waiting for transfers between devices: 0.94 us -> 0.01 us  [body(): lax.ppermute(v, 'radial', twin)]
  transfers between devices with their start and end apart: 14 -> 14, of which waited for: 8 -> 2; matrix products, arithmetic and copies ran while one was open for 0% -> 0% of each run, Pallas kernels for 18% -> 30%
where the time goes in v2:
time: 48.8 us; the launch traced here: 48.4 us
  starting transfers between devices  23.1 us (47%)
  Pallas kernels  15.8 us (32%)
  local copies, waits for them, and re-layouts  4.68 us (10%)
  waiting for transfers between devices  3.98 us (8%)
  between operations  0.8 us (2%)
    ppermute x2, starting transfers between devices, exchange_halos(): lax.ppermute(after, 'shell', pairs(1, True))  8.5 us
    pallas_call x1, Pallas kernels, body(): call(functools.partial(second_stage_kernel, layers), shape_of(fields, cel...  5.12 us
    ppermute x2, starting transfers between devices, exchange_halos(): lax.ppermute(pair, 'shell', pairs(0, True))  4.96 us
    all_to_all x1, starting transfers between devices, body(): lax.all_to_all(sums, ('shell', 'radial'), split_axis=0, concat_axis=0, ti...  4.89 us
    unnamed x18, local copies, waits for them, and re-layouts  4.68 us
    pallas_call x1, Pallas kernels, body(): call(functools.partial(first_stage_kernel, layers), [shape_of(fields, cel...  4.36 us
    pallas_call x1, Pallas kernels, body(): call(functools.partial(sweep_kernel, width), [shape_of(own_rows, half), s...  2.85 us
    all_to_all x1, starting transfers between devices, body(): lax.all_to_all(spread, ('shell', 'radial'), split_axis=0, concat_axis=0,...  2.57 us
  transfers between devices with their start and end apart: 14, of which 2 were waited for; matrix products, arithmetic and copies ran while one was open for 0% of the time, Pallas kernels for 30%

profile of v2, /device:TPU:0, one launch (start us, length us, event | category | flops | bytes accessed | tf_op | source)
XLA Modules:
  0.0 48.4 jit_solution(11362121645736723000)
XLA Ops:
  0.6 1.1 %copy-done.1 = f32[8,16,8,128]{3,2,1,0:T(8,128)S(1)} copy-done((f32[8,16,8,128]{3,2,1,0:T(8,128)S(1)}, f32[8,16,8,128]{3,2,1,0:T(8,128)}, u32[]{:S(2)}) %copy-start.1) | copy-done | bytes 524312
  1.7 0.1 pack.1
  1.8 3.0 %collective-permute-start = (f32[8,2,16,128]{3,2,1,0:T(8,128)S(1)}, f32[8,2,16,128]{3,2,1,0:T(8,128)S(1)}, u32[]{:S(2)}, u32[]{:S(2)}) collective-permute-start(f32[8,2,16,128]{3,2,1,0:T(8,128)S(1)} %get-tuple-element.16), channel_id=1, source_target_pairs={{0,2},{2,0},{4,6},{6,4},{8,10},{10,8},{12,14},{14,12},{16,18},{18,... | collective-permute-start | bytes 393224 | tf_op jit(solution)/shard_map/ppermute | solution.py:486
  4.8 4.5 %collective-permute-start.1 = (f32[8,2,16,128]{3,2,1,0:T(8,128)S(1)}, f32[8,2,16,128]{3,2,1,0:T(8,128)S(1)}, u32[]{:S(2)}, u32[]{:S(2)}) collective-permute-start(f32[8,2,16,128]{3,2,1,0:T(8,128)S(1)} %get-tuple-element.17), channel_id=1, source_target_pairs={{2,4},{4,2},{6,8},{8,6},{10,12},{12,10},{14,16},{16,14},{18,20},{2... | collective-permute-start | bytes 393224 | tf_op jit(solution)/shard_map/ppermute | solution.py:487
  9.3 0.0 collective-permute-start.2
  9.3 0.7 %copy-done.4 = f32[4,8,128]{2,1,0:T(8,128)S(1)} copy-done((f32[4,8,128]{2,1,0:T(8,128)S(1)}, f32[4,8,128]{2,1,0:T(8,128)}, u32[]{:S(2)}) %copy-start.4) | copy-done | bytes 16408
  10.1 0.1 collective-permute-start.6
  10.2 0.7 %collective-permute-start.7 = (f32[3,136,128]{2,1,0:T(8,128)S(1)}, f32[3,136,128]{2,1,0:T(8,128)S(1)}, u32[]{:S(2)}, u32[]{:S(2)}) collective-permute-start(f32[3,136,128]{2,1,0:T(8,128)S(1)} %get-tuple-element.24), channel_id=1, source_target_pairs={{2,4},{4,2},{6,8},{8,6},{10,12},{12,10},{14,16},{16,14},{18,20},{2... | collective-permute-start | bytes 626696 | tf_op jit(solution)/shard_map/ppermute | solution.py:554
  10.9 0.0 collective-permute-done.2.edge
  10.9 0.6 %collective-permute-start.9 = (f32[4,8,128]{2,1,0:T(8,128)S(1)}, f32[4,8,128]{2,1,0:T(8,128)S(1)}, u32[]{:S(2)}, u32[]{:S(2)}) collective-permute-start(f32[4,8,128]{2,1,0:T(8,128)S(1)} %copy-done.5), channel_id=1, source_target_pairs={{0,1},{1,0},{2,3},{3,2},{4,5},{5,4},{6,7},{7,6},{8,9},{9,8},{10,11... | collective-permute-start | bytes 49160 | tf_op jit(solution)/shard_map/ppermute | solution.py:588
  11.5 0.0 collective-permute-done.pair.low
  11.5 0.1 collective-permute-start.8
  11.5 1.9 %collective-permute-done.1.after.high = f32[8,2,16,128]{3,2,1,0:T(8,128)S(1)} collective-permute-done((f32[8,2,16,128]{3,2,1,0:T(8,128)S(1)}, f32[8,2,16,128]{3,2,1,0:T(8,128)S(1)}, u32[]{:S(2)}, u32[]{:S(2)}) %collective-permute-start.1) | collective-permute-done | bytes 131104 | tf_op jit(solution)/shard_map/ppermute | solution.py:487
  13.5 2.1 %currents.1._.refs_2_ = f32[128,128]{1,0:T(8,128)} custom-call(f32[8,128,128]{2,1,0:T(8,128)S(1)} %bitcast.13, f32[8,2,16,128]{3,2,1,0:T(8,128)S(1)} %collective-permute-done.pair.low, f32[8,2,16,128]{3,2,1,0:T(8,128)S(1)} %collective-permute-done.1.after.high, f32[8,16,128]{2,1,0:T(8,128)S(1)} %collective-permute-done.2.edge, s32[128,128]{1,0:T(8,128)S(1)} %bitcast.18), custom_call_target="tpu_custom_call" | custom-call | flops 2000000000 | bytes 1000 | tf_op jit(solution)/shard_map/currents/pallas_call | solution.py:558
  15.6 4.9 %all-to-all-start = ((f32[32,4,128]{2,1,0:T(4,128)}), f32[32,4,128]{2,1,0:T(4,128)S(1)}, u32[]{:S(2)}, u32[]{:S(2)}) async-start(f32[32,4,128]{2,1,0:T(4,128)} %bitcast.2), calls=%async_computation | async-start | bytes 131072 | tf_op jit(solution)/shard_map/all_to_all | solution.py:589
  20.5 0.0 collective-permute-done.6.refs_0_
  20.5 0.3 collective-permute-start.10
  20.8 0.3 collective-permute-start.11
  21.1 4.4 %first_stage.1 = (f32[8,128,128]{2,1,0:T(8,128)S(1)}, f32[8,2,16,128]{3,2,1,0:T(8,128)S(1)}, f32[8,2,16,128]{3,2,1,0:T(8,128)S(1)}, f32[8,16,128]{2,1,0:T(8,128)S(1)}) custom-call(f32[8,128,128]{2,1,0:T(8,128)S(1)} %bitcast.14, f32[8,2,16,128]{3,2,1,0:T(8,128)S(1)} %collective-permute-done.pair.low, f32[8,2,16,128]{3,2,1,0:T(8,128)S(1)} %collective-permute-done.1.after.high, ...), custom_call_target="tpu_custom_call" | custom-call | flops 10000000000 | bytes 1000 | tf_op jit(solution)/shard_map/first_stage/pallas_call | solution.py:566
  25.4 0.0 copy-start.6
  25.4 0.8 %copy-done.6 = f32[8,128,128]{2,1,0:T(8,128)} copy-done((f32[8,128,128]{2,1,0:T(8,128)}, f32[8,128,128]{2,1,0:T(8,128)S(1)}, u32[]{:S(2)}) %copy-start.6) | copy-done | bytes 524312
  26.2 0.3 collective-permute-start.5
  26.5 2.0 %collective-permute-start.3 = (f32[8,2,16,128]{3,2,1,0:T(8,128)S(1)}, f32[8,2,16,128]{3,2,1,0:T(8,128)S(1)}, u32[]{:S(2)}, u32[]{:S(2)}) collective-permute-start(f32[8,2,16,128]{3,2,1,0:T(8,128)S(1)} %get-tuple-element.20), channel_id=1, source_target_pairs={{0,2},{2,0},{4,6},{6,4},{8,10},{10,8},{12,14},{14,12},{16,18},{18,... | collective-permute-start | bytes 393224 | tf_op jit(solution)/shard_map/ppermute | solution.py:486
  28.4 4.0 %collective-permute-start.4 = (f32[8,2,16,128]{3,2,1,0:T(8,128)S(1)}, f32[8,2,16,128]{3,2,1,0:T(8,128)S(1)}, u32[]{:S(2)}, u32[]{:S(2)}) collective-permute-start(f32[8,2,16,128]{3,2,1,0:T(8,128)S(1)} %get-tuple-element.21), channel_id=1, source_target_pairs={{2,4},{4,2},{6,8},{8,6},{10,12},{12,10},{14,16},{16,14},{18,20},{2... | collective-permute-start | bytes 393224 | tf_op jit(solution)/shard_map/ppermute | solution.py:487
  32.4 1.0 %copy-done.7 = f32[8,128,128]{2,1,0:T(8,128)S(1)} copy-done((f32[8,128,128]{2,1,0:T(8,128)S(1)}, f32[8,128,128]{2,1,0:T(8,128)}, u32[]{:S(2)}) %copy-start.7) | copy-done | bytes 524312
  33.5 2.8 %sweeps.1 = (f32[8,128]{1,0:T(8,128)}, f32[256,128]{1,0:T(8,128)}) custom-call(f32[128,128]{1,0:T(8,128)S(1)} %bitcast.17, f32[8,128,128]{2,1,0:T(8,128)S(1)} %bitcast.11, f32[4,8,128]{2,1,0:T(8,128)S(1)} %copy-done.5, f32[3,136,128]{2,1,0:T(8,128)S(1)} %get-tuple-element.25.own_pair, f32[3,136,128]{2,1,0:T(8,128)S(1)} %get-tuple-element.26.own_next, ...), custom_call_target="tpu_custom_call" | custom-call | flops 10000000000 | bytes 1000 | tf_op jit(solution)/shard_map/sweeps/pallas_call | solution.py:590
  36.3 2.6 %all-to-all-start.1 = ((f32[32,8,128]{2,1,0:T(8,128)}), f32[32,8,128]{2,1,0:T(8,128)S(1)}, u32[]{:S(2)}, u32[]{:S(2)}) async-start(f32[32,8,128]{2,1,0:T(8,128)} %bitcast.6), calls=%async_computation.1 | async-start | bytes 262144 | tf_op jit(solution)/shard_map/all_to_all | solution.py:603
  38.9 0.0 copy-start.8
  38.9 1.0 %copy-done.8 = f32[8,128,128]{2,1,0:T(8,128)S(1)} copy-done((f32[8,128,128]{2,1,0:T(8,128)S(1)}, f32[8,128,128]{2,1,0:T(8,128)}, u32[]{:S(2)}) %copy-start.8) | copy-done | bytes 524312
  40.0 5.1 %second_stage.1 = f32[8,128,128]{2,1,0:T(8,128)} custom-call(f32[8,128,128]{2,1,0:T(8,128)S(1)} %copy-done.8, f32[8,2,16,128]{3,2,1,0:T(8,128)S(1)} %collective-permute-done.3.low, f32[8,2,16,128]{3,2,1,0:T(8,128)S(1)} %collective-permute-done.4.high, f32[8,16,128]{2,1,0:T(8,128)S(1)} %collective-permute-done.5.edge, f32[8,128,128]{2,1,0:T(8,128)S(1)} %bitcast.15, ...), custom_call_target="tpu_custom_call" | custom-call | flops 10000000000 | bytes 1000 | tf_op jit(solution)/shard_map/second_stage/pallas_call | solution.py:608
  45.1 2.0 %all-to-all-done.1 = f32[32,8,128]{2,1,0:T(8,128)S(1)} async-done(((f32[32,8,128]{2,1,0:T(8,128)}), f32[32,8,128]{2,1,0:T(8,128)S(1)}, u32[]{:S(2)}, u32[]{:S(2)}) %all-to-all-start.1) | async-done | bytes 131104 | tf_op jit(solution)/shard_map/all_to_all | solution.py:603
  47.1 1.3 %gather.1 = f32[128,128]{1,0:T(8,128)} custom-call(f32[16,2,8,128]{3,2,1,0:T(8,128)S(1)} %bitcast.16, s32[128,128]{1,0:T(8,128)S(1)} %bitcast.19), custom_call_target="tpu_custom_call" | custom-call | flops 1000 | bytes 1000 | tf_op jit(solution)/shard_map/gather/pallas_call | solution.py:617
  (22 shorter events, 0.1 us)
Async XLA Ops:
  0.6 8.7 %copy-start = (f32[8,1,128,128]{3,2,1,0:T(8,128)S(1)}, f32[8,1,128,128]{3,2,1,0:T(8,128)}, u32[]{:S(2)}) copy-start(f32[8,1,128,128]{3,2,1,0:T(8,128)} %param.7) | copy-start | bytes 1572868
  0.6 1.1 %copy-start.1 = (f32[8,16,8,128]{3,2,1,0:T(8,128)S(1)}, f32[8,16,8,128]{3,2,1,0:T(8,128)}, u32[]{:S(2)}) copy-start(f32[8,16,8,128]{3,2,1,0:T(8,128)} %param.4) | copy-start | bytes 1572868
  1.7 11.7 %copy-start.2 = (f32[8,16,8,128]{3,2,1,0:T(8,128)S(1)}, f32[8,16,8,128]{3,2,1,0:T(8,128)}, u32[]{:S(2)}) copy-start(f32[8,16,8,128]{3,2,1,0:T(8,128)} %param.4) | copy-start | bytes 1572868
  1.8 9.7 %collective-permute-start = (f32[8,2,16,128]{3,2,1,0:T(8,128)S(1)}, f32[8,2,16,128]{3,2,1,0:T(8,128)S(1)}, u32[]{:S(2)}, u32[]{:S(2)}) collective-permute-start(f32[8,2,16,128]{3,2,1,0:T(8,128)S(1)} %get-tuple-element.16), channel_id=1, source_target_pairs={{0,2},{2,0},{4,6},{6,4},{8,10},{10,8},{12,14},{14,12},{16,18},{18,... | collective-permute-start | bytes 393224 | tf_op jit(solution)/shard_map/ppermute | solution.py:486
  4.8 8.7 %collective-permute-start.1 = (f32[8,2,16,128]{3,2,1,0:T(8,128)S(1)}, f32[8,2,16,128]{3,2,1,0:T(8,128)S(1)}, u32[]{:S(2)}, u32[]{:S(2)}) collective-permute-start(f32[8,2,16,128]{3,2,1,0:T(8,128)S(1)} %get-tuple-element.17), channel_id=1, source_target_pairs={{2,4},{4,2},{6,8},{8,6},{10,12},{12,10},{14,16},{16,14},{18,20},{2... | collective-permute-start | bytes 393224 | tf_op jit(solution)/shard_map/ppermute | solution.py:487
  9.3 1.5 %collective-permute-start.2 = (f32[8,16,128]{2,1,0:T(8,128)S(1)}, f32[8,16,128]{2,1,0:T(8,128)S(1)}, u32[]{:S(2)}, u32[]{:S(2)}) collective-permute-start(f32[8,16,128]{2,1,0:T(8,128)S(1)} %get-tuple-element.18._), channel_id=1, source_target_pairs={{0,1},{1,0},{2,3},{3,2},{4,5},{5,4},{6,7},{7,6},{8,9},{9,8},{10,11... | collective-permute-start | bytes 196616 | tf_op jit(solution)/shard_map/ppermute | solution.py:488
  9.3 0.7 %copy-start.4 = (f32[4,8,128]{2,1,0:T(8,128)S(1)}, f32[4,8,128]{2,1,0:T(8,128)}, u32[]{:S(2)}) copy-start(f32[4,8,128]{2,1,0:T(8,128)} %own_conductance.1) | copy-start | bytes 49156
  10.1 0.8 %copy-start.5 = (f32[4,8,128]{2,1,0:T(8,128)S(1)}, f32[4,8,128]{2,1,0:T(8,128)}, u32[]{:S(2)}) copy-start(f32[4,8,128]{2,1,0:T(8,128)} %own_conductance.1) | copy-start | bytes 49156
  10.1 3.4 %copy-start.3 = (s32[16,8,128]{2,1,0:T(8,128)S(1)}, s32[16,8,128]{2,1,0:T(8,128)}, u32[]{:S(2)}) copy-start(s32[16,8,128]{2,1,0:T(8,128)} %param.5) | copy-start | bytes 196612
  10.1 10.4 %collective-permute-start.6 = (f32[3,136,128]{2,1,0:T(8,128)S(1)}, f32[3,136,128]{2,1,0:T(8,128)S(1)}, u32[]{:S(2)}, u32[]{:S(2)}) collective-permute-start(f32[3,136,128]{2,1,0:T(8,128)S(1)} %get-tuple-element.23), channel_id=1, source_target_pairs={{0,2},{2,0},{4,6},{6,4},{8,10},{10,8},{12,14},{14,12},{16,18},{18,... | collective-permute-start | bytes 626696 | tf_op jit(solution)/shard_map/ppermute | solution.py:553
  10.2 10.3 %collective-permute-start.7 = (f32[3,136,128]{2,1,0:T(8,128)S(1)}, f32[3,136,128]{2,1,0:T(8,128)S(1)}, u32[]{:S(2)}, u32[]{:S(2)}) collective-permute-start(f32[3,136,128]{2,1,0:T(8,128)S(1)} %get-tuple-element.24), channel_id=1, source_target_pairs={{2,4},{4,2},{6,8},{8,6},{10,12},{12,10},{14,16},{16,14},{18,20},{2... | collective-permute-start | bytes 626696 | tf_op jit(solution)/shard_map/ppermute | solution.py:554
  10.9 15.6 %collective-permute-start.9 = (f32[4,8,128]{2,1,0:T(8,128)S(1)}, f32[4,8,128]{2,1,0:T(8,128)S(1)}, u32[]{:S(2)}, u32[]{:S(2)}) collective-permute-start(f32[4,8,128]{2,1,0:T(8,128)S(1)} %copy-done.5), channel_id=1, source_target_pairs={{0,1},{1,0},{2,3},{3,2},{4,5},{5,4},{6,7},{7,6},{8,9},{9,8},{10,11... | collective-permute-start | bytes 49160 | tf_op jit(solution)/shard_map/ppermute | solution.py:588
  11.5 21.0 %collective-permute-start.8 = (f32[8,128,128]{2,1,0:T(8,128)S(1)}, f32[8,128,128]{2,1,0:T(8,128)S(1)}, u32[]{:S(2)}, u32[]{:S(2)}) collective-permute-start(f32[8,128,128]{2,1,0:T(8,128)S(1)} %bitcast.10), channel_id=1, source_target_pairs={{0,1},{1,0},{2,3},{3,2},{4,5},{5,4},{6,7},{7,6},{8,9},{9,8},{10,11... | collective-permute-start | bytes 1572872 | tf_op jit(solution)/shard_map/ppermute | solution.py:588
  15.6 16.9 %all-to-all-start = ((f32[32,4,128]{2,1,0:T(4,128)}), f32[32,4,128]{2,1,0:T(4,128)S(1)}, u32[]{:S(2)}, u32[]{:S(2)}) async-start(f32[32,4,128]{2,1,0:T(4,128)} %bitcast.2), calls=%async_computation | async-start | bytes 131072 | tf_op jit(solution)/shard_map/all_to_all | solution.py:589
  20.5 8.0 %collective-permute-start.10 = (f32[3,136,128]{2,1,0:T(8,128)S(1)}, f32[3,136,128]{2,1,0:T(8,128)S(1)}, u32[]{:S(2)}, u32[]{:S(2)}) collective-permute-start(f32[3,136,128]{2,1,0:T(8,128)S(1)} %get-tuple-element.25.own_pair), channel_id=1, source_target_pairs={{0,1},{1,0},{2,3},{3,2},{4,5},{5,4},{6,7},{7,6},{8,9},{9,8},{10,11... | collective-permute-start | bytes 626696 | tf_op jit(solution)/shard_map/ppermute | solution.py:588
  20.8 11.6 %collective-permute-start.11 = (f32[3,136,128]{2,1,0:T(8,128)S(1)}, f32[3,136,128]{2,1,0:T(8,128)S(1)}, u32[]{:S(2)}, u32[]{:S(2)}) collective-permute-start(f32[3,136,128]{2,1,0:T(8,128)S(1)} %get-tuple-element.26.own_next), channel_id=1, source_target_pairs={{0,1},{1,0},{2,3},{3,2},{4,5},{5,4},{6,7},{7,6},{8,9},{9,8},{10,11... | collective-permute-start | bytes 626696 | tf_op jit(solution)/shard_map/ppermute | solution.py:588
  25.4 0.8 %copy-start.6 = (f32[8,128,128]{2,1,0:T(8,128)}, f32[8,128,128]{2,1,0:T(8,128)S(1)}, u32[]{:S(2)}) copy-start(f32[8,128,128]{2,1,0:T(8,128)S(1)} %get-tuple-element.19._.x_ref) | copy-start | bytes 1572868
  26.2 12.7 %collective-permute-start.5 = (f32[8,16,128]{2,1,0:T(8,128)S(1)}, f32[8,16,128]{2,1,0:T(8,128)S(1)}, u32[]{:S(2)}, u32[]{:S(2)}) collective-permute-start(f32[8,16,128]{2,1,0:T(8,128)S(1)} %get-tuple-element.22), channel_id=1, source_target_pairs={{0,1},{1,0},{2,3},{3,2},{4,5},{5,4},{6,7},{7,6},{8,9},{9,8},{10,11... | collective-permute-start | bytes 196616 | tf_op jit(solution)/shard_map/ppermute | solution.py:488
  26.5 12.4 %collective-permute-start.3 = (f32[8,2,16,128]{3,2,1,0:T(8,128)S(1)}, f32[8,2,16,128]{3,2,1,0:T(8,128)S(1)}, u32[]{:S(2)}, u32[]{:S(2)}) collective-permute-start(f32[8,2,16,128]{3,2,1,0:T(8,128)S(1)} %get-tuple-element.20), channel_id=1, source_target_pairs={{0,2},{2,0},{4,6},{6,4},{8,10},{10,8},{12,14},{14,12},{16,18},{18,... | collective-permute-start | bytes 393224 | tf_op jit(solution)/shard_map/ppermute | solution.py:486
  28.4 10.5 %collective-permute-start.4 = (f32[8,2,16,128]{3,2,1,0:T(8,128)S(1)}, f32[8,2,16,128]{3,2,1,0:T(8,128)S(1)}, u32[]{:S(2)}, u32[]{:S(2)}) collective-permute-start(f32[8,2,16,128]{3,2,1,0:T(8,128)S(1)} %get-tuple-element.21), channel_id=1, source_target_pairs={{2,4},{4,2},{6,8},{8,6},{10,12},{12,10},{14,16},{16,14},{18,20},{2... | collective-permute-start | bytes 393224 | tf_op jit(solution)/shard_map/ppermute | solution.py:487
  32.4 1.0 %copy-start.7 = (f32[8,128,128]{2,1,0:T(8,128)S(1)}, f32[8,128,128]{2,1,0:T(8,128)}, u32[]{:S(2)}) copy-start(f32[8,128,128]{2,1,0:T(8,128)} %copy-done.6) | copy-start | bytes 1572868
  36.3 10.8 %all-to-all-start.1 = ((f32[32,8,128]{2,1,0:T(8,128)}), f32[32,8,128]{2,1,0:T(8,128)S(1)}, u32[]{:S(2)}, u32[]{:S(2)}) async-start(f32[32,8,128]{2,1,0:T(8,128)} %bitcast.6), calls=%async_computation.1 | async-start | bytes 262144 | tf_op jit(solution)/shard_map/all_to_all | solution.py:603
  38.9 1.0 %copy-start.8 = (f32[8,128,128]{2,1,0:T(8,128)S(1)}, f32[8,128,128]{2,1,0:T(8,128)}, u32[]{:S(2)}) copy-start(f32[8,128,128]{2,1,0:T(8,128)} %copy-done.6) | copy-start | bytes 1572868

commit v3 on v2

--- a/solution.py
+++ b/solution.py
@@ -11,10 +11,12 @@
 GAMMA = 5.0 / 3.0
 TIME_STEP = 0.02
 CELL_AREA = 0.125
+TINY = 1e-37
 LANES = 128
+UNROLL = (4, 4, 8)
 SUB = 8
 PARTS = 3
-VMEM_LIMIT = 40 * 1024 * 1024
+VMEM_LIMIT = 6 * 1024 * 1024
 CHEAP, CURRENTS, RELAY, DEAR = 1_000, 2_000_000_000, 1_000, 10_000_000_000
 IN_VMEM = pl.BlockSpec(memory_space=pltpu.VMEM)
 UNREAD = pl.BlockSpec(memory_space=pl.ANY)
@@ -45,7 +47,7 @@
 
 
 def minmod(a, b):
-    return jnp.maximum(jnp.minimum(a, b), 0.0) + jnp.minimum(jnp.maximum(a, b), 0.0)
+    return jnp.maximum(jnp.minimum(a, jnp.maximum(b, 0.0)), jnp.minimum(b, 0.0))
 
 
 def reciprocal(value):
@@ -67,7 +69,8 @@
     momentum[d] = momentum[d] + total
     induction = [None if j == d else vn * b[j] - bn * v[j] for j in range(3)]
     flux = [m[d]] + momentum + induction + [(energy + total) * vn - bn * alignment]
-    speed = jnp.abs(vn) + jnp.sqrt((GAMMA * jnp.abs(pressure) + field_sq) * inverse)
+    squared = (GAMMA * jnp.abs(pressure) + field_sq) * inverse
+    speed = jnp.abs(vn) + squared * lax.rsqrt(jnp.maximum(squared, TINY))
     return flux, speed
 
 
@@ -79,13 +82,13 @@
     for k in range(8):
         jump = speed * (right[k] - left[k])
         if left_flux[k] is None:
-            out.append(-0.5 * jump)
+            out.append(-jump)
         else:
-            out.append(0.5 * (left_flux[k] + right_flux[k] - jump))
+            out.append(left_flux[k] + right_flux[k] - jump)
     return out, left_flux
 
 
-def march(load, cells, d, emit):
+def march(load, cells, d, emit, unroll):
     before, here, after = load(-2), load(-1), load(0)
     half = [0.5 * minmod(after[k] - here[k], here[k] - before[k]) for k in range(8)]
     left = [here[k] + half[k] for k in range(8)]
@@ -107,14 +110,14 @@
         emit(f - 1, [new[k] - flux[k] for k in range(8)])
         return here, left, jump, new
 
-    lax.fori_loop(1, cells + 1, step, (here, left, jump, flux), unroll=2)
+    lax.fori_loop(1, cells + 1, step, (here, left, jump, flux), unroll=unroll)
 
 
 def parity():
     return lax.axis_index("shell") & 1
 
 
-def pack_halos(source, pair_ref, next_ref, edge_ref, layers, position):
+def pack_halos(source, next_ref, pair_ref, edge_ref, layers, position):
     odd = parity()
     to_pair, to_next = jnp.where(odd == 1, 0, SUB - 2), jnp.where(odd == 1, SUB - 2, 0)
     for k in range(8):
@@ -127,7 +130,7 @@
         edge_ref[k] = source[k, pl.ds(first, 2 * SUB), :]
 
 
-def tendency_into(x_ref, pair_ref, next_ref, edge_ref, xr, xl, div, layers, position, last, finish):
+def tendency_into(x_ref, next_ref, pair_ref, edge_ref, xr, xl, div, layers, position, last, finish):
     cells = layers * SUB
     from_below = parity() == 1
     for k in range(8):
@@ -156,7 +159,7 @@
         for k in range(8):
             div[k, pl.ds(start, SUB), :] = values[k]
 
-    march(load_radial, layers, 0, emit_radial)
+    march(load_radial, layers, 0, emit_radial, UNROLL[0])
 
     def load_lon(c):
         start = (c + 2) * layers
@@ -169,7 +172,7 @@
             rows = pl.ds(c, layers, stride=SUB)
             div[k, rows, :] = div[k, rows, :] + values[k]
 
-    march(load_lon, SUB, 1, emit_lon)
+    march(load_lon, SUB, 1, emit_lon, UNROLL[1])
 
     lane = lane_index(SUB)
     at_first, at_last = lane == 0, lane == LANES - 1
@@ -187,18 +190,18 @@
         flux, left_flux = face_flux(left, right, 2)
         total = []
         for k in range(8):
-            edge = 0.0 if left_flux[k] is None else left_flux[k]
+            edge = 0.0 if left_flux[k] is None else 2.0 * left_flux[k]
             total.append(
                 div[k, rows, :] + flux[k] - jnp.where(at_first, edge, pltpu.roll(flux[k], 1, 1))
             )
         finish(rows, x, total)
         return carry
 
-    lax.fori_loop(0, layers, layer, 0, unroll=2)
-
-
-def pack_kernel(layers, x_ref, low_ref, high_ref, edge_ref):
-    pack_halos(x_ref, low_ref, high_ref, edge_ref, layers, lax.axis_index("radial"))
+    lax.fori_loop(0, layers, layer, 0, unroll=UNROLL[2])
+
+
+def pack_kernel(layers, x_ref, next_ref, pair_ref, edge_ref):
+    pack_halos(x_ref, next_ref, pair_ref, edge_ref, layers, lax.axis_index("radial"))
 
 
 def relay_kernel(*refs):
@@ -206,26 +209,26 @@
 
 
 def first_stage_kernel(
-    layers, x_ref, low, high, edge, _, out_ref, low_ref, high_ref, edge_ref, xr, xl, div
+    layers, x_ref, after, pair, edge, _, out_ref, next_ref, pair_ref, edge_ref, xr, xl, div
 ):
     position, last = lax.axis_index("radial"), lax.axis_size("radial") - 1
 
     def finish(rows, x, total):
         for k in range(8):
-            out_ref[k, rows, :] = x[k] - TIME_STEP * total[k]
-
-    tendency_into(x_ref, low, high, edge, xr, xl, div, layers, position, last, finish)
-    pack_halos(out_ref, low_ref, high_ref, edge_ref, layers, position)
-
-
-def second_stage_kernel(layers, x_ref, low, high, edge, state_ref, _, out_ref, xr, xl, div):
+            out_ref[k, rows, :] = x[k] - 0.5 * TIME_STEP * total[k]
+
+    tendency_into(x_ref, after, pair, edge, xr, xl, div, layers, position, last, finish)
+    pack_halos(out_ref, next_ref, pair_ref, edge_ref, layers, position)
+
+
+def second_stage_kernel(layers, x_ref, after, pair, edge, state_ref, _, out_ref, xr, xl, div):
     position, last = lax.axis_index("radial"), lax.axis_size("radial") - 1
 
     def finish(rows, x, total):
         for k in range(8):
-            out_ref[k, rows, :] = 0.5 * state_ref[k, rows, :] + 0.5 * (x[k] - TIME_STEP * total[k])
-
-    tendency_into(x_ref, low, high, edge, xr, xl, div, layers, position, last, finish)
+            out_ref[k, rows, :] = 0.5 * state_ref[k, rows, :] + 0.5 * (x[k] - 0.5 * TIME_STEP * total[k])
+
+    tendency_into(x_ref, after, pair, edge, xr, xl, div, layers, position, last, finish)
 
 
 def log2_of(value):
@@ -246,7 +249,7 @@
     return parts
 
 
-def current_kernel(layers, width, columns, window, x_ref, pair, after, edge, nodes_ref, out_ref, held):
+def current_kernel(layers, width, columns, window, x_ref, after, pair, edge, nodes_ref, out_ref, held):
     from_below = parity() == 1
     below_all = [None if k == 1 else jnp.where(from_below, pair[4 + k, 1], after[4 + k, 1]) for k in range(3)]
     above_all = [None if k == 1 else jnp.where(from_below, after[4 + k, 0], pair[4 + k, 0]) for k in range(3)]
@@ -481,10 +484,10 @@
     return out
 
 
-def exchange_halos(pair, after, edge):
+def exchange_halos(after, pair, edge):
     return (
+        lax.ppermute(after, "shell", pairs(1, True)),
         lax.ppermute(pair, "shell", pairs(0, True)),
-        lax.ppermute(after, "shell", pairs(1, True)),
         lax.ppermute(edge, "radial", [(0, 1), (1, 0)]),
     )
 
@@ -542,7 +545,7 @@
         pltpu.VMEM((8, cells, lats), jnp.float32),
     ]
     packed = call(functools.partial(pack_kernel, layers), halo_shapes, "pack")(x)
-    below, above, other = exchange_halos(*packed)
+    halos = exchange_halos(*packed)
 
     if fast:
         rim_shape = shape_of(HALO, half + SUB, half)
@@ -561,7 +564,7 @@
         "currents",
         flops=CURRENTS,
         scratch=[pltpu.VMEM((max(16, width) + 2 * SUB, LANES), jnp.float32)],
-    )(x, below, above, other, nodes)
+    )(x, *halos, nodes)
 
     section_one, *packed = call(
         functools.partial(first_stage_kernel, layers),
@@ -570,7 +573,7 @@
         flops=DEAR,
         scratch=stage_scratch,
         in_specs=[IN_VMEM] * 4 + [UNREAD],
-    )(x, below, above, other, sums)
+    )(x, *halos, sums)
     second_halos = exchange_halos(*packed)
     after = sums
 
@@ -598,7 +601,7 @@
             ],
             flops=DEAR,
             in_specs=[IN_VMEM] * 9 + [UNREAD],
-        )(arrived, blocks, conductance, *rims, *twin_parts, section_one)
+        )(arrived, blocks, conductance, *rims, *twin_parts, packed[2])
         after = spread
         table = lax.all_to_all(spread, ("shell", "radial"), split_axis=0, concat_axis=0, tiled=True)
         table = table.reshape(shells, radials, own_rows, half)

time: 48.8 us -> 45.6 us (0.934)
  Pallas kernels: 15.8 us -> 12.2 us
  waiting for transfers between devices: 3.98 us -> 6.33 us
  local copies, waits for them, and re-layouts: 4.68 us -> 3.65 us
  starting transfers between devices: 23.1 us -> 22.3 us
    ppermute x2, starting transfers between devices: 4.96 us -> 0.01 us  [exchange_halos(): lax.ppermute(pair, 'shell', pairs(0, True))]
    ppermute x2, starting transfers between devices: 8.5 us -> 11.9 us  [exchange_halos(): lax.ppermute(after, 'shell', pairs(1, True))]
    ppermute x2, waiting for transfers between devices: 0.01 us -> 2.1 us  [exchange_halos(): lax.ppermute(pair, 'shell', pairs(0, True))]
    ppermute x1, starting transfers between devices: 0.07 us -> 2.08 us  [body(): lax.ppermute(rim_pair, 'shell', pairs(0, False))]
    ppermute x2, waiting for transfers between devices: 1.92 us -> 0.01 us  [exchange_halos(): lax.ppermute(after, 'shell', pairs(1, True))]
    pallas_call x1, Pallas kernels: 4.36 us -> 2.55 us  [body(): call(functools.partial(first_stage_kernel, layers), [shape_of(fields, cel...]
    pallas_call x1, Pallas kernels: 5.12 us -> 3.33 us  [body(): call(functools.partial(second_stage_kernel, layers), shape_of(fields, cel...]
    all_to_all x1, waiting for transfers between devices: 2.03 us -> 3.37 us  [body(): lax.all_to_all(spread, ('shell', 'radial'), split_axis=0, concat_axis=0,...]
  transfers between devices with their start and end apart: 14 -> 14, of which waited for: 2 -> 4; matrix products, arithmetic and copies ran while one was open for 0% -> 0% of each run, Pallas kernels for 30% -> 24%
where the time goes in v3:
time: 45.6 us; the launch traced here: 45.3 us
  starting transfers between devices  22.3 us (49%)
  Pallas kernels  12.2 us (27%)
  waiting for transfers between devices  6.33 us (14%)
  local copies, waits for them, and re-layouts  3.65 us (8%)
  between operations  0.76 us (2%)
    ppermute x2, starting transfers between devices, exchange_halos(): lax.ppermute(after, 'shell', pairs(1, True))  11.9 us
    all_to_all x1, starting transfers between devices, body(): lax.all_to_all(sums, ('shell', 'radial'), split_axis=0, concat_axis=0, ti...  3.74 us
    unnamed x16, local copies, waits for them, and re-layouts  3.65 us
    all_to_all x1, waiting for transfers between devices, body(): lax.all_to_all(spread, ('shell', 'radial'), split_axis=0, concat_axis=0,...  3.37 us
    pallas_call x1, Pallas kernels, body(): call(functools.partial(second_stage_kernel, layers), shape_of(fields, cel...  3.33 us
    all_to_all x1, starting transfers between devices, body(): lax.all_to_all(spread, ('shell', 'radial'), split_axis=0, concat_axis=0,...  2.88 us
    pallas_call x1, Pallas kernels, body(): call(functools.partial(sweep_kernel, width), [shape_of(own_rows, half), s...  2.87 us
    pallas_call x1, Pallas kernels, body(): call(functools.partial(first_stage_kernel, layers), [shape_of(fields, cel...  2.55 us
  transfers between devices with their start and end apart: 14, of which 4 were waited for; matrix products, arithmetic and copies ran while one was open for 0% of the time, Pallas kernels for 24%

profile of v3, /device:TPU:0, one launch (start us, length us, event | category | flops | bytes accessed | tf_op | source)
XLA Modules:
  0.0 45.3 jit_solution(14210274809650768317)
XLA Ops:
  0.6 1.1 %copy-done.1 = f32[8,16,8,128]{3,2,1,0:T(8,128)S(1)} copy-done((f32[8,16,8,128]{3,2,1,0:T(8,128)S(1)}, f32[8,16,8,128]{3,2,1,0:T(8,128)}, u32[]{:S(2)}) %copy-start.1) | copy-done | bytes 524312
  1.7 0.1 pack.1
  1.8 7.0 %collective-permute-start = (f32[8,2,16,128]{3,2,1,0:T(8,128)S(1)}, f32[8,2,16,128]{3,2,1,0:T(8,128)S(1)}, u32[]{:S(2)}, u32[]{:S(2)}) collective-permute-start(f32[8,2,16,128]{3,2,1,0:T(8,128)S(1)} %get-tuple-element.16), channel_id=1, source_target_pairs={{2,4},{4,2},{6,8},{8,6},{10,12},{12,10},{14,16},{16,14},{18,20},{2... | collective-permute-start | bytes 393224 | tf_op jit(solution)/shard_map/ppermute | solution.py:489
  8.8 0.0 collective-permute-start.1
  8.8 0.0 collective-permute-start.2
  8.8 0.0 copy-start.4
  8.8 0.7 %copy-done.4 = f32[4,8,128]{2,1,0:T(8,128)S(1)} copy-done((f32[4,8,128]{2,1,0:T(8,128)S(1)}, f32[4,8,128]{2,1,0:T(8,128)}, u32[]{:S(2)}) %copy-start.4) | copy-done | bytes 16408
  9.6 2.1 %collective-permute-start.6 = (f32[3,136,128]{2,1,0:T(8,128)S(1)}, f32[3,136,128]{2,1,0:T(8,128)S(1)}, u32[]{:S(2)}, u32[]{:S(2)}) collective-permute-start(f32[3,136,128]{2,1,0:T(8,128)S(1)} %get-tuple-element.23), channel_id=1, source_target_pairs={{0,2},{2,0},{4,6},{6,4},{8,10},{10,8},{12,14},{14,12},{16,18},{18,... | collective-permute-start | bytes 626696 | tf_op jit(solution)/shard_map/ppermute | solution.py:556
  11.7 0.7 %collective-permute-start.7 = (f32[3,136,128]{2,1,0:T(8,128)S(1)}, f32[3,136,128]{2,1,0:T(8,128)S(1)}, u32[]{:S(2)}, u32[]{:S(2)}) collective-permute-start(f32[3,136,128]{2,1,0:T(8,128)S(1)} %get-tuple-element.24), channel_id=1, source_target_pairs={{2,4},{4,2},{6,8},{8,6},{10,12},{12,10},{14,16},{16,14},{18,20},{2... | collective-permute-start | bytes 626696 | tf_op jit(solution)/shard_map/ppermute | solution.py:557
  12.3 0.0 collective-permute-done.2.edge
  12.3 0.3 collective-permute-start.8
  12.6 0.0 collective-permute-done.after
  12.6 0.3 collective-permute-start.9
  12.9 1.6 %collective-permute-done.1.pair = f32[8,2,16,128]{3,2,1,0:T(8,128)S(1)} collective-permute-done((f32[8,2,16,128]{3,2,1,0:T(8,128)S(1)}, f32[8,2,16,128]{3,2,1,0:T(8,128)S(1)}, u32[]{:S(2)}, u32[]{:S(2)}) %collective-permute-start.1) | collective-permute-done | bytes 131104 | tf_op jit(solution)/shard_map/ppermute | solution.py:490
  14.6 2.1 %currents.1._.refs_2_ = f32[128,128]{1,0:T(8,128)} custom-call(f32[8,128,128]{2,1,0:T(8,128)S(1)} %bitcast.13, f32[8,2,16,128]{3,2,1,0:T(8,128)S(1)} %collective-permute-done.after, f32[8,2,16,128]{3,2,1,0:T(8,128)S(1)} %collective-permute-done.1.pair, f32[8,16,128]{2,1,0:T(8,128)S(1)} %collective-permute-done.2.edge, s32[128,128]{1,0:T(8,128)S(1)} %bitcast.18), custom_call_target="tpu_custom_call" | custom-call | flops 2000000000 | bytes 1000 | tf_op jit(solution)/shard_map/currents/pallas_call | solution.py:561
  16.7 3.7 %all-to-all-start = ((f32[32,4,128]{2,1,0:T(4,128)}), f32[32,4,128]{2,1,0:T(4,128)S(1)}, u32[]{:S(2)}, u32[]{:S(2)}) async-start(f32[32,4,128]{2,1,0:T(4,128)} %bitcast.2), calls=%async_computation | async-start | bytes 131072 | tf_op jit(solution)/shard_map/all_to_all | solution.py:592
  20.4 0.8 %collective-permute-done.6.refs_0_ = f32[3,136,128]{2,1,0:T(8,128)S(1)} collective-permute-done((f32[3,136,128]{2,1,0:T(8,128)S(1)}, f32[3,136,128]{2,1,0:T(8,128)S(1)}, u32[]{:S(2)}, u32[]{:S(2)}) %collective-permute-start.6) | collective-permute-done | bytes 208928 | tf_op jit(solution)/shard_map/ppermute | solution.py:556
  21.2 0.0 collective-permute-start.10
  21.2 0.5 %collective-permute-start.11 = (f32[3,136,128]{2,1,0:T(8,128)S(1)}, f32[3,136,128]{2,1,0:T(8,128)S(1)}, u32[]{:S(2)}, u32[]{:S(2)}) collective-permute-start(f32[3,136,128]{2,1,0:T(8,128)S(1)} %get-tuple-element.26.own_next), channel_id=1, source_target_pairs={{0,1},{1,0},{2,3},{3,2},{4,5},{5,4},{6,7},{7,6},{8,9},{9,8},{10,11... | collective-permute-start | bytes 626696 | tf_op jit(solution)/shard_map/ppermute | solution.py:591
  21.7 2.6 %first_stage.1 = (f32[8,128,128]{2,1,0:T(8,128)S(1)}, f32[8,2,16,128]{3,2,1,0:T(8,128)S(1)}, f32[8,2,16,128]{3,2,1,0:T(8,128)S(1)}, f32[8,16,128]{2,1,0:T(8,128)S(1)}) custom-call(f32[8,128,128]{2,1,0:T(8,128)S(1)} %bitcast.14, f32[8,2,16,128]{3,2,1,0:T(8,128)S(1)} %collective-permute-done.after, f32[8,2,16,128]{3,2,1,0:T(8,128)S(1)} %collective-permute-done.1.pair, ...), custom_call_target="tpu_custom_call" | custom-call | flops 10000000000 | bytes 1000 | tf_op jit(solution)/shard_map/first_stage/pallas_call | solution.py:569
  24.3 0.0 copy-start.6
  24.3 0.8 %copy-done.6 = f32[8,128,128]{2,1,0:T(8,128)} copy-done((f32[8,128,128]{2,1,0:T(8,128)}, f32[8,128,128]{2,1,0:T(8,128)S(1)}, u32[]{:S(2)}) %copy-start.6) | copy-done | bytes 524312
  25.1 0.0 collective-permute-start.5
  25.1 0.0 collective-permute-done.9.twin_conductance
  25.1 4.9 %collective-permute-start.3 = (f32[8,2,16,128]{3,2,1,0:T(8,128)S(1)}, f32[8,2,16,128]{3,2,1,0:T(8,128)S(1)}, u32[]{:S(2)}, u32[]{:S(2)}) collective-permute-start(f32[8,2,16,128]{3,2,1,0:T(8,128)S(1)} %get-tuple-element.20), channel_id=1, source_target_pairs={{2,4},{4,2},{6,8},{8,6},{10,12},{12,10},{14,16},{16,14},{18,20},{2... | collective-permute-start | bytes 393224 | tf_op jit(solution)/shard_map/ppermute | solution.py:489
  30.0 2.9 %sweeps.1 = (f32[8,128]{1,0:T(8,128)}, f32[256,128]{1,0:T(8,128)}) custom-call(f32[128,128]{1,0:T(8,128)S(1)} %bitcast.17, f32[8,128,128]{2,1,0:T(8,128)S(1)} %bitcast.11, f32[4,8,128]{2,1,0:T(8,128)S(1)} %copy-done.5, f32[3,136,128]{2,1,0:T(8,128)S(1)} %get-tuple-element.25.own_pair, f32[3,136,128]{2,1,0:T(8,128)S(1)} %get-tuple-element.26.own_next, ...), custom_call_target="tpu_custom_call" | custom-call | flops 10000000000 | bytes 1000 | tf_op jit(solution)/shard_map/sweeps/pallas_call | solution.py:593
  32.9 2.9 %all-to-all-start.1 = ((f32[32,8,128]{2,1,0:T(8,128)}), f32[32,8,128]{2,1,0:T(8,128)S(1)}, u32[]{:S(2)}, u32[]{:S(2)}) async-start(f32[32,8,128]{2,1,0:T(8,128)} %bitcast.6), calls=%async_computation.1 | async-start | bytes 262144 | tf_op jit(solution)/shard_map/all_to_all | solution.py:606
  35.8 0.5 %collective-permute-done.4.pair = f32[8,2,16,128]{3,2,1,0:T(8,128)S(1)} collective-permute-done((f32[8,2,16,128]{3,2,1,0:T(8,128)S(1)}, f32[8,2,16,128]{3,2,1,0:T(8,128)S(1)}, u32[]{:S(2)}, u32[]{:S(2)}) %collective-permute-start.4) | collective-permute-done | bytes 131104 | tf_op jit(solution)/shard_map/ppermute | solution.py:490
  36.3 1.0 %copy-done.7 = f32[8,128,128]{2,1,0:T(8,128)S(1)} copy-done((f32[8,128,128]{2,1,0:T(8,128)S(1)}, f32[8,128,128]{2,1,0:T(8,128)}, u32[]{:S(2)}) %copy-start.7) | copy-done | bytes 524312
  37.3 3.3 %second_stage.1 = f32[8,128,128]{2,1,0:T(8,128)} custom-call(f32[8,128,128]{2,1,0:T(8,128)S(1)} %copy-done.7, f32[8,2,16,128]{3,2,1,0:T(8,128)S(1)} %collective-permute-done.3.after, f32[8,2,16,128]{3,2,1,0:T(8,128)S(1)} %collective-permute-done.4.pair, f32[8,16,128]{2,1,0:T(8,128)S(1)} %collective-permute-done.5.edge, f32[8,128,128]{2,1,0:T(8,128)S(1)} %bitcast.15, ...), custom_call_target="tpu_custom_call" | custom-call | flops 10000000000 | bytes 1000 | tf_op jit(solution)/shard_map/second_stage/pallas_call | solution.py:611
  40.6 3.4 %all-to-all-done.1 = f32[32,8,128]{2,1,0:T(8,128)S(1)} async-done(((f32[32,8,128]{2,1,0:T(8,128)}), f32[32,8,128]{2,1,0:T(8,128)S(1)}, u32[]{:S(2)}, u32[]{:S(2)}) %all-to-all-start.1) | async-done | bytes 131104 | tf_op jit(solution)/shard_map/all_to_all | solution.py:606
  44.0 1.3 %gather.1 = f32[128,128]{1,0:T(8,128)} custom-call(f32[16,2,8,128]{3,2,1,0:T(8,128)S(1)} %bitcast.16, s32[128,128]{1,0:T(8,128)S(1)} %bitcast.19), custom_call_target="tpu_custom_call" | custom-call | flops 1000 | bytes 1000 | tf_op jit(solution)/shard_map/gather/pallas_call | solution.py:620
  (20 shorter events, 0.1 us)
Async XLA Ops:
  0.6 8.2 %copy-start = (f32[8,1,128,128]{3,2,1,0:T(8,128)S(1)}, f32[8,1,128,128]{3,2,1,0:T(8,128)}, u32[]{:S(2)}) copy-start(f32[8,1,128,128]{3,2,1,0:T(8,128)} %param.7) | copy-start | bytes 1572868
  0.6 1.1 %copy-start.1 = (f32[8,16,8,128]{3,2,1,0:T(8,128)S(1)}, f32[8,16,8,128]{3,2,1,0:T(8,128)}, u32[]{:S(2)}) copy-start(f32[8,16,8,128]{3,2,1,0:T(8,128)} %param.4) | copy-start | bytes 1572868
  1.7 12.8 %copy-start.2 = (f32[8,16,8,128]{3,2,1,0:T(8,128)S(1)}, f32[8,16,8,128]{3,2,1,0:T(8,128)}, u32[]{:S(2)}) copy-start(f32[8,16,8,128]{3,2,1,0:T(8,128)} %param.4) | copy-start | bytes 1572868
  1.8 10.8 %collective-permute-start = (f32[8,2,16,128]{3,2,1,0:T(8,128)S(1)}, f32[8,2,16,128]{3,2,1,0:T(8,128)S(1)}, u32[]{:S(2)}, u32[]{:S(2)}) collective-permute-start(f32[8,2,16,128]{3,2,1,0:T(8,128)S(1)} %get-tuple-element.16), channel_id=1, source_target_pairs={{2,4},{4,2},{6,8},{8,6},{10,12},{12,10},{14,16},{16,14},{18,20},{2... | collective-permute-start | bytes 393224 | tf_op jit(solution)/shard_map/ppermute | solution.py:489
  8.8 5.8 %collective-permute-start.1 = (f32[8,2,16,128]{3,2,1,0:T(8,128)S(1)}, f32[8,2,16,128]{3,2,1,0:T(8,128)S(1)}, u32[]{:S(2)}, u32[]{:S(2)}) collective-permute-start(f32[8,2,16,128]{3,2,1,0:T(8,128)S(1)} %get-tuple-element.17), channel_id=1, source_target_pairs={{0,2},{2,0},{4,6},{6,4},{8,10},{10,8},{12,14},{14,12},{16,18},{18,... | collective-permute-start | bytes 393224 | tf_op jit(solution)/shard_map/ppermute | solution.py:490
  8.8 3.5 %collective-permute-start.2 = (f32[8,16,128]{2,1,0:T(8,128)S(1)}, f32[8,16,128]{2,1,0:T(8,128)S(1)}, u32[]{:S(2)}, u32[]{:S(2)}) collective-permute-start(f32[8,16,128]{2,1,0:T(8,128)S(1)} %get-tuple-element.18._), channel_id=1, source_target_pairs={{0,1},{1,0},{2,3},{3,2},{4,5},{5,4},{6,7},{7,6},{8,9},{9,8},{10,11... | collective-permute-start | bytes 196616 | tf_op jit(solution)/shard_map/ppermute | solution.py:491
  8.8 0.7 %copy-start.4 = (f32[4,8,128]{2,1,0:T(8,128)S(1)}, f32[4,8,128]{2,1,0:T(8,128)}, u32[]{:S(2)}) copy-start(f32[4,8,128]{2,1,0:T(8,128)} %own_conductance.1) | copy-start | bytes 49156
  9.5 3.1 %copy-start.5 = (f32[4,8,128]{2,1,0:T(8,128)S(1)}, f32[4,8,128]{2,1,0:T(8,128)}, u32[]{:S(2)}) copy-start(f32[4,8,128]{2,1,0:T(8,128)} %own_conductance.1) | copy-start | bytes 49156
  9.5 5.0 %copy-start.3 = (s32[16,8,128]{2,1,0:T(8,128)S(1)}, s32[16,8,128]{2,1,0:T(8,128)}, u32[]{:S(2)}) copy-start(s32[16,8,128]{2,1,0:T(8,128)} %param.5) | copy-start | bytes 196612
  9.6 11.7 %collective-permute-start.6 = (f32[3,136,128]{2,1,0:T(8,128)S(1)}, f32[3,136,128]{2,1,0:T(8,128)S(1)}, u32[]{:S(2)}, u32[]{:S(2)}) collective-permute-start(f32[3,136,128]{2,1,0:T(8,128)S(1)} %get-tuple-element.23), channel_id=1, source_target_pairs={{0,2},{2,0},{4,6},{6,4},{8,10},{10,8},{12,14},{14,12},{16,18},{18,... | collective-permute-start | bytes 626696 | tf_op jit(solution)/shard_map/ppermute | solution.py:556
  11.7 9.6 %collective-permute-start.7 = (f32[3,136,128]{2,1,0:T(8,128)S(1)}, f32[3,136,128]{2,1,0:T(8,128)S(1)}, u32[]{:S(2)}, u32[]{:S(2)}) collective-permute-start(f32[3,136,128]{2,1,0:T(8,128)S(1)} %get-tuple-element.24), channel_id=1, source_target_pairs={{2,4},{4,2},{6,8},{8,6},{10,12},{12,10},{14,16},{16,14},{18,20},{2... | collective-permute-start | bytes 626696 | tf_op jit(solution)/shard_map/ppermute | solution.py:557
  12.3 17.7 %collective-permute-start.8 = (f32[8,128,128]{2,1,0:T(8,128)S(1)}, f32[8,128,128]{2,1,0:T(8,128)S(1)}, u32[]{:S(2)}, u32[]{:S(2)}) collective-permute-start(f32[8,128,128]{2,1,0:T(8,128)S(1)} %bitcast.10), channel_id=1, source_target_pairs={{0,1},{1,0},{2,3},{3,2},{4,5},{5,4},{6,7},{7,6},{8,9},{9,8},{10,11... | collective-permute-start | bytes 1572872 | tf_op jit(solution)/shard_map/ppermute | solution.py:591
  12.6 12.5 %collective-permute-start.9 = (f32[4,8,128]{2,1,0:T(8,128)S(1)}, f32[4,8,128]{2,1,0:T(8,128)S(1)}, u32[]{:S(2)}, u32[]{:S(2)}) collective-permute-start(f32[4,8,128]{2,1,0:T(8,128)S(1)} %copy-done.5), channel_id=1, source_target_pairs={{0,1},{1,0},{2,3},{3,2},{4,5},{5,4},{6,7},{7,6},{8,9},{9,8},{10,11... | collective-permute-start | bytes 49160 | tf_op jit(solution)/shard_map/ppermute | solution.py:591
  16.7 13.4 %all-to-all-start = ((f32[32,4,128]{2,1,0:T(4,128)}), f32[32,4,128]{2,1,0:T(4,128)S(1)}, u32[]{:S(2)}, u32[]{:S(2)}) async-start(f32[32,4,128]{2,1,0:T(4,128)} %bitcast.2), calls=%async_computation | async-start | bytes 131072 | tf_op jit(solution)/shard_map/all_to_all | solution.py:592
  21.2 8.8 %collective-permute-start.10 = (f32[3,136,128]{2,1,0:T(8,128)S(1)}, f32[3,136,128]{2,1,0:T(8,128)S(1)}, u32[]{:S(2)}, u32[]{:S(2)}) collective-permute-start(f32[3,136,128]{2,1,0:T(8,128)S(1)} %get-tuple-element.25.own_pair), channel_id=1, source_target_pairs={{0,1},{1,0},{2,3},{3,2},{4,5},{5,4},{6,7},{7,6},{8,9},{9,8},{10,11... | collective-permute-start | bytes 626696 | tf_op jit(solution)/shard_map/ppermute | solution.py:591
  21.2 8.8 %collective-permute-start.11 = (f32[3,136,128]{2,1,0:T(8,128)S(1)}, f32[3,136,128]{2,1,0:T(8,128)S(1)}, u32[]{:S(2)}, u32[]{:S(2)}) collective-permute-start(f32[3,136,128]{2,1,0:T(8,128)S(1)} %get-tuple-element.26.own_next), channel_id=1, source_target_pairs={{0,1},{1,0},{2,3},{3,2},{4,5},{5,4},{6,7},{7,6},{8,9},{9,8},{10,11... | collective-permute-start | bytes 626696 | tf_op jit(solution)/shard_map/ppermute | solution.py:591
  24.3 0.8 %copy-start.6 = (f32[8,128,128]{2,1,0:T(8,128)}, f32[8,128,128]{2,1,0:T(8,128)S(1)}, u32[]{:S(2)}) copy-start(f32[8,128,128]{2,1,0:T(8,128)S(1)} %get-tuple-element.19.x_ref) | copy-start | bytes 1572868
  25.1 10.7 %collective-permute-start.5 = (f32[8,16,128]{2,1,0:T(8,128)S(1)}, f32[8,16,128]{2,1,0:T(8,128)S(1)}, u32[]{:S(2)}, u32[]{:S(2)}) collective-permute-start(f32[8,16,128]{2,1,0:T(8,128)S(1)} %get-tuple-element.22._), channel_id=1, source_target_pairs={{0,1},{1,0},{2,3},{3,2},{4,5},{5,4},{6,7},{7,6},{8,9},{9,8},{10,11... | collective-permute-start | bytes 196616 | tf_op jit(solution)/shard_map/ppermute | solution.py:491
  25.1 10.7 %collective-permute-start.3 = (f32[8,2,16,128]{3,2,1,0:T(8,128)S(1)}, f32[8,2,16,128]{3,2,1,0:T(8,128)S(1)}, u32[]{:S(2)}, u32[]{:S(2)}) collective-permute-start(f32[8,2,16,128]{3,2,1,0:T(8,128)S(1)} %get-tuple-element.20), channel_id=1, source_target_pairs={{2,4},{4,2},{6,8},{8,6},{10,12},{12,10},{14,16},{16,14},{18,20},{2... | collective-permute-start | bytes 393224 | tf_op jit(solution)/shard_map/ppermute | solution.py:489
  30.0 6.3 %collective-permute-start.4 = (f32[8,2,16,128]{3,2,1,0:T(8,128)S(1)}, f32[8,2,16,128]{3,2,1,0:T(8,128)S(1)}, u32[]{:S(2)}, u32[]{:S(2)}) collective-permute-start(f32[8,2,16,128]{3,2,1,0:T(8,128)S(1)} %get-tuple-element.21), channel_id=1, source_target_pairs={{0,2},{2,0},{4,6},{6,4},{8,10},{10,8},{12,14},{14,12},{16,18},{18,... | collective-permute-start | bytes 393224 | tf_op jit(solution)/shard_map/ppermute | solution.py:490
  32.9 11.1 %all-to-all-start.1 = ((f32[32,8,128]{2,1,0:T(8,128)}), f32[32,8,128]{2,1,0:T(8,128)S(1)}, u32[]{:S(2)}, u32[]{:S(2)}) async-start(f32[32,8,128]{2,1,0:T(8,128)} %bitcast.6), calls=%async_computation.1 | async-start | bytes 262144 | tf_op jit(solution)/shard_map/all_to_all | solution.py:606
  36.3 1.0 %copy-start.7 = (f32[8,128,128]{2,1,0:T(8,128)S(1)}, f32[8,128,128]{2,1,0:T(8,128)}, u32[]{:S(2)}) copy-start(f32[8,128,128]{2,1,0:T(8,128)} %copy-done.6) | copy-start | bytes 1572868

commit v4 on v3

--- a/solution.py
+++ b/solution.py
@@ -13,11 +13,14 @@
 CELL_AREA = 0.125
 TINY = 1e-37
 LANES = 128
+SPLIT = 2
 UNROLL = (4, 4, 8)
 SUB = 8
 PARTS = 3
+SUM_PARTS, MXU_EVERY = 2, 2
 VMEM_LIMIT = 6 * 1024 * 1024
 CHEAP, CURRENTS, RELAY, DEAR = 1_000, 2_000_000_000, 1_000, 10_000_000_000
+IN_HBM = pl.BlockSpec(memory_space=pltpu.HBM)
 IN_VMEM = pl.BlockSpec(memory_space=pltpu.VMEM)
 UNREAD = pl.BlockSpec(memory_space=pl.ANY)
 
@@ -44,6 +47,19 @@
 
 def row_index(rows, width=LANES):
     return lax.broadcasted_iota(jnp.int32, (rows, width), 0)
+
+
+class Fields:
+    def __init__(self, refs):
+        self.refs, self.count = refs, refs[0].shape[0]
+
+    def __getitem__(self, index):
+        k, *rest = index if isinstance(index, tuple) else (index,)
+        return self.refs[k // self.count][(k % self.count, *rest)]
+
+    def __setitem__(self, index, value):
+        k, *rest = index
+        self.refs[k // self.count][(k % self.count, *rest)] = value
 
 
 def minmod(a, b):
@@ -208,9 +224,8 @@
     pass
 
 
-def first_stage_kernel(
-    layers, x_ref, after, pair, edge, _, out_ref, next_ref, pair_ref, edge_ref, xr, xl, div
-):
+def first_stage_kernel(layers, x_ref, after, pair, edge, _, *refs):
+    out_ref, (next_ref, pair_ref, edge_ref, xr, xl, div) = Fields(refs[:-6]), refs[-6:]
     position, last = lax.axis_index("radial"), lax.axis_size("radial") - 1
 
     def finish(rows, x, total):
@@ -221,7 +236,8 @@
     pack_halos(out_ref, next_ref, pair_ref, edge_ref, layers, position)
 
 
-def second_stage_kernel(layers, x_ref, after, pair, edge, state_ref, _, out_ref, xr, xl, div):
+def second_stage_kernel(layers, after, pair, edge, state_ref, _, *refs):
+    x_ref, (out_ref, xr, xl, div) = Fields(refs[:-4]), refs[-4:]
     position, last = lax.axis_index("radial"), lax.axis_size("radial") - 1
 
     def finish(rows, x, total):
@@ -240,76 +256,119 @@
     return lax.shift_right_logical(nodes, log2_of(columns)), nodes & (columns - 1)
 
 
-def three_parts(value):
+def split(value, count):
     parts = []
-    for _ in range(PARTS):
+    for _ in range(count):
         part = value.astype(jnp.bfloat16).astype(jnp.float32)
         parts.append(part)
         value = value - part
     return parts
 
 
-def current_kernel(layers, width, columns, window, x_ref, after, pair, edge, nodes_ref, out_ref, held):
-    from_below = parity() == 1
-    below_all = [None if k == 1 else jnp.where(from_below, pair[4 + k, 1], after[4 + k, 1]) for k in range(3)]
-    above_all = [None if k == 1 else jnp.where(from_below, after[4 + k, 0], pair[4 + k, 0]) for k in range(3)]
-    position, last = lax.axis_index("radial"), lax.axis_size("radial") - 1
-    first_column = lax.axis_index("shell") * width
-    lane, sub = lane_index(SUB), row_index(SUB)
-    groups = max(16, width)
-    group_rows = row_index(groups)
-    slot_rows = row_index(LANES)
-
-    def radial_pair(k, r):
-        rows = lambda c: slice(c * SUB, (c + 1) * SUB)
-        if r == 0:
-            below = jnp.where(position == 0, x_ref[4 + k, rows(0)], edge[4 + k, rows(1)])
-        else:
-            below = x_ref[4 + k, rows(r - 1)]
-        if r == layers - 1:
-            above = jnp.where(position == last, x_ref[4 + k, rows(r)], edge[4 + k, rows(0)])
-        else:
-            above = x_ref[4 + k, rows(r + 1)]
-        return 0.5 * (above - below)
-
-    def lat_pair(value):
-        above = jnp.where(lane == LANES - 1, value, pltpu.roll(value, LANES - 1, 1))
-        below = jnp.where(lane == 0, value, pltpu.roll(value, 1, 1))
-        return 0.5 * (above - below)
-
-    def lon_pair(k, r, value):
-        above = jnp.where(sub == SUB - 1, above_all[k][r : r + 1, :], pltpu.roll(value, SUB - 1, 0))
-        below = jnp.where(sub == 0, below_all[k][r : r + 1, :], pltpu.roll(value, 1, 0))
-        return 0.5 * (above - below)
-
-    total = jnp.zeros((PARTS * groups, LANES), jnp.float32)
-    for r in range(layers):
-        b = [x_ref[4 + k, r * SUB : (r + 1) * SUB] for k in range(3)]
-        first = lon_pair(2, r, b[2]) - lat_pair(b[1])
-        second = lat_pair(b[0]) - radial_pair(2, r)
-        third = radial_pair(1, r) - lon_pair(0, r, b[0])
-        aligned = first * b[0] + second * b[1] + third * b[2]
-        field_sq = b[0] * b[0] + b[1] * b[1] + b[2] * b[2]
-        current = CELL_AREA * aligned * lax.rsqrt(1.0 + field_sq)
-        row, column = node_row_column(nodes_ref[r * SUB : (r + 1) * SUB], columns)
-        slot = row * width + (column - first_column)
+def lat_pair(value):
+    lane = lane_index(value.shape[0])
+    above = jnp.where(lane == LANES - 1, value, pltpu.roll(value, LANES - 1, 1))
+    below = jnp.where(lane == 0, value, pltpu.roll(value, 1, 1))
+    return 0.5 * (above - below)
+
+
+def aligned_current(b, radial, lon):
+    first = lon(2) - lat_pair(b[1])
+    second = lat_pair(b[0]) - radial(2)
+    third = radial(1) - lon(0)
+    aligned = first * b[0] + second * b[1] + third * b[2]
+    field_sq = b[0] * b[0] + b[1] * b[1] + b[2] * b[2]
+    return CELL_AREA * aligned * lax.rsqrt(1.0 + field_sq)
+
+
+class Scatter:
+    def __init__(self, width, columns):
+        self.width, self.columns = width, columns
+        self.first_column = lax.axis_index("shell") * width
+        self.groups = max(16, width)
+        self.group_rows = row_index(self.groups)
+        self.slot_rows = row_index(LANES)
+        self.total = jnp.zeros((PARTS * self.groups, LANES), jnp.float32)
+
+    def add(self, values, nodes, lines):
+        row, column = node_row_column(nodes, self.columns)
+        slot = row * self.width + (column - self.first_column)
         group, place = lax.shift_right_logical(slot, 7), slot & (LANES - 1)
-        parts = three_parts(current)
+        parts = split(values, PARTS)
         lefts, rights = [], []
-        for l in range(SUB):
-            here = group_rows == group[l : l + 1, :]
+        for l in lines:
+            here = self.group_rows == group[l : l + 1, :]
             lefts.append(
                 jnp.concatenate([jnp.where(here, part[l : l + 1, :], 0.0) for part in parts], axis=0)
             )
-            rights.append(jnp.where(slot_rows == place[l : l + 1, :], 1.0, 0.0))
+            rights.append(jnp.where(self.slot_rows == place[l : l + 1, :], 1.0, 0.0))
         left = jnp.concatenate(lefts, axis=1).astype(jnp.bfloat16)
         right = jnp.concatenate(rights, axis=1).astype(jnp.bfloat16)
-        total = total + lax.dot_general(
+        self.total = self.total + lax.dot_general(
             left, right, (((1,), (1,)), ((), ())), preferred_element_type=jnp.float32
         )
-    sums = total[:groups]
-    for part in range(1, PARTS):
-        sums = sums + total[part * groups : (part + 1) * groups]
+
+    def sums(self):
+        sums = self.total[: self.groups]
+        for part in range(1, PARTS):
+            sums = sums + self.total[part * self.groups : (part + 1) * self.groups]
+        return sums
+
+
+def inner_current_kernel(layers, width, columns, x_ref, edge, nodes_ref, _, out_ref):
+    position, last = lax.axis_index("radial"), lax.axis_size("radial") - 1
+    scatter = Scatter(width, columns)
+    rows = lambda r: slice(r * SUB, (r + 1) * SUB)
+    for r in range(layers):
+        b = [x_ref[4 + k, rows(r)] for k in range(3)]
+
+        def radial(k):
+            if r == 0:
+                below = jnp.where(position == 0, b[k], edge[4 + k, rows(1)])
+            else:
+                below = x_ref[4 + k, rows(r - 1)]
+            if r == layers - 1:
+                above = jnp.where(position == last, b[k], edge[4 + k, rows(0)])
+            else:
+                above = x_ref[4 + k, rows(r + 1)]
+            return 0.5 * (above - below)
+
+        def lon(k):
+            return 0.5 * (pltpu.roll(b[k], SUB - 1, 0) - pltpu.roll(b[k], 1, 0))
+
+        scatter.add(aligned_current(b, radial, lon), nodes_ref[rows(r)], range(1, SUB - 1))
+    out_ref[...] = scatter.sums()
+
+
+def outer_current_kernel(
+    layers, width, columns, window, x_ref, after, pair, edge, nodes_ref, inner_ref, _, out_ref, held
+):
+    position, last = lax.axis_index("radial"), lax.axis_size("radial") - 1
+    from_below = parity() == 1
+    scatter = Scatter(width, columns)
+    layer = row_index(layers)
+    for l in (0, SUB - 1):
+        line = lambda k, l: x_ref[4 + k, pl.ds(l, layers, stride=SUB), :]
+        b = [line(k, l) for k in range(3)]
+
+        def radial(k):
+            first = jnp.where(position == 0, b[k][:1], edge[4 + k, SUB + l : SUB + l + 1])
+            final = jnp.where(position == last, b[k][layers - 1 :], edge[4 + k, l : l + 1])
+            below = jnp.where(layer == 0, first, pltpu.roll(b[k], 1, 0))
+            above = jnp.where(layer == layers - 1, final, pltpu.roll(b[k], layers - 1, 0))
+            return 0.5 * (above - below)
+
+        def lon(k):
+            if l == 0:
+                return 0.5 * (line(k, 1) - jnp.where(from_below, pair[4 + k, 1], after[4 + k, 1]))
+            return 0.5 * (jnp.where(from_below, after[4 + k, 0], pair[4 + k, 0]) - line(k, l - 1))
+
+        values = aligned_current(b, radial, lon)
+        nodes = nodes_ref[pl.ds(l, layers, stride=SUB), :]
+        for r in range(0, layers, SUB):
+            scatter.add(values[r : r + SUB], nodes[r : r + SUB], range(SUB))
+    sums = inner_ref[...] + scatter.sums()
+    groups = scatter.groups
     if not window:
         out_ref[...] = sums[: out_ref.shape[0]]
         return
@@ -326,9 +385,9 @@
     high = blocks_ref.shape[0] - HALO
     odd = parity()
     for ref, first in ((pair_ref, jnp.where(odd == 1, 0, high)), (next_ref, jnp.where(odd == 1, high, 0))):
-        ref[...] = jnp.zeros_like(ref)
         for e in range(HALO):
             ref[e, :size] = blocks_ref[first + e]
+            ref[e, size:] = jnp.zeros((SUB, size), jnp.float32)
             for way in range(4):
                 ref[e, size + way : size + way + 1] = conductance_ref[way, pl.ds(first + e, 1)]
 
@@ -364,7 +423,6 @@
 ):
     position = lax.axis_index("radial")
     size = LANES
-    rows = SUB
     span = 3 * SUB
     base = SUB
     halves = []
@@ -382,25 +440,32 @@
     odd = parity()
     rims = ((own_pair, twin_pair, odd == 1), (own_next, twin_next, odd == 0))
 
-    def rim_rows(reach):
+    def rim_rows(side, reach):
         for own, twin, is_low in rims:
             for i in range(reach):
                 row = jnp.where(is_low, HALO - reach + i, i)
-                yield own, twin, row, jnp.where(is_low, SUB - reach + i, 2 * SUB + i)
+                yield (own, twin)[side], row, jnp.where(is_low, SUB - reach + i, 2 * SUB + i)
 
     for side, mid in enumerate((own_conductance, twin_conductance)):
         for way in range(4):
             cond[side, way, SUB : 2 * SUB] = mid[way]
-    for own, twin, row, place in rim_rows(HALO):
-        for side, rim in enumerate((own, twin)):
+    for side in range(2):
+        for rim, row, place in rim_rows(side, HALO - side):
             for way in range(4):
                 cond[side, way, pl.ds(place, 1)] = rim[row, size + way : size + way + 1]
     pot[...] = jnp.zeros_like(pot)
     eye = row_index(size, size) == lane_index(size, size)
+    ones = jnp.ones((SUM_PARTS * size, size), jnp.bfloat16)
+    turn = [0]
 
     def solve_row(side, matrix, row):
         product = matrix * rhs_ref[side, pl.ds(row, 1)]
-        column = jnp.sum(product, axis=1, keepdims=True)
+        turn[0] += 1
+        if turn[0] % MXU_EVERY == 0:
+            parts = jnp.concatenate(split(product, SUM_PARTS), axis=1).astype(jnp.bfloat16)
+            column = jnp.dot(parts, ones, preferred_element_type=jnp.float32)
+        else:
+            column = jnp.sum(product, axis=1, keepdims=True)
         line = jnp.sum(jnp.where(eye, column, 0.0), axis=0, keepdims=True)
         pot[side, pl.ds(base + row, 1)] = line
 
@@ -426,16 +491,18 @@
                 rhs.append(coupled)
         for side in sides:
             rhs_ref[side] = rhs[side]
-        for own, twin, row, place in rim_rows(reach):
-            for side, rim in enumerate((own, twin)):
+        for side in sides:
+            for rim, row, place in rim_rows(side, reach - side):
                 solve_row(side, rim[row, :size], place)
         for side in sides:
             for e in range(SUB):
                 solve_row(side, (own_blocks, twin_blocks)[side][e], SUB + e)
     result = pot[0, base + SUB : base + 2 * SUB]
     out_ref[...] = result
-    for d in range(send_ref.shape[0] // rows):
-        send_ref[d * rows : (d + 1) * rows] = result
+    packed = swap_blocks(result, width)
+    send_ref[...] = jnp.zeros_like(send_ref)
+    for twin in range(2):
+        send_ref[pl.ds(position * 2 * SUB + twin, SUB, stride=2), :] = packed
 
 
 def gather_kernel(width, columns, direct, table_ref, nodes_ref, out_ref):
@@ -444,24 +511,16 @@
         table = table_ref[...]
     else:
         half = lax.shift_right_logical(first_column, 7)
-        strip = table_ref[:, pl.ds(half, 1), :, :]
-        strip = strip.reshape(strip.shape[0] * SUB, LANES)
-        pick = lane_index(width) == row_index(width) + (first_column & (LANES - 1))
-        table = lax.dot_general(
-            jnp.where(pick, 1.0, 0.0),
-            strip,
-            (((1,), (1,)), ((), ())),
-            precision=lax.Precision.HIGHEST,
-            preferred_element_type=jnp.float32,
-        )
-    lines = [jnp.broadcast_to(table[c : c + 1, :], (SUB, LANES)) for c in range(width)]
+        table = table_ref[pl.ds(half, table_ref.shape[0] // 2, stride=2), :]
+    lines = [jnp.broadcast_to(table[c : c + 1, :], (SUB, LANES)) for c in range(table.shape[0])]
     for r in range(nodes_ref.shape[0] // SUB):
         rows = slice(r * SUB, (r + 1) * SUB)
         row, column = node_row_column(nodes_ref[rows], columns)
-        column = column - first_column
+        slot = row * width + (column - first_column)
+        group, place = lax.shift_right_logical(slot, 7), slot & (LANES - 1)
         value = jnp.zeros((SUB, LANES), jnp.float32)
-        for c in range(width):
-            value = jnp.where(column == c, jnp.take_along_axis(lines[c], row, axis=1), value)
+        for c, line in enumerate(lines):
+            value = jnp.where(group == c, jnp.take_along_axis(line, place, axis=1), value)
         out_ref[rows] = value
 
 
@@ -521,7 +580,7 @@
         potential = apply_blocks(coupled)
     full_rows = lax.all_gather(potential, "radial", axis=1, tiled=True)
     strip = lax.all_to_all(full_rows, "shell", split_axis=1, concat_axis=0, tiled=True)
-    return potential, strip.T
+    return potential, strip.reshape(width, LANES)
 
 
 def body(state, footpoints, conductance, inverse_blocks):
@@ -550,7 +609,10 @@
     if fast:
         rim_shape = shape_of(HALO, half + SUB, half)
         rim_pair, rim_next = call(
-            rim_kernel, [rim_shape, rim_shape], "rim", in_specs=[IN_VMEM, IN_VMEM, UNREAD]
+            rim_kernel,
+            [rim_shape, rim_shape],
+            "rim",
+            in_specs=[IN_VMEM, IN_VMEM, UNREAD],
         )(blocks, conductance, packed[2])
         rims = [
             lax.ppermute(rim_pair, "shell", pairs(0, False)),
@@ -558,24 +620,30 @@
         ]
 
     send_shape = shape_of(shells * radials * 4, LANES) if fast else shape_of(width, LANES)
+    groups = max(16, width)
+    inner = call(
+        functools.partial(inner_current_kernel, layers, width, columns), shape_of(groups, LANES), "inner_currents",
+        in_specs=[IN_VMEM] * 3 + [UNREAD],
+    )(x, halos[2], nodes, blocks)
     sums = call(
-        functools.partial(current_kernel, layers, width, columns, fast),
+        functools.partial(outer_current_kernel, layers, width, columns, fast),
         send_shape,
-        "currents",
+        "outer_currents",
         flops=CURRENTS,
-        scratch=[pltpu.VMEM((max(16, width) + 2 * SUB, LANES), jnp.float32)],
-    )(x, *halos, nodes)
-
-    section_one, *packed = call(
+        scratch=[pltpu.VMEM((groups + 2 * SUB, LANES), jnp.float32)],
+        in_specs=[IN_VMEM] * 6 + [UNREAD],
+    )(x, *halos, nodes, inner, blocks)
+
+    *section_one, after, pair, edge = call(
         functools.partial(first_stage_kernel, layers),
-        [shape_of(fields, cells, lats)] + halo_shapes,
+        [shape_of(fields // SPLIT, cells, lats)] * SPLIT + halo_shapes,
         "first_stage",
         flops=DEAR,
         scratch=stage_scratch,
         in_specs=[IN_VMEM] * 4 + [UNREAD],
     )(x, *halos, sums)
-    second_halos = exchange_halos(*packed)
-    after = sums
+    second_halos = exchange_halos(after, pair, edge)
+    later = sums
 
     if fast:
         rims = call(
@@ -592,7 +660,7 @@
         arrived = lax.all_to_all(sums, ("shell", "radial"), split_axis=0, concat_axis=0, tiled=True)
         potential, spread = call(
             functools.partial(sweep_kernel, width),
-            [shape_of(own_rows, half), shape_of(shells * radials * own_rows, half)],
+            [shape_of(own_rows, half), shape_of(shells * radials, half)],
             "sweeps",
             scratch=[
                 pltpu.VMEM((2, 5 * SUB, half), jnp.float32),
@@ -601,10 +669,9 @@
             ],
             flops=DEAR,
             in_specs=[IN_VMEM] * 9 + [UNREAD],
-        )(arrived, blocks, conductance, *rims, *twin_parts, packed[2])
-        after = spread
+        )(arrived, blocks, conductance, *rims, *twin_parts, edge)
+        later = spread
         table = lax.all_to_all(spread, ("shell", "radial"), split_axis=0, concat_axis=0, tiled=True)
-        table = table.reshape(shells, radials, own_rows, half)
     else:
         potential, table = general_solve(sums, conductance, blocks, rows_total, width)
 
@@ -614,8 +681,8 @@
         "second_stage",
         flops=DEAR,
         scratch=stage_scratch,
-        in_specs=[IN_VMEM] * 5 + [UNREAD],
-    )(section_one, *second_halos, x, after)
+        in_specs=[IN_VMEM] * 4 + [UNREAD] + [IN_VMEM] * SPLIT,
+    )(*second_halos, x, later, *section_one)
 
     footpoint_potential = call(
         functools.partial(gather_kernel, width, columns, not fast), shape_of(cells, lats), "gather"

time: 45.6 us -> 44 us (0.965)
  waiting for transfers between devices: 6.33 us -> 4.86 us
    ppermute x2, waiting for transfers between devices: 2.1 us -> 0.58 us  [exchange_halos(): lax.ppermute(pair, 'shell', pairs(0, True))]
    ppermute x2, starting transfers between devices: 11.9 us -> 11 us  [exchange_halos(): lax.ppermute(after, 'shell', pairs(1, True))]
    ppermute x1, waiting for transfers between devices: 0.83 us -> 1.6 us  [body(): lax.ppermute(rim_pair, 'shell', pairs(0, False))]
    all_to_all x1, waiting for transfers between devices: 3.37 us -> 2.65 us  [body(): lax.all_to_all(spread, ('shell', 'radial'), split_axis=0, concat_axis=0,...]
    ppermute x2, starting transfers between devices: 0.01 us -> 0.53 us  [exchange_halos(): lax.ppermute(pair, 'shell', pairs(0, True))]
    pallas_call x2 -> x3, Pallas kernels: 4.64 us -> 4.83 us  [the longest x1 2.56 us: body(): call(functools.partial(first_stage_kernel, layers), [shape_of(fields // S...]
  transfers between devices with their start and end apart: 14 -> 14, of which waited for: 4 -> 4; matrix products, arithmetic and copies ran while one was open for 0% -> 0% of each run, Pallas kernels for 24% -> 25%
where the time goes in v4:
time: 44 us; the launch traced here: 43.7 us
  starting transfers between devices  22.7 us (52%)
  Pallas kernels  11.9 us (27%)
  waiting for transfers between devices  4.86 us (11%)
  local copies, waits for them, and re-layouts  3.48 us (8%)
  between operations  0.77 us (2%)
    ppermute x2, starting transfers between devices, exchange_halos(): lax.ppermute(after, 'shell', pairs(1, True))  11 us
    all_to_all x1, starting transfers between devices, body(): lax.all_to_all(sums, ('shell', 'radial'), split_axis=0, concat_axis=0, ti...  3.97 us
    unnamed x16, local copies, waits for them, and re-layouts  3.48 us
    all_to_all x1, starting transfers between devices, body(): lax.all_to_all(spread, ('shell', 'radial'), split_axis=0, concat_axis=0,...  3.32 us
    pallas_call x1, Pallas kernels, body(): call(functools.partial(second_stage_kernel, layers), shape_of(fields, cel...  3.31 us
    pallas_call x1, Pallas kernels, body(): call(functools.partial(sweep_kernel, width), [shape_of(own_rows, half), s...  2.67 us
    all_to_all x1, waiting for transfers between devices, body(): lax.all_to_all(spread, ('shell', 'radial'), split_axis=0, concat_axis=0,...  2.65 us
    pallas_call x1, Pallas kernels, body(): call(functools.partial(first_stage_kernel, layers), [shape_of(fields // S...  2.56 us
  transfers between devices with their start and end apart: 14, of which 4 were waited for; matrix products, arithmetic and copies ran while one was open for 0% of the time, Pallas kernels for 25%

profile of v4, /device:TPU:0, one launch (start us, length us, event | category | flops | bytes accessed | tf_op | source)
XLA Modules:
  0.0 43.7 jit_solution(10043010891914239823)
XLA Ops:
  0.6 1.1 %copy-done.1 = f32[8,16,8,128]{3,2,1,0:T(8,128)S(1)} copy-done((f32[8,16,8,128]{3,2,1,0:T(8,128)S(1)}, f32[8,16,8,128]{3,2,1,0:T(8,128)}, u32[]{:S(2)}) %copy-start.1) | copy-done | bytes 524312
  1.7 0.1 pack.1
  1.8 7.0 %collective-permute-start = (f32[8,2,16,128]{3,2,1,0:T(8,128)S(1)}, f32[8,2,16,128]{3,2,1,0:T(8,128)S(1)}, u32[]{:S(2)}, u32[]{:S(2)}) collective-permute-start(f32[8,2,16,128]{3,2,1,0:T(8,128)S(1)} %get-tuple-element.17), channel_id=1, source_target_pairs={{2,4},{4,2},{6,8},{8,6},{10,12},{12,10},{14,16},{16,14},{18,20},{2... | collective-permute-start | bytes 393224 | tf_op jit(solution)/shard_map/ppermute | solution.py:548
  8.8 0.0 collective-permute-start.1
  8.8 0.0 collective-permute-start.2
  8.8 0.0 copy-start.4
  8.8 0.7 %copy-done.4 = f32[4,8,128]{2,1,0:T(8,128)S(1)} copy-done((f32[4,8,128]{2,1,0:T(8,128)S(1)}, f32[4,8,128]{2,1,0:T(8,128)}, u32[]{:S(2)}) %copy-start.4) | copy-done | bytes 16408
  9.6 2.1 %collective-permute-start.6 = (f32[3,136,128]{2,1,0:T(8,128)S(1)}, f32[3,136,128]{2,1,0:T(8,128)S(1)}, u32[]{:S(2)}, u32[]{:S(2)}) collective-permute-start(f32[3,136,128]{2,1,0:T(8,128)S(1)} %get-tuple-element.23), channel_id=1, source_target_pairs={{0,2},{2,0},{4,6},{6,4},{8,10},{10,8},{12,14},{14,12},{16,18},{18,... | collective-permute-start | bytes 626696 | tf_op jit(solution)/shard_map/ppermute | solution.py:618
  11.7 0.7 %collective-permute-start.7 = (f32[3,136,128]{2,1,0:T(8,128)S(1)}, f32[3,136,128]{2,1,0:T(8,128)S(1)}, u32[]{:S(2)}, u32[]{:S(2)}) collective-permute-start(f32[3,136,128]{2,1,0:T(8,128)S(1)} %get-tuple-element.24), channel_id=1, source_target_pairs={{2,4},{4,2},{6,8},{8,6},{10,12},{12,10},{14,16},{16,14},{18,20},{2... | collective-permute-start | bytes 626696 | tf_op jit(solution)/shard_map/ppermute | solution.py:619
  12.3 0.3 collective-permute-start.8
  12.6 1.1 %inner_currents.1.inner_ref = f32[16,128]{1,0:T(8,128)S(1)} custom-call(f32[8,128,128]{2,1,0:T(8,128)S(1)} %bitcast.17, f32[8,16,128]{2,1,0:T(8,128)S(1)} %collective-permute-done.2.edge, s32[128,128]{1,0:T(8,128)S(1)} %bitcast.21, f32[8,128,128]{2,1,0:T(8,128)S(1)} %bitcast.13), custom_call_target="tpu_custom_call" | custom-call | flops 1000 | bytes 1000 | tf_op jit(solution)/shard_map/inner_currents/pallas_call | solution.py:624
  13.7 0.0 collective-permute-done.after
  13.7 0.0 copy-done.5
  13.8 0.3 collective-permute-start.9
  14.1 0.4 %collective-permute-done.1.pair = f32[8,2,16,128]{3,2,1,0:T(8,128)S(1)} collective-permute-done((f32[8,2,16,128]{3,2,1,0:T(8,128)S(1)}, f32[8,2,16,128]{3,2,1,0:T(8,128)S(1)}, u32[]{:S(2)}, u32[]{:S(2)}) %collective-permute-start.1) | collective-permute-done | bytes 131104 | tf_op jit(solution)/shard_map/ppermute | solution.py:549
  14.6 1.2 %outer_currents.1._.refs_2_ = f32[128,128]{1,0:T(8,128)} custom-call(f32[8,128,128]{2,1,0:T(8,128)S(1)} %bitcast.18, f32[8,2,16,128]{3,2,1,0:T(8,128)S(1)} %collective-permute-done.after, f32[8,2,16,128]{3,2,1,0:T(8,128)S(1)} %collective-permute-done.1.pair, f32[8,16,128]{2,1,0:T(8,128)S(1)} %collective-permute-done.2.edge, s32[128,128]{1,0:T(8,128)S(1)} %bitcast.22, ...), custom_call_target="tpu_custom_call" | custom-call | flops 2000000000 | bytes 1000 | tf_op jit(solution)/shard_map/outer_currents/pallas_call | solution.py:628
  15.7 4.0 %all-to-all-start = ((f32[32,4,128]{2,1,0:T(4,128)}), f32[32,4,128]{2,1,0:T(4,128)S(1)}, u32[]{:S(2)}, u32[]{:S(2)}) async-start(f32[32,4,128]{2,1,0:T(4,128)} %bitcast.3), calls=%async_computation | async-start | bytes 131072 | tf_op jit(solution)/shard_map/all_to_all | solution.py:660
  19.7 1.6 %collective-permute-done.6.refs_0_ = f32[3,136,128]{2,1,0:T(8,128)S(1)} collective-permute-done((f32[3,136,128]{2,1,0:T(8,128)S(1)}, f32[3,136,128]{2,1,0:T(8,128)S(1)}, u32[]{:S(2)}, u32[]{:S(2)}) %collective-permute-start.6) | collective-permute-done | bytes 208928 | tf_op jit(solution)/shard_map/ppermute | solution.py:618
  21.3 0.0 collective-permute-start.10
  21.3 0.5 %collective-permute-start.11 = (f32[3,136,128]{2,1,0:T(8,128)S(1)}, f32[3,136,128]{2,1,0:T(8,128)S(1)}, u32[]{:S(2)}, u32[]{:S(2)}) collective-permute-start(f32[3,136,128]{2,1,0:T(8,128)S(1)} %get-tuple-element.26.own_next), channel_id=1, source_target_pairs={{0,1},{1,0},{2,3},{3,2},{4,5},{5,4},{6,7},{7,6},{8,9},{9,8},{10,11... | collective-permute-start | bytes 626696 | tf_op jit(solution)/shard_map/ppermute | solution.py:659
  21.8 2.6 %first_stage.1 = (f32[4,128,128]{2,1,0:T(8,128)S(1)}, f32[4,128,128]{2,1,0:T(8,128)S(1)}, f32[8,2,16,128]{3,2,1,0:T(8,128)S(1)}, f32[8,2,16,128]{3,2,1,0:T(8,128)S(1)}, f32[8,16,128]{2,1,0:T(8,128)S(1)}) custom-call(f32[8,128,128]{2,1,0:T(8,128)S(1)} %bitcast.19, f32[8,2,16,128]{3,2,1,0:T(8,128)S(1)} %collective-permute-done.after, ...), custom_call_target="tpu_custom_call" | custom-call | flops 10000000000 | bytes 1000 | tf_op jit(solution)/shard_map/first_stage/pallas_call | solution.py:637
  24.4 0.0 copy-start.6
  24.4 0.7 %copy-done.6 = f32[4,128,128]{2,1,0:T(8,128)} copy-done((f32[4,128,128]{2,1,0:T(8,128)}, f32[4,128,128]{2,1,0:T(8,128)S(1)}, u32[]{:S(2)}) %copy-start.6) | copy-done | bytes 262168
  25.1 4.0 %collective-permute-start.3 = (f32[8,2,16,128]{3,2,1,0:T(8,128)S(1)}, f32[8,2,16,128]{3,2,1,0:T(8,128)S(1)}, u32[]{:S(2)}, u32[]{:S(2)}) collective-permute-start(f32[8,2,16,128]{3,2,1,0:T(8,128)S(1)} %get-tuple-element.20), channel_id=1, source_target_pairs={{2,4},{4,2},{6,8},{8,6},{10,12},{12,10},{14,16},{16,14},{18,20},{2... | collective-permute-start | bytes 393224 | tf_op jit(solution)/shard_map/ppermute | solution.py:548
  29.1 0.5 %collective-permute-start.4 = (f32[8,2,16,128]{3,2,1,0:T(8,128)S(1)}, f32[8,2,16,128]{3,2,1,0:T(8,128)S(1)}, u32[]{:S(2)}, u32[]{:S(2)}) collective-permute-start(f32[8,2,16,128]{3,2,1,0:T(8,128)S(1)} %get-tuple-element.21), channel_id=1, source_target_pairs={{0,2},{2,0},{4,6},{6,4},{8,10},{10,8},{12,14},{14,12},{16,18},{18,... | collective-permute-start | bytes 393224 | tf_op jit(solution)/shard_map/ppermute | solution.py:549
  29.6 2.7 %sweeps.1 = (f32[8,128]{1,0:T(8,128)}, f32[32,128]{1,0:T(8,128)}) custom-call(f32[128,128]{1,0:T(8,128)S(1)} %bitcast.25, f32[8,128,128]{2,1,0:T(8,128)S(1)} %bitcast.15, f32[4,8,128]{2,1,0:T(8,128)S(1)} %copy-done.5, f32[3,136,128]{2,1,0:T(8,128)S(1)} %get-tuple-element.25.own_pair, f32[3,136,128]{2,1,0:T(8,128)S(1)} %get-tuple-element.26.own_next, ...), custom_call_target="tpu_custom_call" | custom-call | flops 10000000000 | bytes 1000 | tf_op jit(solution)/shard_map/sweeps/pallas_call | solution.py:661
  32.3 3.3 %all-to-all-start.1 = ((f32[32,1,128]{2,1,0:T(1,128)}), f32[32,1,128]{2,1,0:T(1,128)S(1)}, u32[]{:S(2)}, u32[]{:S(2)}) async-start(f32[32,1,128]{2,1,0:T(1,128)} %bitcast.7), calls=%async_computation.1 | async-start | bytes 32768 | tf_op jit(solution)/shard_map/all_to_all | solution.py:674
  35.6 0.1 collective-permute-done.4.pair
  35.8 0.9 %copy-done.7 = f32[4,128,128]{2,1,0:T(8,128)S(1)} copy-done((f32[4,128,128]{2,1,0:T(8,128)S(1)}, f32[4,128,128]{2,1,0:T(8,128)}, u32[]{:S(2)}) %copy-start.7) | copy-done | bytes 262168
  36.7 3.3 %second_stage.1 = f32[8,128,128]{2,1,0:T(8,128)} custom-call(f32[8,2,16,128]{3,2,1,0:T(8,128)S(1)} %collective-permute-done.3.after, f32[8,2,16,128]{3,2,1,0:T(8,128)S(1)} %collective-permute-done.4.pair, f32[8,16,128]{2,1,0:T(8,128)S(1)} %collective-permute-done.5.edge, f32[8,128,128]{2,1,0:T(8,128)S(1)} %bitcast.20, f32[32,128]{1,0:T(8,128)} %get-tuple-element.27._, ...), custom_call_target="tpu_custom_call" | custom-call | flops 10000000000 | bytes 1000 | tf_op jit(solution)/shard_map/second_stage/pallas_call | solution.py:678
  40.0 2.7 %all-to-all-done.1 = f32[32,1,128]{2,1,0:T(1,128)S(1)} async-done(((f32[32,1,128]{2,1,0:T(1,128)}), f32[32,1,128]{2,1,0:T(1,128)S(1)}, u32[]{:S(2)}, u32[]{:S(2)}) %all-to-all-start.1) | async-done | bytes 16416 | tf_op jit(solution)/shard_map/all_to_all | solution.py:674
  42.7 1.0 %gather.1 = f32[128,128]{1,0:T(8,128)} custom-call(f32[32,128]{1,0:T(8,128)S(1)} %bitcast.24, s32[128,128]{1,0:T(8,128)S(1)} %bitcast.23), custom_call_target="tpu_custom_call" | custom-call | flops 1000 | bytes 1000 | tf_op jit(solution)/shard_map/gather/pallas_call | solution.py:687
  (21 shorter events, 0.1 us)
Async XLA Ops:
  0.6 8.2 %copy-start = (f32[8,1,128,128]{3,2,1,0:T(8,128)S(1)}, f32[8,1,128,128]{3,2,1,0:T(8,128)}, u32[]{:S(2)}) copy-start(f32[8,1,128,128]{3,2,1,0:T(8,128)} %param.7) | copy-start | bytes 1572868
  0.6 1.1 %copy-start.1 = (f32[8,16,8,128]{3,2,1,0:T(8,128)S(1)}, f32[8,16,8,128]{3,2,1,0:T(8,128)}, u32[]{:S(2)}) copy-start(f32[8,16,8,128]{3,2,1,0:T(8,128)} %param.4) | copy-start | bytes 1572868
  1.7 10.9 %copy-start.2 = (f32[8,16,8,128]{3,2,1,0:T(8,128)S(1)}, f32[8,16,8,128]{3,2,1,0:T(8,128)}, u32[]{:S(2)}) copy-start(f32[8,16,8,128]{3,2,1,0:T(8,128)} %param.4) | copy-start | bytes 1572868
  1.8 11.9 %collective-permute-start = (f32[8,2,16,128]{3,2,1,0:T(8,128)S(1)}, f32[8,2,16,128]{3,2,1,0:T(8,128)S(1)}, u32[]{:S(2)}, u32[]{:S(2)}) collective-permute-start(f32[8,2,16,128]{3,2,1,0:T(8,128)S(1)} %get-tuple-element.17), channel_id=1, source_target_pairs={{2,4},{4,2},{6,8},{8,6},{10,12},{12,10},{14,16},{16,14},{18,20},{2... | collective-permute-start | bytes 393224 | tf_op jit(solution)/shard_map/ppermute | solution.py:548
  8.8 5.8 %collective-permute-start.1 = (f32[8,2,16,128]{3,2,1,0:T(8,128)S(1)}, f32[8,2,16,128]{3,2,1,0:T(8,128)S(1)}, u32[]{:S(2)}, u32[]{:S(2)}) collective-permute-start(f32[8,2,16,128]{3,2,1,0:T(8,128)S(1)} %get-tuple-element.18), channel_id=1, source_target_pairs={{0,2},{2,0},{4,6},{6,4},{8,10},{10,8},{12,14},{14,12},{16,18},{18,... | collective-permute-start | bytes 393224 | tf_op jit(solution)/shard_map/ppermute | solution.py:549
  8.8 3.5 %collective-permute-start.2 = (f32[8,16,128]{2,1,0:T(8,128)S(1)}, f32[8,16,128]{2,1,0:T(8,128)S(1)}, u32[]{:S(2)}, u32[]{:S(2)}) collective-permute-start(f32[8,16,128]{2,1,0:T(8,128)S(1)} %get-tuple-element.19._), channel_id=1, source_target_pairs={{0,1},{1,0},{2,3},{3,2},{4,5},{5,4},{6,7},{7,6},{8,9},{9,8},{10,11... | collective-permute-start | bytes 196616 | tf_op jit(solution)/shard_map/ppermute | solution.py:550
  8.8 0.7 %copy-start.4 = (f32[4,8,128]{2,1,0:T(8,128)S(1)}, f32[4,8,128]{2,1,0:T(8,128)}, u32[]{:S(2)}) copy-start(f32[4,8,128]{2,1,0:T(8,128)} %own_conductance.1) | copy-start | bytes 49156
  9.5 3.1 %copy-start.3 = (s32[16,8,128]{2,1,0:T(8,128)S(1)}, s32[16,8,128]{2,1,0:T(8,128)}, u32[]{:S(2)}) copy-start(s32[16,8,128]{2,1,0:T(8,128)} %param.5) | copy-start | bytes 196612
  9.6 11.7 %collective-permute-start.6 = (f32[3,136,128]{2,1,0:T(8,128)S(1)}, f32[3,136,128]{2,1,0:T(8,128)S(1)}, u32[]{:S(2)}, u32[]{:S(2)}) collective-permute-start(f32[3,136,128]{2,1,0:T(8,128)S(1)} %get-tuple-element.23), channel_id=1, source_target_pairs={{0,2},{2,0},{4,6},{6,4},{8,10},{10,8},{12,14},{14,12},{16,18},{18,... | collective-permute-start | bytes 626696 | tf_op jit(solution)/shard_map/ppermute | solution.py:618
  11.7 9.7 %collective-permute-start.7 = (f32[3,136,128]{2,1,0:T(8,128)S(1)}, f32[3,136,128]{2,1,0:T(8,128)S(1)}, u32[]{:S(2)}, u32[]{:S(2)}) collective-permute-start(f32[3,136,128]{2,1,0:T(8,128)S(1)} %get-tuple-element.24), channel_id=1, source_target_pairs={{2,4},{4,2},{6,8},{8,6},{10,12},{12,10},{14,16},{16,14},{18,20},{2... | collective-permute-start | bytes 626696 | tf_op jit(solution)/shard_map/ppermute | solution.py:619
  12.3 17.3 %collective-permute-start.8 = (f32[8,128,128]{2,1,0:T(8,128)S(1)}, f32[8,128,128]{2,1,0:T(8,128)S(1)}, u32[]{:S(2)}, u32[]{:S(2)}) collective-permute-start(f32[8,128,128]{2,1,0:T(8,128)S(1)} %bitcast.12), channel_id=1, source_target_pairs={{0,1},{1,0},{2,3},{3,2},{4,5},{5,4},{6,7},{7,6},{8,9},{9,8},{10,11... | collective-permute-start | bytes 1572872 | tf_op jit(solution)/shard_map/ppermute | solution.py:659
  12.6 1.1 %copy-start.5 = (f32[4,8,128]{2,1,0:T(8,128)S(1)}, f32[4,8,128]{2,1,0:T(8,128)}, u32[]{:S(2)}) copy-start(f32[4,8,128]{2,1,0:T(8,128)} %own_conductance.1) | copy-start | bytes 49156
  13.8 15.3 %collective-permute-start.9 = (f32[4,8,128]{2,1,0:T(8,128)S(1)}, f32[4,8,128]{2,1,0:T(8,128)S(1)}, u32[]{:S(2)}, u32[]{:S(2)}) collective-permute-start(f32[4,8,128]{2,1,0:T(8,128)S(1)} %copy-done.5), channel_id=1, source_target_pairs={{0,1},{1,0},{2,3},{3,2},{4,5},{5,4},{6,7},{7,6},{8,9},{9,8},{10,11... | collective-permute-start | bytes 49160 | tf_op jit(solution)/shard_map/ppermute | solution.py:659
  15.7 13.9 %all-to-all-start = ((f32[32,4,128]{2,1,0:T(4,128)}), f32[32,4,128]{2,1,0:T(4,128)S(1)}, u32[]{:S(2)}, u32[]{:S(2)}) async-start(f32[32,4,128]{2,1,0:T(4,128)} %bitcast.3), calls=%async_computation | async-start | bytes 131072 | tf_op jit(solution)/shard_map/all_to_all | solution.py:660
  21.3 8.3 %collective-permute-start.10 = (f32[3,136,128]{2,1,0:T(8,128)S(1)}, f32[3,136,128]{2,1,0:T(8,128)S(1)}, u32[]{:S(2)}, u32[]{:S(2)}) collective-permute-start(f32[3,136,128]{2,1,0:T(8,128)S(1)} %get-tuple-element.25.own_pair), channel_id=1, source_target_pairs={{0,1},{1,0},{2,3},{3,2},{4,5},{5,4},{6,7},{7,6},{8,9},{9,8},{10,11... | collective-permute-start | bytes 626696 | tf_op jit(solution)/shard_map/ppermute | solution.py:659
  21.3 8.3 %collective-permute-start.11 = (f32[3,136,128]{2,1,0:T(8,128)S(1)}, f32[3,136,128]{2,1,0:T(8,128)S(1)}, u32[]{:S(2)}, u32[]{:S(2)}) collective-permute-start(f32[3,136,128]{2,1,0:T(8,128)S(1)} %get-tuple-element.26.own_next), channel_id=1, source_target_pairs={{0,1},{1,0},{2,3},{3,2},{4,5},{5,4},{6,7},{7,6},{8,9},{9,8},{10,11... | collective-permute-start | bytes 626696 | tf_op jit(solution)/shard_map/ppermute | solution.py:659
  24.4 0.7 %copy-start.6 = (f32[4,128,128]{2,1,0:T(8,128)}, f32[4,128,128]{2,1,0:T(8,128)S(1)}, u32[]{:S(2)}) copy-start(f32[4,128,128]{2,1,0:T(8,128)S(1)} %get-tuple-element.29.refs_1_) | copy-start | bytes 786436
  25.1 10.5 %collective-permute-start.3 = (f32[8,2,16,128]{3,2,1,0:T(8,128)S(1)}, f32[8,2,16,128]{3,2,1,0:T(8,128)S(1)}, u32[]{:S(2)}, u32[]{:S(2)}) collective-permute-start(f32[8,2,16,128]{3,2,1,0:T(8,128)S(1)} %get-tuple-element.20), channel_id=1, source_target_pairs={{2,4},{4,2},{6,8},{8,6},{10,12},{12,10},{14,16},{16,14},{18,20},{2... | collective-permute-start | bytes 393224 | tf_op jit(solution)/shard_map/ppermute | solution.py:548
  29.1 6.7 %collective-permute-start.4 = (f32[8,2,16,128]{3,2,1,0:T(8,128)S(1)}, f32[8,2,16,128]{3,2,1,0:T(8,128)S(1)}, u32[]{:S(2)}, u32[]{:S(2)}) collective-permute-start(f32[8,2,16,128]{3,2,1,0:T(8,128)S(1)} %get-tuple-element.21), channel_id=1, source_target_pairs={{0,2},{2,0},{4,6},{6,4},{8,10},{10,8},{12,14},{14,12},{16,18},{18,... | collective-permute-start | bytes 393224 | tf_op jit(solution)/shard_map/ppermute | solution.py:549
  29.6 6.0 %collective-permute-start.5 = (f32[8,16,128]{2,1,0:T(8,128)S(1)}, f32[8,16,128]{2,1,0:T(8,128)S(1)}, u32[]{:S(2)}, u32[]{:S(2)}) collective-permute-start(f32[8,16,128]{2,1,0:T(8,128)S(1)} %get-tuple-element.22._), channel_id=1, source_target_pairs={{0,1},{1,0},{2,3},{3,2},{4,5},{5,4},{6,7},{7,6},{8,9},{9,8},{10,11... | collective-permute-start | bytes 196616 | tf_op jit(solution)/shard_map/ppermute | solution.py:550
  32.3 10.4 %all-to-all-start.1 = ((f32[32,1,128]{2,1,0:T(1,128)}), f32[32,1,128]{2,1,0:T(1,128)S(1)}, u32[]{:S(2)}, u32[]{:S(2)}) async-start(f32[32,1,128]{2,1,0:T(1,128)} %bitcast.7), calls=%async_computation.1 | async-start | bytes 32768 | tf_op jit(solution)/shard_map/all_to_all | solution.py:674
  35.8 1.0 %copy-start.7 = (f32[4,128,128]{2,1,0:T(8,128)S(1)}, f32[4,128,128]{2,1,0:T(8,128)}, u32[]{:S(2)}) copy-start(f32[4,128,128]{2,1,0:T(8,128)} %copy-done.6) | copy-start | bytes 786436

commit v5 on v4

--- a/solution.py
+++ b/solution.py
@@ -14,10 +14,10 @@
 TINY = 1e-37
 LANES = 128
 SPLIT = 2
-UNROLL = (4, 4, 8)
+UNROLL = (8, 8, 8)
 SUB = 8
 PARTS = 3
-SUM_PARTS, MXU_EVERY = 2, 2
+SUM_PARTS, MXU_EVERY = 2, 3
 VMEM_LIMIT = 6 * 1024 * 1024
 CHEAP, CURRENTS, RELAY, DEAR = 1_000, 2_000_000_000, 1_000, 10_000_000_000
 IN_HBM = pl.BlockSpec(memory_space=pltpu.HBM)
@@ -146,7 +146,7 @@
         edge_ref[k] = source[k, pl.ds(first, 2 * SUB), :]
 
 
-def tendency_into(x_ref, next_ref, pair_ref, edge_ref, xr, xl, div, layers, position, last, finish):
+def tendency_into(x_ref, next_ref, pair_ref, edge_ref, xr, xl, div, lon_div, layers, position, last, finish):
     cells = layers * SUB
     from_below = parity() == 1
     for k in range(8):
@@ -184,22 +184,23 @@
         return [xl[k, pl.ds(start, layers), :] for k in range(8)]
 
     def emit_lon(c, values):
+        start = pl.multiple_of(c * layers, SUB)
         for k in range(8):
-            rows = pl.ds(c, layers, stride=SUB)
-            div[k, rows, :] = div[k, rows, :] + values[k]
+            lon_div[k, pl.ds(start, layers), :] = values[k]
 
     march(load_lon, SUB, 1, emit_lon, UNROLL[1])
 
     lane = lane_index(SUB)
     at_first, at_last = lane == 0, lane == LANES - 1
+    half_inside = jnp.where(at_first | at_last, 0.0, 0.5)
 
     def layer(r, carry):
         rows = pl.ds(pl.multiple_of(r * SUB, SUB), SUB)
         x = [x_ref[k, rows, :] for k in range(8)]
         left, right = [], []
         for k in range(8):
-            jump = jnp.where(at_last, 0.0, pltpu.roll(x[k], LANES - 1, 1) - x[k])
-            half = 0.5 * minmod(jump, pltpu.roll(jump, 1, 1))
+            jump = pltpu.roll(x[k], LANES - 1, 1) - x[k]
+            half = half_inside * minmod(jump, pltpu.roll(jump, 1, 1))
             left.append(x[k] + half)
             down = x[k] - half
             right.append(jnp.where(at_last, down, pltpu.roll(down, LANES - 1, 1)))
@@ -207,8 +208,9 @@
         total = []
         for k in range(8):
             edge = 0.0 if left_flux[k] is None else 2.0 * left_flux[k]
+            aside = div[k, rows, :] + lon_div[k, pl.ds(r, SUB, stride=layers), :]
             total.append(
-                div[k, rows, :] + flux[k] - jnp.where(at_first, edge, pltpu.roll(flux[k], 1, 1))
+                aside + flux[k] - jnp.where(at_first, edge, pltpu.roll(flux[k], 1, 1))
             )
         finish(rows, x, total)
         return carry
@@ -225,26 +227,26 @@
 
 
 def first_stage_kernel(layers, x_ref, after, pair, edge, _, *refs):
-    out_ref, (next_ref, pair_ref, edge_ref, xr, xl, div) = Fields(refs[:-6]), refs[-6:]
+    out_ref, (next_ref, pair_ref, edge_ref, xr, xl, div, lon_div) = Fields(refs[:-7]), refs[-7:]
     position, last = lax.axis_index("radial"), lax.axis_size("radial") - 1
 
     def finish(rows, x, total):
         for k in range(8):
             out_ref[k, rows, :] = x[k] - 0.5 * TIME_STEP * total[k]
 
-    tendency_into(x_ref, after, pair, edge, xr, xl, div, layers, position, last, finish)
+    tendency_into(x_ref, after, pair, edge, xr, xl, div, lon_div, layers, position, last, finish)
     pack_halos(out_ref, next_ref, pair_ref, edge_ref, layers, position)
 
 
 def second_stage_kernel(layers, after, pair, edge, state_ref, _, *refs):
-    x_ref, (out_ref, xr, xl, div) = Fields(refs[:-4]), refs[-4:]
+    x_ref, (out_ref, xr, xl, div, lon_div) = Fields(refs[:-5]), refs[-5:]
     position, last = lax.axis_index("radial"), lax.axis_size("radial") - 1
 
     def finish(rows, x, total):
         for k in range(8):
             out_ref[k, rows, :] = 0.5 * state_ref[k, rows, :] + 0.5 * (x[k] - 0.5 * TIME_STEP * total[k])
 
-    tendency_into(x_ref, after, pair, edge, xr, xl, div, layers, position, last, finish)
+    tendency_into(x_ref, after, pair, edge, xr, xl, div, lon_div, layers, position, last, finish)
 
 
 def log2_of(value):
@@ -602,6 +604,7 @@
         pltpu.VMEM((8, cells + 4 * SUB, lats), jnp.float32),
         pltpu.VMEM((8, (SUB + 4) * layers, lats), jnp.float32),
         pltpu.VMEM((8, cells, lats), jnp.float32),
+        pltpu.VMEM((8, cells, lats), jnp.float32),
     ]
     packed = call(functools.partial(pack_kernel, layers), halo_shapes, "pack")(x)
     halos = exchange_halos(*packed)

time: 44 us -> 43.8 us (level)
  transfers between devices with their start and end apart: 14 -> 14, of which waited for: 4 -> 4; matrix products, arithmetic and copies ran while one was open for 0% -> 0% of each run, Pallas kernels for 25% -> 24%
where the time goes in v5:
time: 43.8 us; the launch traced here: 43.5 us
  starting transfers between devices  22.7 us (52%)
  Pallas kernels  11.7 us (27%)
  waiting for transfers between devices  4.89 us (11%)
  local copies, waits for them, and re-layouts  3.48 us (8%)
  between operations  0.77 us (2%)
    ppermute x2, starting transfers between devices, exchange_halos(): lax.ppermute(after, 'shell', pairs(1, True))  11 us
    all_to_all x1, starting transfers between devices, body(): lax.all_to_all(sums, ('shell', 'radial'), split_axis=0, concat_axis=0, ti...  3.97 us
    unnamed x16, local copies, waits for them, and re-layouts  3.48 us
    all_to_all x1, starting transfers between devices, body(): lax.all_to_all(spread, ('shell', 'radial'), split_axis=0, concat_axis=0,...  3.33 us
    pallas_call x1, Pallas kernels, body(): call(functools.partial(second_stage_kernel, layers), shape_of(fields, cel...  3.28 us
    all_to_all x1, waiting for transfers between devices, body(): lax.all_to_all(spread, ('shell', 'radial'), split_axis=0, concat_axis=0,...  2.63 us
    pallas_call x1, Pallas kernels, body(): call(functools.partial(sweep_kernel, width), [shape_of(own_rows, half), s...  2.61 us
    pallas_call x1, Pallas kernels, body(): call(functools.partial(first_stage_kernel, layers), [shape_of(fields // S...  2.43 us
  transfers between devices with their start and end apart: 14, of which 4 were waited for; matrix products, arithmetic and copies ran while one was open for 0% of the time, Pallas kernels for 24%

profile of v5, /device:TPU:0, one launch (start us, length us, event | category | flops | bytes accessed | tf_op | source)
XLA Modules:
  0.0 43.5 jit_solution(7932282351652439512)
XLA Ops:
  0.6 1.1 %copy-done.1 = f32[8,16,8,128]{3,2,1,0:T(8,128)S(1)} copy-done((f32[8,16,8,128]{3,2,1,0:T(8,128)S(1)}, f32[8,16,8,128]{3,2,1,0:T(8,128)}, u32[]{:S(2)}) %copy-start.1) | copy-done | bytes 524312
  1.7 0.1 pack.1
  1.8 7.0 %collective-permute-start = (f32[8,2,16,128]{3,2,1,0:T(8,128)S(1)}, f32[8,2,16,128]{3,2,1,0:T(8,128)S(1)}, u32[]{:S(2)}, u32[]{:S(2)}) collective-permute-start(f32[8,2,16,128]{3,2,1,0:T(8,128)S(1)} %get-tuple-element.17), channel_id=1, source_target_pairs={{2,4},{4,2},{6,8},{8,6},{10,12},{12,10},{14,16},{16,14},{18,20},{2... | collective-permute-start | bytes 393224 | tf_op jit(solution)/shard_map/ppermute | solution.py:550
  8.8 0.0 collective-permute-start.1
  8.8 0.0 collective-permute-start.2
  8.8 0.0 copy-start.4
  8.8 0.7 %copy-done.4 = f32[4,8,128]{2,1,0:T(8,128)S(1)} copy-done((f32[4,8,128]{2,1,0:T(8,128)S(1)}, f32[4,8,128]{2,1,0:T(8,128)}, u32[]{:S(2)}) %copy-start.4) | copy-done | bytes 16408
  9.6 2.1 %collective-permute-start.6 = (f32[3,136,128]{2,1,0:T(8,128)S(1)}, f32[3,136,128]{2,1,0:T(8,128)S(1)}, u32[]{:S(2)}, u32[]{:S(2)}) collective-permute-start(f32[3,136,128]{2,1,0:T(8,128)S(1)} %get-tuple-element.23), channel_id=1, source_target_pairs={{0,2},{2,0},{4,6},{6,4},{8,10},{10,8},{12,14},{14,12},{16,18},{18,... | collective-permute-start | bytes 626696 | tf_op jit(solution)/shard_map/ppermute | solution.py:621
  11.7 0.7 %collective-permute-start.7 = (f32[3,136,128]{2,1,0:T(8,128)S(1)}, f32[3,136,128]{2,1,0:T(8,128)S(1)}, u32[]{:S(2)}, u32[]{:S(2)}) collective-permute-start(f32[3,136,128]{2,1,0:T(8,128)S(1)} %get-tuple-element.24), channel_id=1, source_target_pairs={{2,4},{4,2},{6,8},{8,6},{10,12},{12,10},{14,16},{16,14},{18,20},{2... | collective-permute-start | bytes 626696 | tf_op jit(solution)/shard_map/ppermute | solution.py:622
  12.3 0.3 collective-permute-start.8
  12.6 1.1 %inner_currents.1.inner_ref = f32[16,128]{1,0:T(8,128)S(1)} custom-call(f32[8,128,128]{2,1,0:T(8,128)S(1)} %bitcast.17, f32[8,16,128]{2,1,0:T(8,128)S(1)} %collective-permute-done.2.edge, s32[128,128]{1,0:T(8,128)S(1)} %bitcast.21, f32[8,128,128]{2,1,0:T(8,128)S(1)} %bitcast.13), custom_call_target="tpu_custom_call" | custom-call | flops 1000 | bytes 1000 | tf_op jit(solution)/shard_map/inner_currents/pallas_call | solution.py:627
  13.7 0.0 collective-permute-done.after
  13.7 0.0 copy-done.5
  13.8 0.3 collective-permute-start.9
  14.1 0.4 %collective-permute-done.1.pair = f32[8,2,16,128]{3,2,1,0:T(8,128)S(1)} collective-permute-done((f32[8,2,16,128]{3,2,1,0:T(8,128)S(1)}, f32[8,2,16,128]{3,2,1,0:T(8,128)S(1)}, u32[]{:S(2)}, u32[]{:S(2)}) %collective-permute-start.1) | collective-permute-done | bytes 131104 | tf_op jit(solution)/shard_map/ppermute | solution.py:551
  14.6 1.2 %outer_currents.1._.refs_2_ = f32[128,128]{1,0:T(8,128)} custom-call(f32[8,128,128]{2,1,0:T(8,128)S(1)} %bitcast.18, f32[8,2,16,128]{3,2,1,0:T(8,128)S(1)} %collective-permute-done.after, f32[8,2,16,128]{3,2,1,0:T(8,128)S(1)} %collective-permute-done.1.pair, f32[8,16,128]{2,1,0:T(8,128)S(1)} %collective-permute-done.2.edge, s32[128,128]{1,0:T(8,128)S(1)} %bitcast.22, ...), custom_call_target="tpu_custom_call" | custom-call | flops 2000000000 | bytes 1000 | tf_op jit(solution)/shard_map/outer_currents/pallas_call | solution.py:631
  15.7 4.0 %all-to-all-start = ((f32[32,4,128]{2,1,0:T(4,128)}), f32[32,4,128]{2,1,0:T(4,128)S(1)}, u32[]{:S(2)}, u32[]{:S(2)}) async-start(f32[32,4,128]{2,1,0:T(4,128)} %bitcast.3), calls=%async_computation | async-start | bytes 131072 | tf_op jit(solution)/shard_map/all_to_all | solution.py:663
  19.7 1.6 %collective-permute-done.6.refs_0_ = f32[3,136,128]{2,1,0:T(8,128)S(1)} collective-permute-done((f32[3,136,128]{2,1,0:T(8,128)S(1)}, f32[3,136,128]{2,1,0:T(8,128)S(1)}, u32[]{:S(2)}, u32[]{:S(2)}) %collective-permute-start.6) | collective-permute-done | bytes 208928 | tf_op jit(solution)/shard_map/ppermute | solution.py:621
  21.3 0.0 collective-permute-start.10
  21.3 0.5 %collective-permute-start.11 = (f32[3,136,128]{2,1,0:T(8,128)S(1)}, f32[3,136,128]{2,1,0:T(8,128)S(1)}, u32[]{:S(2)}, u32[]{:S(2)}) collective-permute-start(f32[3,136,128]{2,1,0:T(8,128)S(1)} %get-tuple-element.26.own_next), channel_id=1, source_target_pairs={{0,1},{1,0},{2,3},{3,2},{4,5},{5,4},{6,7},{7,6},{8,9},{9,8},{10,11... | collective-permute-start | bytes 626696 | tf_op jit(solution)/shard_map/ppermute | solution.py:662
  21.8 2.4 %first_stage.1 = (f32[4,128,128]{2,1,0:T(8,128)S(1)}, f32[4,128,128]{2,1,0:T(8,128)S(1)}, f32[8,2,16,128]{3,2,1,0:T(8,128)S(1)}, f32[8,2,16,128]{3,2,1,0:T(8,128)S(1)}, f32[8,16,128]{2,1,0:T(8,128)S(1)}) custom-call(f32[8,128,128]{2,1,0:T(8,128)S(1)} %bitcast.19, f32[8,2,16,128]{3,2,1,0:T(8,128)S(1)} %collective-permute-done.after, ...), custom_call_target="tpu_custom_call" | custom-call | flops 10000000000 | bytes 1000 | tf_op jit(solution)/shard_map/first_stage/pallas_call | solution.py:640
  24.3 0.0 copy-start.6
  24.3 0.7 %copy-done.6 = f32[4,128,128]{2,1,0:T(8,128)} copy-done((f32[4,128,128]{2,1,0:T(8,128)}, f32[4,128,128]{2,1,0:T(8,128)S(1)}, u32[]{:S(2)}) %copy-start.6) | copy-done | bytes 262168
  25.0 4.0 %collective-permute-start.3 = (f32[8,2,16,128]{3,2,1,0:T(8,128)S(1)}, f32[8,2,16,128]{3,2,1,0:T(8,128)S(1)}, u32[]{:S(2)}, u32[]{:S(2)}) collective-permute-start(f32[8,2,16,128]{3,2,1,0:T(8,128)S(1)} %get-tuple-element.20), channel_id=1, source_target_pairs={{2,4},{4,2},{6,8},{8,6},{10,12},{12,10},{14,16},{16,14},{18,20},{2... | collective-permute-start | bytes 393224 | tf_op jit(solution)/shard_map/ppermute | solution.py:550
  28.9 0.5 %collective-permute-start.4 = (f32[8,2,16,128]{3,2,1,0:T(8,128)S(1)}, f32[8,2,16,128]{3,2,1,0:T(8,128)S(1)}, u32[]{:S(2)}, u32[]{:S(2)}) collective-permute-start(f32[8,2,16,128]{3,2,1,0:T(8,128)S(1)} %get-tuple-element.21), channel_id=1, source_target_pairs={{0,2},{2,0},{4,6},{6,4},{8,10},{10,8},{12,14},{14,12},{16,18},{18,... | collective-permute-start | bytes 393224 | tf_op jit(solution)/shard_map/ppermute | solution.py:551
  29.5 2.6 %sweeps.1 = (f32[8,128]{1,0:T(8,128)}, f32[32,128]{1,0:T(8,128)}) custom-call(f32[128,128]{1,0:T(8,128)S(1)} %bitcast.25, f32[8,128,128]{2,1,0:T(8,128)S(1)} %bitcast.15, f32[4,8,128]{2,1,0:T(8,128)S(1)} %copy-done.5, f32[3,136,128]{2,1,0:T(8,128)S(1)} %get-tuple-element.25.own_pair, f32[3,136,128]{2,1,0:T(8,128)S(1)} %get-tuple-element.26.own_next, ...), custom_call_target="tpu_custom_call" | custom-call | flops 10000000000 | bytes 1000 | tf_op jit(solution)/shard_map/sweeps/pallas_call | solution.py:664
  32.1 3.3 %all-to-all-start.1 = ((f32[32,1,128]{2,1,0:T(1,128)}), f32[32,1,128]{2,1,0:T(1,128)S(1)}, u32[]{:S(2)}, u32[]{:S(2)}) async-start(f32[32,1,128]{2,1,0:T(1,128)} %bitcast.7), calls=%async_computation.1 | async-start | bytes 32768 | tf_op jit(solution)/shard_map/all_to_all | solution.py:677
  35.5 0.2 collective-permute-done.4.pair
  35.6 0.9 %copy-done.7 = f32[4,128,128]{2,1,0:T(8,128)S(1)} copy-done((f32[4,128,128]{2,1,0:T(8,128)S(1)}, f32[4,128,128]{2,1,0:T(8,128)}, u32[]{:S(2)}) %copy-start.7) | copy-done | bytes 262168
  36.6 3.3 %second_stage.1 = f32[8,128,128]{2,1,0:T(8,128)} custom-call(f32[8,2,16,128]{3,2,1,0:T(8,128)S(1)} %collective-permute-done.3.after, f32[8,2,16,128]{3,2,1,0:T(8,128)S(1)} %collective-permute-done.4.pair, f32[8,16,128]{2,1,0:T(8,128)S(1)} %collective-permute-done.5.edge, f32[8,128,128]{2,1,0:T(8,128)S(1)} %bitcast.20, f32[32,128]{1,0:T(8,128)} %get-tuple-element.27._, ...), custom_call_target="tpu_custom_call" | custom-call | flops 10000000000 | bytes 1000 | tf_op jit(solution)/shard_map/second_stage/pallas_call | solution.py:681
  39.9 2.6 %all-to-all-done.1 = f32[32,1,128]{2,1,0:T(1,128)S(1)} async-done(((f32[32,1,128]{2,1,0:T(1,128)}), f32[32,1,128]{2,1,0:T(1,128)S(1)}, u32[]{:S(2)}, u32[]{:S(2)}) %all-to-all-start.1) | async-done | bytes 16416 | tf_op jit(solution)/shard_map/all_to_all | solution.py:677
  42.5 1.0 %gather.1 = f32[128,128]{1,0:T(8,128)} custom-call(f32[32,128]{1,0:T(8,128)S(1)} %bitcast.24, s32[128,128]{1,0:T(8,128)S(1)} %bitcast.23), custom_call_target="tpu_custom_call" | custom-call | flops 1000 | bytes 1000 | tf_op jit(solution)/shard_map/gather/pallas_call | solution.py:690
  (21 shorter events, 0.1 us)
Async XLA Ops:
  0.6 8.2 %copy-start = (f32[8,1,128,128]{3,2,1,0:T(8,128)S(1)}, f32[8,1,128,128]{3,2,1,0:T(8,128)}, u32[]{:S(2)}) copy-start(f32[8,1,128,128]{3,2,1,0:T(8,128)} %param.7) | copy-start | bytes 1572868
  0.6 1.1 %copy-start.1 = (f32[8,16,8,128]{3,2,1,0:T(8,128)S(1)}, f32[8,16,8,128]{3,2,1,0:T(8,128)}, u32[]{:S(2)}) copy-start(f32[8,16,8,128]{3,2,1,0:T(8,128)} %param.4) | copy-start | bytes 1572868
  1.7 10.9 %copy-start.2 = (f32[8,16,8,128]{3,2,1,0:T(8,128)S(1)}, f32[8,16,8,128]{3,2,1,0:T(8,128)}, u32[]{:S(2)}) copy-start(f32[8,16,8,128]{3,2,1,0:T(8,128)} %param.4) | copy-start | bytes 1572868
  1.8 11.9 %collective-permute-start = (f32[8,2,16,128]{3,2,1,0:T(8,128)S(1)}, f32[8,2,16,128]{3,2,1,0:T(8,128)S(1)}, u32[]{:S(2)}, u32[]{:S(2)}) collective-permute-start(f32[8,2,16,128]{3,2,1,0:T(8,128)S(1)} %get-tuple-element.17), channel_id=1, source_target_pairs={{2,4},{4,2},{6,8},{8,6},{10,12},{12,10},{14,16},{16,14},{18,20},{2... | collective-permute-start | bytes 393224 | tf_op jit(solution)/shard_map/ppermute | solution.py:550
  8.8 5.8 %collective-permute-start.1 = (f32[8,2,16,128]{3,2,1,0:T(8,128)S(1)}, f32[8,2,16,128]{3,2,1,0:T(8,128)S(1)}, u32[]{:S(2)}, u32[]{:S(2)}) collective-permute-start(f32[8,2,16,128]{3,2,1,0:T(8,128)S(1)} %get-tuple-element.18), channel_id=1, source_target_pairs={{0,2},{2,0},{4,6},{6,4},{8,10},{10,8},{12,14},{14,12},{16,18},{18,... | collective-permute-start | bytes 393224 | tf_op jit(solution)/shard_map/ppermute | solution.py:551
  8.8 3.5 %collective-permute-start.2 = (f32[8,16,128]{2,1,0:T(8,128)S(1)}, f32[8,16,128]{2,1,0:T(8,128)S(1)}, u32[]{:S(2)}, u32[]{:S(2)}) collective-permute-start(f32[8,16,128]{2,1,0:T(8,128)S(1)} %get-tuple-element.19._), channel_id=1, source_target_pairs={{0,1},{1,0},{2,3},{3,2},{4,5},{5,4},{6,7},{7,6},{8,9},{9,8},{10,11... | collective-permute-start | bytes 196616 | tf_op jit(solution)/shard_map/ppermute | solution.py:552
  8.8 0.7 %copy-start.4 = (f32[4,8,128]{2,1,0:T(8,128)S(1)}, f32[4,8,128]{2,1,0:T(8,128)}, u32[]{:S(2)}) copy-start(f32[4,8,128]{2,1,0:T(8,128)} %own_conductance.1) | copy-start | bytes 49156
  9.5 3.1 %copy-start.3 = (s32[16,8,128]{2,1,0:T(8,128)S(1)}, s32[16,8,128]{2,1,0:T(8,128)}, u32[]{:S(2)}) copy-start(s32[16,8,128]{2,1,0:T(8,128)} %param.5) | copy-start | bytes 196612
  9.6 11.7 %collective-permute-start.6 = (f32[3,136,128]{2,1,0:T(8,128)S(1)}, f32[3,136,128]{2,1,0:T(8,128)S(1)}, u32[]{:S(2)}, u32[]{:S(2)}) collective-permute-start(f32[3,136,128]{2,1,0:T(8,128)S(1)} %get-tuple-element.23), channel_id=1, source_target_pairs={{0,2},{2,0},{4,6},{6,4},{8,10},{10,8},{12,14},{14,12},{16,18},{18,... | collective-permute-start | bytes 626696 | tf_op jit(solution)/shard_map/ppermute | solution.py:621
  11.7 9.7 %collective-permute-start.7 = (f32[3,136,128]{2,1,0:T(8,128)S(1)}, f32[3,136,128]{2,1,0:T(8,128)S(1)}, u32[]{:S(2)}, u32[]{:S(2)}) collective-permute-start(f32[3,136,128]{2,1,0:T(8,128)S(1)} %get-tuple-element.24), channel_id=1, source_target_pairs={{2,4},{4,2},{6,8},{8,6},{10,12},{12,10},{14,16},{16,14},{18,20},{2... | collective-permute-start | bytes 626696 | tf_op jit(solution)/shard_map/ppermute | solution.py:622
  12.3 17.2 %collective-permute-start.8 = (f32[8,128,128]{2,1,0:T(8,128)S(1)}, f32[8,128,128]{2,1,0:T(8,128)S(1)}, u32[]{:S(2)}, u32[]{:S(2)}) collective-permute-start(f32[8,128,128]{2,1,0:T(8,128)S(1)} %bitcast.12), channel_id=1, source_target_pairs={{0,1},{1,0},{2,3},{3,2},{4,5},{5,4},{6,7},{7,6},{8,9},{9,8},{10,11... | collective-permute-start | bytes 1572872 | tf_op jit(solution)/shard_map/ppermute | solution.py:662
  12.6 1.1 %copy-start.5 = (f32[4,8,128]{2,1,0:T(8,128)S(1)}, f32[4,8,128]{2,1,0:T(8,128)}, u32[]{:S(2)}) copy-start(f32[4,8,128]{2,1,0:T(8,128)} %own_conductance.1) | copy-start | bytes 49156
  13.8 15.2 %collective-permute-start.9 = (f32[4,8,128]{2,1,0:T(8,128)S(1)}, f32[4,8,128]{2,1,0:T(8,128)S(1)}, u32[]{:S(2)}, u32[]{:S(2)}) collective-permute-start(f32[4,8,128]{2,1,0:T(8,128)S(1)} %copy-done.5), channel_id=1, source_target_pairs={{0,1},{1,0},{2,3},{3,2},{4,5},{5,4},{6,7},{7,6},{8,9},{9,8},{10,11... | collective-permute-start | bytes 49160 | tf_op jit(solution)/shard_map/ppermute | solution.py:662
  15.7 13.7 %all-to-all-start = ((f32[32,4,128]{2,1,0:T(4,128)}), f32[32,4,128]{2,1,0:T(4,128)S(1)}, u32[]{:S(2)}, u32[]{:S(2)}) async-start(f32[32,4,128]{2,1,0:T(4,128)} %bitcast.3), calls=%async_computation | async-start | bytes 131072 | tf_op jit(solution)/shard_map/all_to_all | solution.py:663
  21.3 8.2 %collective-permute-start.10 = (f32[3,136,128]{2,1,0:T(8,128)S(1)}, f32[3,136,128]{2,1,0:T(8,128)S(1)}, u32[]{:S(2)}, u32[]{:S(2)}) collective-permute-start(f32[3,136,128]{2,1,0:T(8,128)S(1)} %get-tuple-element.25.own_pair), channel_id=1, source_target_pairs={{0,1},{1,0},{2,3},{3,2},{4,5},{5,4},{6,7},{7,6},{8,9},{9,8},{10,11... | collective-permute-start | bytes 626696 | tf_op jit(solution)/shard_map/ppermute | solution.py:662
  21.3 8.2 %collective-permute-start.11 = (f32[3,136,128]{2,1,0:T(8,128)S(1)}, f32[3,136,128]{2,1,0:T(8,128)S(1)}, u32[]{:S(2)}, u32[]{:S(2)}) collective-permute-start(f32[3,136,128]{2,1,0:T(8,128)S(1)} %get-tuple-element.26.own_next), channel_id=1, source_target_pairs={{0,1},{1,0},{2,3},{3,2},{4,5},{5,4},{6,7},{7,6},{8,9},{9,8},{10,11... | collective-permute-start | bytes 626696 | tf_op jit(solution)/shard_map/ppermute | solution.py:662
  24.3 0.7 %copy-start.6 = (f32[4,128,128]{2,1,0:T(8,128)}, f32[4,128,128]{2,1,0:T(8,128)S(1)}, u32[]{:S(2)}) copy-start(f32[4,128,128]{2,1,0:T(8,128)S(1)} %get-tuple-element.29.refs_1_) | copy-start | bytes 786436
  25.0 10.5 %collective-permute-start.3 = (f32[8,2,16,128]{3,2,1,0:T(8,128)S(1)}, f32[8,2,16,128]{3,2,1,0:T(8,128)S(1)}, u32[]{:S(2)}, u32[]{:S(2)}) collective-permute-start(f32[8,2,16,128]{3,2,1,0:T(8,128)S(1)} %get-tuple-element.20), channel_id=1, source_target_pairs={{2,4},{4,2},{6,8},{8,6},{10,12},{12,10},{14,16},{16,14},{18,20},{2... | collective-permute-start | bytes 393224 | tf_op jit(solution)/shard_map/ppermute | solution.py:550
  28.9 6.7 %collective-permute-start.4 = (f32[8,2,16,128]{3,2,1,0:T(8,128)S(1)}, f32[8,2,16,128]{3,2,1,0:T(8,128)S(1)}, u32[]{:S(2)}, u32[]{:S(2)}) collective-permute-start(f32[8,2,16,128]{3,2,1,0:T(8,128)S(1)} %get-tuple-element.21), channel_id=1, source_target_pairs={{0,2},{2,0},{4,6},{6,4},{8,10},{10,8},{12,14},{14,12},{16,18},{18,... | collective-permute-start | bytes 393224 | tf_op jit(solution)/shard_map/ppermute | solution.py:551
  29.5 6.0 %collective-permute-start.5 = (f32[8,16,128]{2,1,0:T(8,128)S(1)}, f32[8,16,128]{2,1,0:T(8,128)S(1)}, u32[]{:S(2)}, u32[]{:S(2)}) collective-permute-start(f32[8,16,128]{2,1,0:T(8,128)S(1)} %get-tuple-element.22._), channel_id=1, source_target_pairs={{0,1},{1,0},{2,3},{3,2},{4,5},{5,4},{6,7},{7,6},{8,9},{9,8},{10,11... | collective-permute-start | bytes 196616 | tf_op jit(solution)/shard_map/ppermute | solution.py:552
  32.1 10.4 %all-to-all-start.1 = ((f32[32,1,128]{2,1,0:T(1,128)}), f32[32,1,128]{2,1,0:T(1,128)S(1)}, u32[]{:S(2)}, u32[]{:S(2)}) async-start(f32[32,1,128]{2,1,0:T(1,128)} %bitcast.7), calls=%async_computation.1 | async-start | bytes 32768 | tf_op jit(solution)/shard_map/all_to_all | solution.py:677
  35.6 1.0 %copy-start.7 = (f32[4,128,128]{2,1,0:T(8,128)S(1)}, f32[4,128,128]{2,1,0:T(8,128)}, u32[]{:S(2)}) copy-start(f32[4,128,128]{2,1,0:T(8,128)} %copy-done.6) | copy-start | bytes 786436

commit v6 on v5

--- a/solution.py
+++ b/solution.py
@@ -14,7 +14,7 @@
 TINY = 1e-37
 LANES = 128
 SPLIT = 2
-UNROLL = (8, 8, 8)
+UNROLL = (16, 8, 8)
 SUB = 8
 PARTS = 3
 SUM_PARTS, MXU_EVERY = 2, 3

time: 43.8 us -> 43.8 us (level)
  no operation moved by 1% of the time
where the time goes in v6:
time: 43.8 us; the launch traced here: 43.5 us
  starting transfers between devices  22.7 us (52%)
  Pallas kernels  11.6 us (26%)
  waiting for transfers between devices  4.97 us (11%)
  local copies, waits for them, and re-layouts  3.48 us (8%)
  between operations  0.77 us (2%)
    ppermute x2, starting transfers between devices, exchange_halos(): lax.ppermute(after, 'shell', pairs(1, True))  11 us
    all_to_all x1, starting transfers between devices, body(): lax.all_to_all(sums, ('shell', 'radial'), split_axis=0, concat_axis=0, ti...  3.97 us
    unnamed x16, local copies, waits for them, and re-layouts  3.48 us
    all_to_all x1, starting transfers between devices, body(): lax.all_to_all(spread, ('shell', 'radial'), split_axis=0, concat_axis=0,...  3.32 us
    pallas_call x1, Pallas kernels, body(): call(functools.partial(second_stage_kernel, layers), shape_of(fields, cel...  3.2 us
    all_to_all x1, waiting for transfers between devices, body(): lax.all_to_all(spread, ('shell', 'radial'), split_axis=0, concat_axis=0,...  2.71 us
    pallas_call x1, Pallas kernels, body(): call(functools.partial(sweep_kernel, width), [shape_of(own_rows, half), s...  2.61 us
    pallas_call x1, Pallas kernels, body(): call(functools.partial(first_stage_kernel, layers), [shape_of(fields // S...  2.36 us
  transfers between devices with their start and end apart: 14, of which 4 were waited for; matrix products, arithmetic and copies ran while one was open for 0% of the time, Pallas kernels for 24%

profile of v6, /device:TPU:0, one launch (start us, length us, event | category | flops | bytes accessed | tf_op | source)
XLA Modules:
  0.0 43.5 jit_solution(11389971725269601467)
XLA Ops:
  0.6 1.1 %copy-done.1 = f32[8,16,8,128]{3,2,1,0:T(8,128)S(1)} copy-done((f32[8,16,8,128]{3,2,1,0:T(8,128)S(1)}, f32[8,16,8,128]{3,2,1,0:T(8,128)}, u32[]{:S(2)}) %copy-start.1) | copy-done | bytes 524312
  1.7 0.1 pack.1
  1.8 7.0 %collective-permute-start = (f32[8,2,16,128]{3,2,1,0:T(8,128)S(1)}, f32[8,2,16,128]{3,2,1,0:T(8,128)S(1)}, u32[]{:S(2)}, u32[]{:S(2)}) collective-permute-start(f32[8,2,16,128]{3,2,1,0:T(8,128)S(1)} %get-tuple-element.17), channel_id=1, source_target_pairs={{2,4},{4,2},{6,8},{8,6},{10,12},{12,10},{14,16},{16,14},{18,20},{2... | collective-permute-start | bytes 393224 | tf_op jit(solution)/shard_map/ppermute | solution.py:550
  8.8 0.0 collective-permute-start.1
  8.8 0.0 collective-permute-start.2
  8.8 0.0 copy-start.4
  8.8 0.7 %copy-done.4 = f32[4,8,128]{2,1,0:T(8,128)S(1)} copy-done((f32[4,8,128]{2,1,0:T(8,128)S(1)}, f32[4,8,128]{2,1,0:T(8,128)}, u32[]{:S(2)}) %copy-start.4) | copy-done | bytes 16408
  9.6 2.1 %collective-permute-start.6 = (f32[3,136,128]{2,1,0:T(8,128)S(1)}, f32[3,136,128]{2,1,0:T(8,128)S(1)}, u32[]{:S(2)}, u32[]{:S(2)}) collective-permute-start(f32[3,136,128]{2,1,0:T(8,128)S(1)} %get-tuple-element.23), channel_id=1, source_target_pairs={{0,2},{2,0},{4,6},{6,4},{8,10},{10,8},{12,14},{14,12},{16,18},{18,... | collective-permute-start | bytes 626696 | tf_op jit(solution)/shard_map/ppermute | solution.py:621
  11.7 0.7 %collective-permute-start.7 = (f32[3,136,128]{2,1,0:T(8,128)S(1)}, f32[3,136,128]{2,1,0:T(8,128)S(1)}, u32[]{:S(2)}, u32[]{:S(2)}) collective-permute-start(f32[3,136,128]{2,1,0:T(8,128)S(1)} %get-tuple-element.24), channel_id=1, source_target_pairs={{2,4},{4,2},{6,8},{8,6},{10,12},{12,10},{14,16},{16,14},{18,20},{2... | collective-permute-start | bytes 626696 | tf_op jit(solution)/shard_map/ppermute | solution.py:622
  12.3 0.3 collective-permute-start.8
  12.6 1.1 %inner_currents.1.inner_ref = f32[16,128]{1,0:T(8,128)S(1)} custom-call(f32[8,128,128]{2,1,0:T(8,128)S(1)} %bitcast.17, f32[8,16,128]{2,1,0:T(8,128)S(1)} %collective-permute-done.2.edge, s32[128,128]{1,0:T(8,128)S(1)} %bitcast.21, f32[8,128,128]{2,1,0:T(8,128)S(1)} %bitcast.13), custom_call_target="tpu_custom_call" | custom-call | flops 1000 | bytes 1000 | tf_op jit(solution)/shard_map/inner_currents/pallas_call | solution.py:627
  13.7 0.0 collective-permute-done.after
  13.7 0.0 copy-done.5
  13.8 0.3 collective-permute-start.9
  14.1 0.4 %collective-permute-done.1.pair = f32[8,2,16,128]{3,2,1,0:T(8,128)S(1)} collective-permute-done((f32[8,2,16,128]{3,2,1,0:T(8,128)S(1)}, f32[8,2,16,128]{3,2,1,0:T(8,128)S(1)}, u32[]{:S(2)}, u32[]{:S(2)}) %collective-permute-start.1) | collective-permute-done | bytes 131104 | tf_op jit(solution)/shard_map/ppermute | solution.py:551
  14.6 1.2 %outer_currents.1._.refs_2_ = f32[128,128]{1,0:T(8,128)} custom-call(f32[8,128,128]{2,1,0:T(8,128)S(1)} %bitcast.18, f32[8,2,16,128]{3,2,1,0:T(8,128)S(1)} %collective-permute-done.after, f32[8,2,16,128]{3,2,1,0:T(8,128)S(1)} %collective-permute-done.1.pair, f32[8,16,128]{2,1,0:T(8,128)S(1)} %collective-permute-done.2.edge, s32[128,128]{1,0:T(8,128)S(1)} %bitcast.22, ...), custom_call_target="tpu_custom_call" | custom-call | flops 2000000000 | bytes 1000 | tf_op jit(solution)/shard_map/outer_currents/pallas_call | solution.py:631
  15.7 4.0 %all-to-all-start = ((f32[32,4,128]{2,1,0:T(4,128)}), f32[32,4,128]{2,1,0:T(4,128)S(1)}, u32[]{:S(2)}, u32[]{:S(2)}) async-start(f32[32,4,128]{2,1,0:T(4,128)} %bitcast.3), calls=%async_computation | async-start | bytes 131072 | tf_op jit(solution)/shard_map/all_to_all | solution.py:663
  19.7 1.6 %collective-permute-done.6.refs_0_ = f32[3,136,128]{2,1,0:T(8,128)S(1)} collective-permute-done((f32[3,136,128]{2,1,0:T(8,128)S(1)}, f32[3,136,128]{2,1,0:T(8,128)S(1)}, u32[]{:S(2)}, u32[]{:S(2)}) %collective-permute-start.6) | collective-permute-done | bytes 208928 | tf_op jit(solution)/shard_map/ppermute | solution.py:621
  21.3 0.0 collective-permute-start.10
  21.3 0.5 %collective-permute-start.11 = (f32[3,136,128]{2,1,0:T(8,128)S(1)}, f32[3,136,128]{2,1,0:T(8,128)S(1)}, u32[]{:S(2)}, u32[]{:S(2)}) collective-permute-start(f32[3,136,128]{2,1,0:T(8,128)S(1)} %get-tuple-element.26.own_next), channel_id=1, source_target_pairs={{0,1},{1,0},{2,3},{3,2},{4,5},{5,4},{6,7},{7,6},{8,9},{9,8},{10,11... | collective-permute-start | bytes 626696 | tf_op jit(solution)/shard_map/ppermute | solution.py:662
  21.8 2.4 %first_stage.1 = (f32[4,128,128]{2,1,0:T(8,128)S(1)}, f32[4,128,128]{2,1,0:T(8,128)S(1)}, f32[8,2,16,128]{3,2,1,0:T(8,128)S(1)}, f32[8,2,16,128]{3,2,1,0:T(8,128)S(1)}, f32[8,16,128]{2,1,0:T(8,128)S(1)}) custom-call(f32[8,128,128]{2,1,0:T(8,128)S(1)} %bitcast.19, f32[8,2,16,128]{3,2,1,0:T(8,128)S(1)} %collective-permute-done.after, ...), custom_call_target="tpu_custom_call" | custom-call | flops 10000000000 | bytes 1000 | tf_op jit(solution)/shard_map/first_stage/pallas_call | solution.py:640
  24.2 0.0 copy-start.6
  24.2 0.7 %copy-done.6 = f32[4,128,128]{2,1,0:T(8,128)} copy-done((f32[4,128,128]{2,1,0:T(8,128)}, f32[4,128,128]{2,1,0:T(8,128)S(1)}, u32[]{:S(2)}) %copy-start.6) | copy-done | bytes 262168
  24.9 4.0 %collective-permute-start.3 = (f32[8,2,16,128]{3,2,1,0:T(8,128)S(1)}, f32[8,2,16,128]{3,2,1,0:T(8,128)S(1)}, u32[]{:S(2)}, u32[]{:S(2)}) collective-permute-start(f32[8,2,16,128]{3,2,1,0:T(8,128)S(1)} %get-tuple-element.20), channel_id=1, source_target_pairs={{2,4},{4,2},{6,8},{8,6},{10,12},{12,10},{14,16},{16,14},{18,20},{2... | collective-permute-start | bytes 393224 | tf_op jit(solution)/shard_map/ppermute | solution.py:550
  28.9 0.5 %collective-permute-start.4 = (f32[8,2,16,128]{3,2,1,0:T(8,128)S(1)}, f32[8,2,16,128]{3,2,1,0:T(8,128)S(1)}, u32[]{:S(2)}, u32[]{:S(2)}) collective-permute-start(f32[8,2,16,128]{3,2,1,0:T(8,128)S(1)} %get-tuple-element.21), channel_id=1, source_target_pairs={{0,2},{2,0},{4,6},{6,4},{8,10},{10,8},{12,14},{14,12},{16,18},{18,... | collective-permute-start | bytes 393224 | tf_op jit(solution)/shard_map/ppermute | solution.py:551
  29.4 2.6 %sweeps.1 = (f32[8,128]{1,0:T(8,128)}, f32[32,128]{1,0:T(8,128)}) custom-call(f32[128,128]{1,0:T(8,128)S(1)} %bitcast.25, f32[8,128,128]{2,1,0:T(8,128)S(1)} %bitcast.15, f32[4,8,128]{2,1,0:T(8,128)S(1)} %copy-done.5, f32[3,136,128]{2,1,0:T(8,128)S(1)} %get-tuple-element.25.own_pair, f32[3,136,128]{2,1,0:T(8,128)S(1)} %get-tuple-element.26.own_next, ...), custom_call_target="tpu_custom_call" | custom-call | flops 10000000000 | bytes 1000 | tf_op jit(solution)/shard_map/sweeps/pallas_call | solution.py:664
  32.0 3.3 %all-to-all-start.1 = ((f32[32,1,128]{2,1,0:T(1,128)}), f32[32,1,128]{2,1,0:T(1,128)S(1)}, u32[]{:S(2)}, u32[]{:S(2)}) async-start(f32[32,1,128]{2,1,0:T(1,128)} %bitcast.7), calls=%async_computation.1 | async-start | bytes 32768 | tf_op jit(solution)/shard_map/all_to_all | solution.py:677
  35.4 0.2 collective-permute-done.4.pair
  35.6 0.9 %copy-done.7 = f32[4,128,128]{2,1,0:T(8,128)S(1)} copy-done((f32[4,128,128]{2,1,0:T(8,128)S(1)}, f32[4,128,128]{2,1,0:T(8,128)}, u32[]{:S(2)}) %copy-start.7) | copy-done | bytes 262168
  36.5 3.2 %second_stage.1 = f32[8,128,128]{2,1,0:T(8,128)} custom-call(f32[8,2,16,128]{3,2,1,0:T(8,128)S(1)} %collective-permute-done.3.after, f32[8,2,16,128]{3,2,1,0:T(8,128)S(1)} %collective-permute-done.4.pair, f32[8,16,128]{2,1,0:T(8,128)S(1)} %collective-permute-done.5.edge, f32[8,128,128]{2,1,0:T(8,128)S(1)} %bitcast.20, f32[32,128]{1,0:T(8,128)} %get-tuple-element.27._, ...), custom_call_target="tpu_custom_call" | custom-call | flops 10000000000 | bytes 1000 | tf_op jit(solution)/shard_map/second_stage/pallas_call | solution.py:681
  39.7 2.7 %all-to-all-done.1 = f32[32,1,128]{2,1,0:T(1,128)S(1)} async-done(((f32[32,1,128]{2,1,0:T(1,128)}), f32[32,1,128]{2,1,0:T(1,128)S(1)}, u32[]{:S(2)}, u32[]{:S(2)}) %all-to-all-start.1) | async-done | bytes 16416 | tf_op jit(solution)/shard_map/all_to_all | solution.py:677
  42.4 1.0 %gather.1 = f32[128,128]{1,0:T(8,128)} custom-call(f32[32,128]{1,0:T(8,128)S(1)} %bitcast.24, s32[128,128]{1,0:T(8,128)S(1)} %bitcast.23), custom_call_target="tpu_custom_call" | custom-call | flops 1000 | bytes 1000 | tf_op jit(solution)/shard_map/gather/pallas_call | solution.py:690
  (21 shorter events, 0.1 us)
Async XLA Ops:
  0.6 8.2 %copy-start = (f32[8,1,128,128]{3,2,1,0:T(8,128)S(1)}, f32[8,1,128,128]{3,2,1,0:T(8,128)}, u32[]{:S(2)}) copy-start(f32[8,1,128,128]{3,2,1,0:T(8,128)} %param.7) | copy-start | bytes 1572868
  0.6 1.1 %copy-start.1 = (f32[8,16,8,128]{3,2,1,0:T(8,128)S(1)}, f32[8,16,8,128]{3,2,1,0:T(8,128)}, u32[]{:S(2)}) copy-start(f32[8,16,8,128]{3,2,1,0:T(8,128)} %param.4) | copy-start | bytes 1572868
  1.7 10.9 %copy-start.2 = (f32[8,16,8,128]{3,2,1,0:T(8,128)S(1)}, f32[8,16,8,128]{3,2,1,0:T(8,128)}, u32[]{:S(2)}) copy-start(f32[8,16,8,128]{3,2,1,0:T(8,128)} %param.4) | copy-start | bytes 1572868
  1.8 11.9 %collective-permute-start = (f32[8,2,16,128]{3,2,1,0:T(8,128)S(1)}, f32[8,2,16,128]{3,2,1,0:T(8,128)S(1)}, u32[]{:S(2)}, u32[]{:S(2)}) collective-permute-start(f32[8,2,16,128]{3,2,1,0:T(8,128)S(1)} %get-tuple-element.17), channel_id=1, source_target_pairs={{2,4},{4,2},{6,8},{8,6},{10,12},{12,10},{14,16},{16,14},{18,20},{2... | collective-permute-start | bytes 393224 | tf_op jit(solution)/shard_map/ppermute | solution.py:550
  8.8 5.8 %collective-permute-start.1 = (f32[8,2,16,128]{3,2,1,0:T(8,128)S(1)}, f32[8,2,16,128]{3,2,1,0:T(8,128)S(1)}, u32[]{:S(2)}, u32[]{:S(2)}) collective-permute-start(f32[8,2,16,128]{3,2,1,0:T(8,128)S(1)} %get-tuple-element.18), channel_id=1, source_target_pairs={{0,2},{2,0},{4,6},{6,4},{8,10},{10,8},{12,14},{14,12},{16,18},{18,... | collective-permute-start | bytes 393224 | tf_op jit(solution)/shard_map/ppermute | solution.py:551
  8.8 3.5 %collective-permute-start.2 = (f32[8,16,128]{2,1,0:T(8,128)S(1)}, f32[8,16,128]{2,1,0:T(8,128)S(1)}, u32[]{:S(2)}, u32[]{:S(2)}) collective-permute-start(f32[8,16,128]{2,1,0:T(8,128)S(1)} %get-tuple-element.19._), channel_id=1, source_target_pairs={{0,1},{1,0},{2,3},{3,2},{4,5},{5,4},{6,7},{7,6},{8,9},{9,8},{10,11... | collective-permute-start | bytes 196616 | tf_op jit(solution)/shard_map/ppermute | solution.py:552
  8.8 0.7 %copy-start.4 = (f32[4,8,128]{2,1,0:T(8,128)S(1)}, f32[4,8,128]{2,1,0:T(8,128)}, u32[]{:S(2)}) copy-start(f32[4,8,128]{2,1,0:T(8,128)} %own_conductance.1) | copy-start | bytes 49156
  9.5 3.1 %copy-start.3 = (s32[16,8,128]{2,1,0:T(8,128)S(1)}, s32[16,8,128]{2,1,0:T(8,128)}, u32[]{:S(2)}) copy-start(s32[16,8,128]{2,1,0:T(8,128)} %param.5) | copy-start | bytes 196612
  9.6 11.7 %collective-permute-start.6 = (f32[3,136,128]{2,1,0:T(8,128)S(1)}, f32[3,136,128]{2,1,0:T(8,128)S(1)}, u32[]{:S(2)}, u32[]{:S(2)}) collective-permute-start(f32[3,136,128]{2,1,0:T(8,128)S(1)} %get-tuple-element.23), channel_id=1, source_target_pairs={{0,2},{2,0},{4,6},{6,4},{8,10},{10,8},{12,14},{14,12},{16,18},{18,... | collective-permute-start | bytes 626696 | tf_op jit(solution)/shard_map/ppermute | solution.py:621
  11.7 9.7 %collective-permute-start.7 = (f32[3,136,128]{2,1,0:T(8,128)S(1)}, f32[3,136,128]{2,1,0:T(8,128)S(1)}, u32[]{:S(2)}, u32[]{:S(2)}) collective-permute-start(f32[3,136,128]{2,1,0:T(8,128)S(1)} %get-tuple-element.24), channel_id=1, source_target_pairs={{2,4},{4,2},{6,8},{8,6},{10,12},{12,10},{14,16},{16,14},{18,20},{2... | collective-permute-start | bytes 626696 | tf_op jit(solution)/shard_map/ppermute | solution.py:622
  12.3 17.1 %collective-permute-start.8 = (f32[8,128,128]{2,1,0:T(8,128)S(1)}, f32[8,128,128]{2,1,0:T(8,128)S(1)}, u32[]{:S(2)}, u32[]{:S(2)}) collective-permute-start(f32[8,128,128]{2,1,0:T(8,128)S(1)} %bitcast.12), channel_id=1, source_target_pairs={{0,1},{1,0},{2,3},{3,2},{4,5},{5,4},{6,7},{7,6},{8,9},{9,8},{10,11... | collective-permute-start | bytes 1572872 | tf_op jit(solution)/shard_map/ppermute | solution.py:662
  12.6 1.1 %copy-start.5 = (f32[4,8,128]{2,1,0:T(8,128)S(1)}, f32[4,8,128]{2,1,0:T(8,128)}, u32[]{:S(2)}) copy-start(f32[4,8,128]{2,1,0:T(8,128)} %own_conductance.1) | copy-start | bytes 49156
  13.8 15.1 %collective-permute-start.9 = (f32[4,8,128]{2,1,0:T(8,128)S(1)}, f32[4,8,128]{2,1,0:T(8,128)S(1)}, u32[]{:S(2)}, u32[]{:S(2)}) collective-permute-start(f32[4,8,128]{2,1,0:T(8,128)S(1)} %copy-done.5), channel_id=1, source_target_pairs={{0,1},{1,0},{2,3},{3,2},{4,5},{5,4},{6,7},{7,6},{8,9},{9,8},{10,11... | collective-permute-start | bytes 49160 | tf_op jit(solution)/shard_map/ppermute | solution.py:662
  15.7 13.7 %all-to-all-start = ((f32[32,4,128]{2,1,0:T(4,128)}), f32[32,4,128]{2,1,0:T(4,128)S(1)}, u32[]{:S(2)}, u32[]{:S(2)}) async-start(f32[32,4,128]{2,1,0:T(4,128)} %bitcast.3), calls=%async_computation | async-start | bytes 131072 | tf_op jit(solution)/shard_map/all_to_all | solution.py:663
  21.3 8.1 %collective-permute-start.10 = (f32[3,136,128]{2,1,0:T(8,128)S(1)}, f32[3,136,128]{2,1,0:T(8,128)S(1)}, u32[]{:S(2)}, u32[]{:S(2)}) collective-permute-start(f32[3,136,128]{2,1,0:T(8,128)S(1)} %get-tuple-element.25.own_pair), channel_id=1, source_target_pairs={{0,1},{1,0},{2,3},{3,2},{4,5},{5,4},{6,7},{7,6},{8,9},{9,8},{10,11... | collective-permute-start | bytes 626696 | tf_op jit(solution)/shard_map/ppermute | solution.py:662
  21.3 8.1 %collective-permute-start.11 = (f32[3,136,128]{2,1,0:T(8,128)S(1)}, f32[3,136,128]{2,1,0:T(8,128)S(1)}, u32[]{:S(2)}, u32[]{:S(2)}) collective-permute-start(f32[3,136,128]{2,1,0:T(8,128)S(1)} %get-tuple-element.26.own_next), channel_id=1, source_target_pairs={{0,1},{1,0},{2,3},{3,2},{4,5},{5,4},{6,7},{7,6},{8,9},{9,8},{10,11... | collective-permute-start | bytes 626696 | tf_op jit(solution)/shard_map/ppermute | solution.py:662
  24.2 0.7 %copy-start.6 = (f32[4,128,128]{2,1,0:T(8,128)}, f32[4,128,128]{2,1,0:T(8,128)S(1)}, u32[]{:S(2)}) copy-start(f32[4,128,128]{2,1,0:T(8,128)S(1)} %get-tuple-element.29.refs_1_) | copy-start | bytes 786436
  24.9 10.5 %collective-permute-start.3 = (f32[8,2,16,128]{3,2,1,0:T(8,128)S(1)}, f32[8,2,16,128]{3,2,1,0:T(8,128)S(1)}, u32[]{:S(2)}, u32[]{:S(2)}) collective-permute-start(f32[8,2,16,128]{3,2,1,0:T(8,128)S(1)} %get-tuple-element.20), channel_id=1, source_target_pairs={{2,4},{4,2},{6,8},{8,6},{10,12},{12,10},{14,16},{16,14},{18,20},{2... | collective-permute-start | bytes 393224 | tf_op jit(solution)/shard_map/ppermute | solution.py:550
  28.9 6.7 %collective-permute-start.4 = (f32[8,2,16,128]{3,2,1,0:T(8,128)S(1)}, f32[8,2,16,128]{3,2,1,0:T(8,128)S(1)}, u32[]{:S(2)}, u32[]{:S(2)}) collective-permute-start(f32[8,2,16,128]{3,2,1,0:T(8,128)S(1)} %get-tuple-element.21), channel_id=1, source_target_pairs={{0,2},{2,0},{4,6},{6,4},{8,10},{10,8},{12,14},{14,12},{16,18},{18,... | collective-permute-start | bytes 393224 | tf_op jit(solution)/shard_map/ppermute | solution.py:551
  29.4 6.0 %collective-permute-start.5 = (f32[8,16,128]{2,1,0:T(8,128)S(1)}, f32[8,16,128]{2,1,0:T(8,128)S(1)}, u32[]{:S(2)}, u32[]{:S(2)}) collective-permute-start(f32[8,16,128]{2,1,0:T(8,128)S(1)} %get-tuple-element.22._), channel_id=1, source_target_pairs={{0,1},{1,0},{2,3},{3,2},{4,5},{5,4},{6,7},{7,6},{8,9},{9,8},{10,11... | collective-permute-start | bytes 196616 | tf_op jit(solution)/shard_map/ppermute | solution.py:552
  32.0 10.4 %all-to-all-start.1 = ((f32[32,1,128]{2,1,0:T(1,128)}), f32[32,1,128]{2,1,0:T(1,128)S(1)}, u32[]{:S(2)}, u32[]{:S(2)}) async-start(f32[32,1,128]{2,1,0:T(1,128)} %bitcast.7), calls=%async_computation.1 | async-start | bytes 32768 | tf_op jit(solution)/shard_map/all_to_all | solution.py:677
  35.6 1.0 %copy-start.7 = (f32[4,128,128]{2,1,0:T(8,128)S(1)}, f32[4,128,128]{2,1,0:T(8,128)}, u32[]{:S(2)}) copy-start(f32[4,128,128]{2,1,0:T(8,128)} %copy-done.6) | copy-start | bytes 786436

commit v7 on v6

--- a/solution.py
+++ b/solution.py
@@ -17,7 +17,7 @@
 UNROLL = (16, 8, 8)
 SUB = 8
 PARTS = 3
-SUM_PARTS, MXU_EVERY = 2, 3
+SUM_PARTS, MXU_EVERY = 3, 4
 VMEM_LIMIT = 6 * 1024 * 1024
 CHEAP, CURRENTS, RELAY, DEAR = 1_000, 2_000_000_000, 1_000, 10_000_000_000
 IN_HBM = pl.BlockSpec(memory_space=pltpu.HBM)

time: 43.8 us -> 43.9 us (level)
  no operation moved by 1% of the time
where the time goes in v7:
time: 43.9 us; the launch traced here: 43.6 us
  starting transfers between devices  22.7 us (52%)
  Pallas kernels  11.7 us (27%)
  waiting for transfers between devices  4.97 us (11%)
  local copies, waits for them, and re-layouts  3.48 us (8%)
  between operations  0.77 us (2%)
    ppermute x2, starting transfers between devices, exchange_halos(): lax.ppermute(after, 'shell', pairs(1, True))  11 us
    all_to_all x1, starting transfers between devices, body(): lax.all_to_all(sums, ('shell', 'radial'), split_axis=0, concat_axis=0, ti...  3.97 us
    unnamed x16, local copies, waits for them, and re-layouts  3.48 us
    all_to_all x1, starting transfers between devices, body(): lax.all_to_all(spread, ('shell', 'radial'), split_axis=0, concat_axis=0,...  3.33 us
    pallas_call x1, Pallas kernels, body(): call(functools.partial(second_stage_kernel, layers), shape_of(fields, cel...  3.2 us
    all_to_all x1, waiting for transfers between devices, body(): lax.all_to_all(spread, ('shell', 'radial'), split_axis=0, concat_axis=0,...  2.85 us
    pallas_call x1, Pallas kernels, body(): call(functools.partial(sweep_kernel, width), [shape_of(own_rows, half), s...  2.74 us
    pallas_call x1, Pallas kernels, body(): call(functools.partial(first_stage_kernel, layers), [shape_of(fields // S...  2.36 us
  transfers between devices with their start and end apart: 14, of which 4 were waited for; matrix products, arithmetic and copies ran while one was open for 0% of the time, Pallas kernels for 24%

profile of v7, /device:TPU:0, one launch (start us, length us, event | category | flops | bytes accessed | tf_op | source)
XLA Modules:
  0.0 43.6 jit_solution(14590593529262294079)
XLA Ops:
  0.6 1.1 %copy-done.1 = f32[8,16,8,128]{3,2,1,0:T(8,128)S(1)} copy-done((f32[8,16,8,128]{3,2,1,0:T(8,128)S(1)}, f32[8,16,8,128]{3,2,1,0:T(8,128)}, u32[]{:S(2)}) %copy-start.1) | copy-done | bytes 524312
  1.7 0.1 pack.1
  1.8 7.0 %collective-permute-start = (f32[8,2,16,128]{3,2,1,0:T(8,128)S(1)}, f32[8,2,16,128]{3,2,1,0:T(8,128)S(1)}, u32[]{:S(2)}, u32[]{:S(2)}) collective-permute-start(f32[8,2,16,128]{3,2,1,0:T(8,128)S(1)} %get-tuple-element.17), channel_id=1, source_target_pairs={{2,4},{4,2},{6,8},{8,6},{10,12},{12,10},{14,16},{16,14},{18,20},{2... | collective-permute-start | bytes 393224 | tf_op jit(solution)/shard_map/ppermute | solution.py:550
  8.8 0.0 collective-permute-start.1
  8.8 0.0 collective-permute-start.2
  8.8 0.0 copy-start.4
  8.8 0.7 %copy-done.4 = f32[4,8,128]{2,1,0:T(8,128)S(1)} copy-done((f32[4,8,128]{2,1,0:T(8,128)S(1)}, f32[4,8,128]{2,1,0:T(8,128)}, u32[]{:S(2)}) %copy-start.4) | copy-done | bytes 16408
  9.6 2.1 %collective-permute-start.6 = (f32[3,136,128]{2,1,0:T(8,128)S(1)}, f32[3,136,128]{2,1,0:T(8,128)S(1)}, u32[]{:S(2)}, u32[]{:S(2)}) collective-permute-start(f32[3,136,128]{2,1,0:T(8,128)S(1)} %get-tuple-element.23), channel_id=1, source_target_pairs={{0,2},{2,0},{4,6},{6,4},{8,10},{10,8},{12,14},{14,12},{16,18},{18,... | collective-permute-start | bytes 626696 | tf_op jit(solution)/shard_map/ppermute | solution.py:621
  11.7 0.7 %collective-permute-start.7 = (f32[3,136,128]{2,1,0:T(8,128)S(1)}, f32[3,136,128]{2,1,0:T(8,128)S(1)}, u32[]{:S(2)}, u32[]{:S(2)}) collective-permute-start(f32[3,136,128]{2,1,0:T(8,128)S(1)} %get-tuple-element.24), channel_id=1, source_target_pairs={{2,4},{4,2},{6,8},{8,6},{10,12},{12,10},{14,16},{16,14},{18,20},{2... | collective-permute-start | bytes 626696 | tf_op jit(solution)/shard_map/ppermute | solution.py:622
  12.3 0.3 collective-permute-start.8
  12.6 1.1 %inner_currents.1.inner_ref = f32[16,128]{1,0:T(8,128)S(1)} custom-call(f32[8,128,128]{2,1,0:T(8,128)S(1)} %bitcast.17, f32[8,16,128]{2,1,0:T(8,128)S(1)} %collective-permute-done.2.edge, s32[128,128]{1,0:T(8,128)S(1)} %bitcast.21, f32[8,128,128]{2,1,0:T(8,128)S(1)} %bitcast.13), custom_call_target="tpu_custom_call" | custom-call | flops 1000 | bytes 1000 | tf_op jit(solution)/shard_map/inner_currents/pallas_call | solution.py:627
  13.7 0.0 collective-permute-done.after
  13.7 0.0 copy-done.5
  13.8 0.3 collective-permute-start.9
  14.1 0.4 %collective-permute-done.1.pair = f32[8,2,16,128]{3,2,1,0:T(8,128)S(1)} collective-permute-done((f32[8,2,16,128]{3,2,1,0:T(8,128)S(1)}, f32[8,2,16,128]{3,2,1,0:T(8,128)S(1)}, u32[]{:S(2)}, u32[]{:S(2)}) %collective-permute-start.1) | collective-permute-done | bytes 131104 | tf_op jit(solution)/shard_map/ppermute | solution.py:551
  14.6 1.2 %outer_currents.1._.refs_2_ = f32[128,128]{1,0:T(8,128)} custom-call(f32[8,128,128]{2,1,0:T(8,128)S(1)} %bitcast.18, f32[8,2,16,128]{3,2,1,0:T(8,128)S(1)} %collective-permute-done.after, f32[8,2,16,128]{3,2,1,0:T(8,128)S(1)} %collective-permute-done.1.pair, f32[8,16,128]{2,1,0:T(8,128)S(1)} %collective-permute-done.2.edge, s32[128,128]{1,0:T(8,128)S(1)} %bitcast.22, ...), custom_call_target="tpu_custom_call" | custom-call | flops 2000000000 | bytes 1000 | tf_op jit(solution)/shard_map/outer_currents/pallas_call | solution.py:631
  15.7 4.0 %all-to-all-start = ((f32[32,4,128]{2,1,0:T(4,128)}), f32[32,4,128]{2,1,0:T(4,128)S(1)}, u32[]{:S(2)}, u32[]{:S(2)}) async-start(f32[32,4,128]{2,1,0:T(4,128)} %bitcast.3), calls=%async_computation | async-start | bytes 131072 | tf_op jit(solution)/shard_map/all_to_all | solution.py:663
  19.7 1.6 %collective-permute-done.6.refs_0_ = f32[3,136,128]{2,1,0:T(8,128)S(1)} collective-permute-done((f32[3,136,128]{2,1,0:T(8,128)S(1)}, f32[3,136,128]{2,1,0:T(8,128)S(1)}, u32[]{:S(2)}, u32[]{:S(2)}) %collective-permute-start.6) | collective-permute-done | bytes 208928 | tf_op jit(solution)/shard_map/ppermute | solution.py:621
  21.3 0.0 collective-permute-start.10
  21.3 0.5 %collective-permute-start.11 = (f32[3,136,128]{2,1,0:T(8,128)S(1)}, f32[3,136,128]{2,1,0:T(8,128)S(1)}, u32[]{:S(2)}, u32[]{:S(2)}) collective-permute-start(f32[3,136,128]{2,1,0:T(8,128)S(1)} %get-tuple-element.26.own_next), channel_id=1, source_target_pairs={{0,1},{1,0},{2,3},{3,2},{4,5},{5,4},{6,7},{7,6},{8,9},{9,8},{10,11... | collective-permute-start | bytes 626696 | tf_op jit(solution)/shard_map/ppermute | solution.py:662
  21.8 2.4 %first_stage.1 = (f32[4,128,128]{2,1,0:T(8,128)S(1)}, f32[4,128,128]{2,1,0:T(8,128)S(1)}, f32[8,2,16,128]{3,2,1,0:T(8,128)S(1)}, f32[8,2,16,128]{3,2,1,0:T(8,128)S(1)}, f32[8,16,128]{2,1,0:T(8,128)S(1)}) custom-call(f32[8,128,128]{2,1,0:T(8,128)S(1)} %bitcast.19, f32[8,2,16,128]{3,2,1,0:T(8,128)S(1)} %collective-permute-done.after, ...), custom_call_target="tpu_custom_call" | custom-call | flops 10000000000 | bytes 1000 | tf_op jit(solution)/shard_map/first_stage/pallas_call | solution.py:640
  24.2 0.0 copy-start.6
  24.2 0.7 %copy-done.6 = f32[4,128,128]{2,1,0:T(8,128)} copy-done((f32[4,128,128]{2,1,0:T(8,128)}, f32[4,128,128]{2,1,0:T(8,128)S(1)}, u32[]{:S(2)}) %copy-start.6) | copy-done | bytes 262168
  24.9 4.0 %collective-permute-start.3 = (f32[8,2,16,128]{3,2,1,0:T(8,128)S(1)}, f32[8,2,16,128]{3,2,1,0:T(8,128)S(1)}, u32[]{:S(2)}, u32[]{:S(2)}) collective-permute-start(f32[8,2,16,128]{3,2,1,0:T(8,128)S(1)} %get-tuple-element.20), channel_id=1, source_target_pairs={{2,4},{4,2},{6,8},{8,6},{10,12},{12,10},{14,16},{16,14},{18,20},{2... | collective-permute-start | bytes 393224 | tf_op jit(solution)/shard_map/ppermute | solution.py:550
  28.9 0.5 %collective-permute-start.4 = (f32[8,2,16,128]{3,2,1,0:T(8,128)S(1)}, f32[8,2,16,128]{3,2,1,0:T(8,128)S(1)}, u32[]{:S(2)}, u32[]{:S(2)}) collective-permute-start(f32[8,2,16,128]{3,2,1,0:T(8,128)S(1)} %get-tuple-element.21), channel_id=1, source_target_pairs={{0,2},{2,0},{4,6},{6,4},{8,10},{10,8},{12,14},{14,12},{16,18},{18,... | collective-permute-start | bytes 393224 | tf_op jit(solution)/shard_map/ppermute | solution.py:551
  29.4 2.7 %sweeps.1 = (f32[8,128]{1,0:T(8,128)}, f32[32,128]{1,0:T(8,128)}) custom-call(f32[128,128]{1,0:T(8,128)S(1)} %bitcast.25, f32[8,128,128]{2,1,0:T(8,128)S(1)} %bitcast.15, f32[4,8,128]{2,1,0:T(8,128)S(1)} %copy-done.5, f32[3,136,128]{2,1,0:T(8,128)S(1)} %get-tuple-element.25.own_pair, f32[3,136,128]{2,1,0:T(8,128)S(1)} %get-tuple-element.26.own_next, ...), custom_call_target="tpu_custom_call" | custom-call | flops 10000000000 | bytes 1000 | tf_op jit(solution)/shard_map/sweeps/pallas_call | solution.py:664
  32.2 3.3 %all-to-all-start.1 = ((f32[32,1,128]{2,1,0:T(1,128)}), f32[32,1,128]{2,1,0:T(1,128)S(1)}, u32[]{:S(2)}, u32[]{:S(2)}) async-start(f32[32,1,128]{2,1,0:T(1,128)} %bitcast.7), calls=%async_computation.1 | async-start | bytes 32768 | tf_op jit(solution)/shard_map/all_to_all | solution.py:677
  35.5 0.1 collective-permute-done.4.pair
  35.6 0.9 %copy-done.7 = f32[4,128,128]{2,1,0:T(8,128)S(1)} copy-done((f32[4,128,128]{2,1,0:T(8,128)S(1)}, f32[4,128,128]{2,1,0:T(8,128)}, u32[]{:S(2)}) %copy-start.7) | copy-done | bytes 262168
  36.5 3.2 %second_stage.1 = f32[8,128,128]{2,1,0:T(8,128)} custom-call(f32[8,2,16,128]{3,2,1,0:T(8,128)S(1)} %collective-permute-done.3.after, f32[8,2,16,128]{3,2,1,0:T(8,128)S(1)} %collective-permute-done.4.pair, f32[8,16,128]{2,1,0:T(8,128)S(1)} %collective-permute-done.5.edge, f32[8,128,128]{2,1,0:T(8,128)S(1)} %bitcast.20, f32[32,128]{1,0:T(8,128)} %get-tuple-element.27._, ...), custom_call_target="tpu_custom_call" | custom-call | flops 10000000000 | bytes 1000 | tf_op jit(solution)/shard_map/second_stage/pallas_call | solution.py:681
  39.7 2.8 %all-to-all-done.1 = f32[32,1,128]{2,1,0:T(1,128)S(1)} async-done(((f32[32,1,128]{2,1,0:T(1,128)}), f32[32,1,128]{2,1,0:T(1,128)S(1)}, u32[]{:S(2)}, u32[]{:S(2)}) %all-to-all-start.1) | async-done | bytes 16416 | tf_op jit(solution)/shard_map/all_to_all | solution.py:677
  42.6 1.0 %gather.1 = f32[128,128]{1,0:T(8,128)} custom-call(f32[32,128]{1,0:T(8,128)S(1)} %bitcast.24, s32[128,128]{1,0:T(8,128)S(1)} %bitcast.23), custom_call_target="tpu_custom_call" | custom-call | flops 1000 | bytes 1000 | tf_op jit(solution)/shard_map/gather/pallas_call | solution.py:690
  (21 shorter events, 0.1 us)
Async XLA Ops:
  0.6 8.2 %copy-start = (f32[8,1,128,128]{3,2,1,0:T(8,128)S(1)}, f32[8,1,128,128]{3,2,1,0:T(8,128)}, u32[]{:S(2)}) copy-start(f32[8,1,128,128]{3,2,1,0:T(8,128)} %param.7) | copy-start | bytes 1572868
  0.6 1.1 %copy-start.1 = (f32[8,16,8,128]{3,2,1,0:T(8,128)S(1)}, f32[8,16,8,128]{3,2,1,0:T(8,128)}, u32[]{:S(2)}) copy-start(f32[8,16,8,128]{3,2,1,0:T(8,128)} %param.4) | copy-start | bytes 1572868
  1.7 10.9 %copy-start.2 = (f32[8,16,8,128]{3,2,1,0:T(8,128)S(1)}, f32[8,16,8,128]{3,2,1,0:T(8,128)}, u32[]{:S(2)}) copy-start(f32[8,16,8,128]{3,2,1,0:T(8,128)} %param.4) | copy-start | bytes 1572868
  1.8 11.9 %collective-permute-start = (f32[8,2,16,128]{3,2,1,0:T(8,128)S(1)}, f32[8,2,16,128]{3,2,1,0:T(8,128)S(1)}, u32[]{:S(2)}, u32[]{:S(2)}) collective-permute-start(f32[8,2,16,128]{3,2,1,0:T(8,128)S(1)} %get-tuple-element.17), channel_id=1, source_target_pairs={{2,4},{4,2},{6,8},{8,6},{10,12},{12,10},{14,16},{16,14},{18,20},{2... | collective-permute-start | bytes 393224 | tf_op jit(solution)/shard_map/ppermute | solution.py:550
  8.8 5.8 %collective-permute-start.1 = (f32[8,2,16,128]{3,2,1,0:T(8,128)S(1)}, f32[8,2,16,128]{3,2,1,0:T(8,128)S(1)}, u32[]{:S(2)}, u32[]{:S(2)}) collective-permute-start(f32[8,2,16,128]{3,2,1,0:T(8,128)S(1)} %get-tuple-element.18), channel_id=1, source_target_pairs={{0,2},{2,0},{4,6},{6,4},{8,10},{10,8},{12,14},{14,12},{16,18},{18,... | collective-permute-start | bytes 393224 | tf_op jit(solution)/shard_map/ppermute | solution.py:551
  8.8 3.5 %collective-permute-start.2 = (f32[8,16,128]{2,1,0:T(8,128)S(1)}, f32[8,16,128]{2,1,0:T(8,128)S(1)}, u32[]{:S(2)}, u32[]{:S(2)}) collective-permute-start(f32[8,16,128]{2,1,0:T(8,128)S(1)} %get-tuple-element.19._), channel_id=1, source_target_pairs={{0,1},{1,0},{2,3},{3,2},{4,5},{5,4},{6,7},{7,6},{8,9},{9,8},{10,11... | collective-permute-start | bytes 196616 | tf_op jit(solution)/shard_map/ppermute | solution.py:552
  8.8 0.7 %copy-start.4 = (f32[4,8,128]{2,1,0:T(8,128)S(1)}, f32[4,8,128]{2,1,0:T(8,128)}, u32[]{:S(2)}) copy-start(f32[4,8,128]{2,1,0:T(8,128)} %own_conductance.1) | copy-start | bytes 49156
  9.5 3.1 %copy-start.3 = (s32[16,8,128]{2,1,0:T(8,128)S(1)}, s32[16,8,128]{2,1,0:T(8,128)}, u32[]{:S(2)}) copy-start(s32[16,8,128]{2,1,0:T(8,128)} %param.5) | copy-start | bytes 196612
  9.6 11.7 %collective-permute-start.6 = (f32[3,136,128]{2,1,0:T(8,128)S(1)}, f32[3,136,128]{2,1,0:T(8,128)S(1)}, u32[]{:S(2)}, u32[]{:S(2)}) collective-permute-start(f32[3,136,128]{2,1,0:T(8,128)S(1)} %get-tuple-element.23), channel_id=1, source_target_pairs={{0,2},{2,0},{4,6},{6,4},{8,10},{10,8},{12,14},{14,12},{16,18},{18,... | collective-permute-start | bytes 626696 | tf_op jit(solution)/shard_map/ppermute | solution.py:621
  11.7 9.7 %collective-permute-start.7 = (f32[3,136,128]{2,1,0:T(8,128)S(1)}, f32[3,136,128]{2,1,0:T(8,128)S(1)}, u32[]{:S(2)}, u32[]{:S(2)}) collective-permute-start(f32[3,136,128]{2,1,0:T(8,128)S(1)} %get-tuple-element.24), channel_id=1, source_target_pairs={{2,4},{4,2},{6,8},{8,6},{10,12},{12,10},{14,16},{16,14},{18,20},{2... | collective-permute-start | bytes 626696 | tf_op jit(solution)/shard_map/ppermute | solution.py:622
  12.3 17.1 %collective-permute-start.8 = (f32[8,128,128]{2,1,0:T(8,128)S(1)}, f32[8,128,128]{2,1,0:T(8,128)S(1)}, u32[]{:S(2)}, u32[]{:S(2)}) collective-permute-start(f32[8,128,128]{2,1,0:T(8,128)S(1)} %bitcast.12), channel_id=1, source_target_pairs={{0,1},{1,0},{2,3},{3,2},{4,5},{5,4},{6,7},{7,6},{8,9},{9,8},{10,11... | collective-permute-start | bytes 1572872 | tf_op jit(solution)/shard_map/ppermute | solution.py:662
  12.6 1.1 %copy-start.5 = (f32[4,8,128]{2,1,0:T(8,128)S(1)}, f32[4,8,128]{2,1,0:T(8,128)}, u32[]{:S(2)}) copy-start(f32[4,8,128]{2,1,0:T(8,128)} %own_conductance.1) | copy-start | bytes 49156
  13.8 15.1 %collective-permute-start.9 = (f32[4,8,128]{2,1,0:T(8,128)S(1)}, f32[4,8,128]{2,1,0:T(8,128)S(1)}, u32[]{:S(2)}, u32[]{:S(2)}) collective-permute-start(f32[4,8,128]{2,1,0:T(8,128)S(1)} %copy-done.5), channel_id=1, source_target_pairs={{0,1},{1,0},{2,3},{3,2},{4,5},{5,4},{6,7},{7,6},{8,9},{9,8},{10,11... | collective-permute-start | bytes 49160 | tf_op jit(solution)/shard_map/ppermute | solution.py:662
  15.7 13.7 %all-to-all-start = ((f32[32,4,128]{2,1,0:T(4,128)}), f32[32,4,128]{2,1,0:T(4,128)S(1)}, u32[]{:S(2)}, u32[]{:S(2)}) async-start(f32[32,4,128]{2,1,0:T(4,128)} %bitcast.3), calls=%async_computation | async-start | bytes 131072 | tf_op jit(solution)/shard_map/all_to_all | solution.py:663
  21.3 8.1 %collective-permute-start.10 = (f32[3,136,128]{2,1,0:T(8,128)S(1)}, f32[3,136,128]{2,1,0:T(8,128)S(1)}, u32[]{:S(2)}, u32[]{:S(2)}) collective-permute-start(f32[3,136,128]{2,1,0:T(8,128)S(1)} %get-tuple-element.25.own_pair), channel_id=1, source_target_pairs={{0,1},{1,0},{2,3},{3,2},{4,5},{5,4},{6,7},{7,6},{8,9},{9,8},{10,11... | collective-permute-start | bytes 626696 | tf_op jit(solution)/shard_map/ppermute | solution.py:662
  21.3 8.1 %collective-permute-start.11 = (f32[3,136,128]{2,1,0:T(8,128)S(1)}, f32[3,136,128]{2,1,0:T(8,128)S(1)}, u32[]{:S(2)}, u32[]{:S(2)}) collective-permute-start(f32[3,136,128]{2,1,0:T(8,128)S(1)} %get-tuple-element.26.own_next), channel_id=1, source_target_pairs={{0,1},{1,0},{2,3},{3,2},{4,5},{5,4},{6,7},{7,6},{8,9},{9,8},{10,11... | collective-permute-start | bytes 626696 | tf_op jit(solution)/shard_map/ppermute | solution.py:662
  24.2 0.7 %copy-start.6 = (f32[4,128,128]{2,1,0:T(8,128)}, f32[4,128,128]{2,1,0:T(8,128)S(1)}, u32[]{:S(2)}) copy-start(f32[4,128,128]{2,1,0:T(8,128)S(1)} %get-tuple-element.29.refs_1_) | copy-start | bytes 786436
  24.9 10.6 %collective-permute-start.3 = (f32[8,2,16,128]{3,2,1,0:T(8,128)S(1)}, f32[8,2,16,128]{3,2,1,0:T(8,128)S(1)}, u32[]{:S(2)}, u32[]{:S(2)}) collective-permute-start(f32[8,2,16,128]{3,2,1,0:T(8,128)S(1)} %get-tuple-element.20), channel_id=1, source_target_pairs={{2,4},{4,2},{6,8},{8,6},{10,12},{12,10},{14,16},{16,14},{18,20},{2... | collective-permute-start | bytes 393224 | tf_op jit(solution)/shard_map/ppermute | solution.py:550
  28.9 6.7 %collective-permute-start.4 = (f32[8,2,16,128]{3,2,1,0:T(8,128)S(1)}, f32[8,2,16,128]{3,2,1,0:T(8,128)S(1)}, u32[]{:S(2)}, u32[]{:S(2)}) collective-permute-start(f32[8,2,16,128]{3,2,1,0:T(8,128)S(1)} %get-tuple-element.21), channel_id=1, source_target_pairs={{0,2},{2,0},{4,6},{6,4},{8,10},{10,8},{12,14},{14,12},{16,18},{18,... | collective-permute-start | bytes 393224 | tf_op jit(solution)/shard_map/ppermute | solution.py:551
  29.4 6.1 %collective-permute-start.5 = (f32[8,16,128]{2,1,0:T(8,128)S(1)}, f32[8,16,128]{2,1,0:T(8,128)S(1)}, u32[]{:S(2)}, u32[]{:S(2)}) collective-permute-start(f32[8,16,128]{2,1,0:T(8,128)S(1)} %get-tuple-element.22._), channel_id=1, source_target_pairs={{0,1},{1,0},{2,3},{3,2},{4,5},{5,4},{6,7},{7,6},{8,9},{9,8},{10,11... | collective-permute-start | bytes 196616 | tf_op jit(solution)/shard_map/ppermute | solution.py:552
  32.2 10.4 %all-to-all-start.1 = ((f32[32,1,128]{2,1,0:T(1,128)}), f32[32,1,128]{2,1,0:T(1,128)S(1)}, u32[]{:S(2)}, u32[]{:S(2)}) async-start(f32[32,1,128]{2,1,0:T(1,128)} %bitcast.7), calls=%async_computation.1 | async-start | bytes 32768 | tf_op jit(solution)/shard_map/all_to_all | solution.py:677
  35.6 1.0 %copy-start.7 = (f32[4,128,128]{2,1,0:T(8,128)S(1)}, f32[4,128,128]{2,1,0:T(8,128)}, u32[]{:S(2)}) copy-start(f32[4,128,128]{2,1,0:T(8,128)} %copy-done.6) | copy-start | bytes 786436
